TPU v7x, 256 devices: a whole 4x4x8 slice. The times are simulated.
256 devices in a mesh: row: 16 (over z_hi, y, core), col: 16 (over x, z_lo).
Axes of the slice: x: 4, y: 4, z: 8 (z_hi: 2, z_lo: 4; z = z_hi * 4 + z_lo), core: 2. Of those that a mesh axis runs over, the one named last changes fastest.
Arguments:
- tile_values: bfloat16 [90112, 128, 128], P(('row', 'col')), may hold values from 0.049804688 to 20
- tile_rows: int32 [90112], P(('row', 'col')), may hold values from 0 to 63
- tile_cols: int32 [90112], P(('row', 'col')), may hold values from 0 to 31
- seed_users: int32 [32, 16], replicated, may hold values from 0 to 131071
Outputs:
- hub: float32 [32, 131072], P(None, ('row', 'col'))
- authority: float32 [32, 65536], P(None, ('col', 'row'))
All inputs are finite; a program needn't handle non-finite values.
Results may differ from a plain program's by a relative error of at most 0.0003.
Values may be sent and summed in bfloat16 or wider, within the bound.
No kernel may reach another device: no remote copies, remote signals or barrier semaphores. Data moves between devices by JAX's collectives and lax.ppermute only.
A program may use at most 64 MiB of HBM per device.

v0:
```python
import jax
import jax.numpy as jnp
from jax import lax
from jax.sharding import PartitionSpec as P

SEEDK = 16
ITERS = 2
U_DEV = 512
I_DEV = 256


def per_device(tile_values, tile_rows, tile_cols, seed_users):
    n_rows = lax.axis_size("row")
    n_cols = lax.axis_size("col")
    row_index = lax.axis_index("row")
    col_index = lax.axis_index("col")
    seeds = seed_users.shape[0]
    edge = tile_values.shape[1]
    user_tiles = U_DEV * n_cols // edge
    item_tiles = I_DEV * n_rows // edge
    users_total = U_DEV * n_rows * n_cols
    items_total = I_DEV * n_rows * n_cols
    cell = row_index * n_cols + col_index
    user_ids = cell * U_DEV + jnp.arange(U_DEV, dtype=jnp.int32)
    counts = jnp.sum(
        (seed_users[:, :, None] == user_ids[None, None, :]).astype(jnp.float32), axis=1
    )
    teleport = counts * jnp.float32((users_total / SEEDK) ** 0.5)
    hub = teleport
    authority = jnp.zeros((seeds, I_DEV), jnp.float32)
    for step_index in range(ITERS):
        hub_full = lax.all_gather(hub.astype(jnp.bfloat16), "col", axis=1, tiled=True)
        item_picked = hub_full.reshape(seeds, user_tiles, edge)[:, tile_rows, :]
        item_prod = jnp.einsum(
            "stk,tkj->stj", item_picked, tile_values, preferred_element_type=jnp.float32
        )
        item_summed = (
            jnp.zeros((seeds, item_tiles, edge), jnp.float32).at[:, tile_cols, :].add(item_prod)
        )
        item_part = item_summed.reshape(seeds, item_tiles * edge)
        item_raw = lax.psum_scatter(item_part, "row", scatter_dimension=1, tiled=True)
        item_sq = lax.psum(jnp.sum(item_raw * item_raw, axis=1, keepdims=True), ("row", "col"))
        authority = item_raw * lax.rsqrt(item_sq / items_total + 1e-06)
        item_full = lax.all_gather(authority.astype(jnp.bfloat16), "row", axis=1, tiled=True)
        picked = item_full.reshape(seeds, item_tiles, edge)[:, tile_cols, :]
        prod = jnp.einsum("stj,tkj->stk", picked, tile_values, preferred_element_type=jnp.float32)
        summed = jnp.zeros((seeds, user_tiles, edge), jnp.float32).at[:, tile_rows, :].add(prod)
        user_part = summed.reshape(seeds, user_tiles * edge)
        user_raw = lax.psum_scatter(user_part, "col", scatter_dimension=1, tiled=True)
        user_sq = lax.psum(jnp.sum(user_raw * user_raw, axis=1, keepdims=True), ("row", "col"))
        hub = 0.85 * user_raw * lax.rsqrt(user_sq / users_total + 1e-06) + 0.15 * teleport
    return (hub, authority)


def solution(mesh):
    return jax.shard_map(
        per_device,
        mesh=mesh,
        in_specs=(P(("row", "col"), None, None), P(("row", "col")), P(("row", "col")), P()),
        out_specs=(P(None, ("row", "col")), P(None, ("col", "row"))),
        check_vma=False,
    )
```

profile of v0, /device:TPU:1, one launch (start us, length us, event | category | flops | bytes accessed | tf_op | source)
XLA Modules:
  0.0 956.9 jit_solution(1048076385656931821)
XLA Ops:
  7.2 0.0 reduce-scatter.5.cloned.1.call-start
  7.2 0.8 copy.21
  8.0 0.3 convert_reduce_fusion
  8.3 41.9 %all_gather.12 = bf16[32,8192]{1,0:T(8,128)(2,1)S(1)} all-gather(bf16[32,512]{1,0:T(8,128)(2,1)S(1)} %multiply_convert_fusion), channel_id=1, replica_groups=mesh['row'=16,'col'=16] {'col'}, dimensions={1}, use_global_device_ids=true | all-gather | bytes 557056 | tf_op jit(solution)/shard_map/all_gather | solution.py:32
  50.2 0.1 copy_bitcast_fusion.5
  50.3 0.7 compare_select_fusion.1
  51.0 0.7 compare_select_fusion
  51.7 2.4 gather_fusion
  54.1 7.6 fusion.6
  61.7 31.6 %scatter_fusion = f32[32,32,128]{2,0,1:T(8,128)S(1)} fusion(f32[32,32,128]{2,0,1:T(8,128)S(1)} %broadcast.46.clone, s32[352]{0:T(512)S(1)} %compare_select_fusion, f32[352,32,128]{2,1,0:T(8,128)} %fusion.6), kind=kCustom, calls=%fused_computation.4 | custom fusion | flops 1441792 | bytes 17302912 | tf_op jit(solution)/shard_map/scatter-add | solution.py:38
  93.3 0.8 copy_bitcast_fusion.3
  94.2 0.0 reduce-scatter.7.cloned.1.call-start
  94.2 80.3 %reduce-scatter.5.cloned.1.call-done = f32[32,256]{1,0:T(8,128)} async-done(((f32[32,4096]{1,0:T(8,128)}), f32[32,256]{1,0:T(8,128)}) %reduce-scatter.5.cloned.1.call-update) | async-done | bytes 32784 | tf_op jit(solution)/shard_map/reduce_scatter | solution.py:41
  174.6 0.9 multiply_reduce_fusion.3
  175.5 75.8 %psum.28 = f32[32,1]{0,1:T(1,128)S(1)} all-reduce(f32[32,1]{0,1:T(1,128)S(1)} %bitcast.68), channel_id=1, replica_groups=mesh['row'=16,'col'=16] {'row','col'}, use_global_device_ids=true, to_apply=%region_4.0 | all-reduce | flops 32 | bytes 256 | tf_op jit(solution)/shard_map/psum | solution.py:42
  251.2 0.8 multiply_convert_fusion.1
  252.1 28.7 %all_gather.13 = bf16[32,4096]{1,0:T(8,128)(2,1)S(1)} all-gather(bf16[32,256]{1,0:T(8,128)(2,1)S(1)} %multiply_convert_fusion.1), channel_id=1, replica_groups=mesh['row'=16,'col'=16] {'row'}, dimensions={1}, use_global_device_ids=true | all-gather | bytes 278528 | tf_op jit(solution)/shard_map/all_gather | solution.py:44
  280.8 2.4 gather_fusion.1
  283.2 10.5 %fusion.4 = f32[352,32,128]{2,1,0:T(8,128)} fusion(bf16[352,128,128]{2,1,0:T(8,128)(2,1)} %param.4, bf16[352,32,128]{2,1,0:T(8,128)(2,1)S(1)} %gather_fusion.1), kind=kOutput, calls=%fused_computation.12 | convolution fusion | flops 369098752 | bytes 20185088 | tf_op jit(solution)/shard_map/stj,tkj->stk/dot_general | solution.py:46
  293.7 0.1 broadcast.43.clone
  293.9 31.5 %scatter_fusion.1 = f32[32,64,128]{2,0,1:T(8,128)S(1)} fusion(f32[32,64,128]{2,0,1:T(8,128)S(1)} %broadcast.43.clone, s32[352]{0:T(512)S(1)} %compare_select_fusion.1, f32[352,32,128]{2,1,0:T(8,128)} %fusion.4), kind=kCustom, calls=%fused_computation.5 | custom fusion | flops 1441792 | bytes 17302912 | tf_op jit(solution)/shard_map/scatter-add | solution.py:47
  325.4 1.1 copy_bitcast_fusion.1
  326.5 0.0 reduce-scatter.9.cloned.1.call-start
  326.5 70.4 %reduce-scatter.7.cloned.1.call-done = f32[32,512]{1,0:T(8,128)} async-done(((f32[32,8192]{1,0:T(8,128)}), f32[32,512]{1,0:T(8,128)}) %reduce-scatter.7.cloned.1.call-update) | async-done | bytes 65552 | tf_op jit(solution)/shard_map/reduce_scatter | solution.py:49
  396.9 1.0 multiply_reduce_fusion.1
  397.9 84.8 %psum.29 = f32[32,1]{0,1:T(1,128)S(1)} all-reduce(f32[32,1]{0,1:T(1,128)S(1)} %bitcast.69), channel_id=1, replica_groups=mesh['row'=16,'col'=16] {'row','col'}, use_global_device_ids=true, to_apply=%region_8.0 | all-reduce | flops 32 | bytes 256 | tf_op jit(solution)/shard_map/psum | solution.py:50
  482.7 0.9 add_convert_fusion
  483.6 36.8 %all_gather.14 = bf16[32,8192]{1,0:T(8,128)(2,1)S(1)} all-gather(bf16[32,512]{1,0:T(8,128)(2,1)S(1)} %add_convert_fusion), channel_id=1, replica_groups=mesh['row'=16,'col'=16] {'col'}, dimensions={1}, use_global_device_ids=true | all-gather | bytes 557056 | tf_op jit(solution)/shard_map/all_gather | solution.py:32
  520.4 0.1 copy_bitcast_fusion.4
  520.5 2.4 gather_fusion.2
  522.9 7.6 fusion.2
  530.5 31.6 %scatter_fusion.2 = f32[32,32,128]{2,0,1:T(8,128)S(1)} fusion(f32[32,32,128]{2,0,1:T(8,128)S(1)} %broadcast.46, s32[352]{0:T(512)S(1)} %compare_select_fusion, f32[352,32,128]{2,1,0:T(8,128)} %fusion.2), kind=kCustom, calls=%fused_computation.6 | custom fusion | flops 1441792 | bytes 17302912 | tf_op jit(solution)/shard_map/scatter-add | solution.py:38
  562.1 0.8 copy_bitcast_fusion.2
  563.0 0.0 reduce-scatter.11.cloned.1.call-start
  563.0 77.0 %reduce-scatter.9.cloned.1.call-done = f32[32,256]{1,0:T(8,128)} async-done(((f32[32,4096]{1,0:T(8,128)}), f32[32,256]{1,0:T(8,128)}) %reduce-scatter.9.cloned.1.call-update) | async-done | bytes 32784 | tf_op jit(solution)/shard_map/reduce_scatter | solution.py:41
  640.0 0.9 multiply_reduce_fusion.2
  640.9 76.0 %psum.30 = f32[32,1]{0,1:T(1,128)S(1)} all-reduce(f32[32,1]{0,1:T(1,128)S(1)} %bitcast.70), channel_id=1, replica_groups=mesh['row'=16,'col'=16] {'row','col'}, use_global_device_ids=true, to_apply=%region_12.0 | all-reduce | flops 32 | bytes 256 | tf_op jit(solution)/shard_map/psum | solution.py:42
  716.8 1.4 fusion.8
  718.3 28.7 %all_gather.15 = bf16[32,4096]{1,0:T(8,128)(2,1)S(1)} all-gather(bf16[32,256]{1,0:T(8,128)(2,1)S(1)} %get-tuple-element.2), channel_id=1, replica_groups=mesh['row'=16,'col'=16] {'row'}, dimensions={1}, use_global_device_ids=true | all-gather | bytes 278528 | tf_op jit(solution)/shard_map/all_gather | solution.py:44
  747.0 2.4 gather_fusion.3
  749.4 10.5 %fusion = f32[352,32,128]{2,1,0:T(8,128)} fusion(bf16[352,128,128]{2,1,0:T(8,128)(2,1)} %param.4, bf16[352,32,128]{2,1,0:T(8,128)(2,1)S(1)} %gather_fusion.3), kind=kOutput, calls=%fused_computation.8 | convolution fusion | flops 369098752 | bytes 20185088 | tf_op jit(solution)/shard_map/stj,tkj->stk/dot_general | solution.py:46
  759.9 0.1 broadcast.43
  760.0 31.5 %scatter_fusion.3 = f32[32,64,128]{2,0,1:T(8,128)S(1)} fusion(f32[32,64,128]{2,0,1:T(8,128)S(1)} %broadcast.43, s32[352]{0:T(512)S(1)} %compare_select_fusion.1, f32[352,32,128]{2,1,0:T(8,128)} %fusion), kind=kCustom, calls=%fused_computation.7 | custom fusion | flops 1441792 | bytes 17302912 | tf_op jit(solution)/shard_map/scatter-add | solution.py:47
  791.6 1.1 copy_bitcast_fusion
  792.7 70.4 %reduce-scatter.11.cloned.1.call-done = f32[32,512]{1,0:T(8,128)} async-done(((f32[32,8192]{1,0:T(8,128)}), f32[32,512]{1,0:T(8,128)}) %reduce-scatter.11.cloned.1.call-update) | async-done | bytes 65552 | tf_op jit(solution)/shard_map/reduce_scatter | solution.py:49
  863.0 1.0 multiply_reduce_fusion
  864.0 84.9 %psum.31 = f32[32,1]{0,1:T(1,128)S(1)} all-reduce(f32[32,1]{0,1:T(1,128)S(1)} %bitcast.71), channel_id=1, replica_groups=mesh['row'=16,'col'=16] {'row','col'}, use_global_device_ids=true, to_apply=%region_16.0 | all-reduce | flops 32 | bytes 256 | tf_op jit(solution)/shard_map/psum | solution.py:50
  948.8 1.5 multiply_add_fusion
  (16 shorter events, 0.3 us)
Async XLA Ops:
  7.2 167.4 %reduce-scatter.5.cloned.1.call-start = ((), (), s32[]{:S(2)}) async-start(), calls=%async_computation.4 | async-start | bytes 557056 | tf_op jit(solution)/shard_map/reduce_scatter | solution.py:41
  94.2 302.7 %reduce-scatter.7.cloned.1.call-start = ((), (), s32[]{:S(2)}) async-start(), calls=%async_computation.5 | async-start | bytes 1114112 | tf_op jit(solution)/shard_map/reduce_scatter | solution.py:49
  326.5 313.6 %reduce-scatter.9.cloned.1.call-start = ((), (), s32[]{:S(2)}) async-start(), calls=%async_computation.6 | async-start | bytes 557056 | tf_op jit(solution)/shard_map/reduce_scatter | solution.py:41
  563.0 300.0 %reduce-scatter.11.cloned.1.call-start = ((), (), s32[]{:S(2)}) async-start(), calls=%async_computation.7 | async-start | bytes 1114112 | tf_op jit(solution)/shard_map/reduce_scatter | solution.py:49
Sparse Core Ops, SparseCore 0:
  94.3 80.2 reduce-scatter.4
  326.6 70.2 reduce-scatter.6
  563.1 76.8 reduce-scatter.8
  792.8 70.1 reduce-scatter.10
where the time goes:
time: 961 us; the launch traced here: 957 us
  blocking collectives  458 us (48%)
  waiting for transfers between devices  298 us (31%)
  other arithmetic  136 us (14%)
  matrix products  36.2 us (4%)
  local copies, waits for them, and re-layouts  14.7 us (2%)
  between operations  13.9 us (1%)
    psum x2, blocking collectives, per_device(): lax.psum(jnp.sum(user_raw * user_raw, axis=1, keepdims=True), ('row', 'co...  170 us
    reduce_scatter x2, waiting for transfers between devices, per_device(): lax.psum_scatter(item_part, 'row', scatter_dimension=1, tiled=True)  157 us
    psum x2, blocking collectives, per_device(): lax.psum(jnp.sum(item_raw * item_raw, axis=1, keepdims=True), ('row', 'co...  152 us
    reduce_scatter x2, waiting for transfers between devices, per_device(): lax.psum_scatter(user_part, 'col', scatter_dimension=1, tiled=True)  141 us
    all_gather x2, blocking collectives, per_device(): lax.all_gather(hub.astype(jnp.bfloat16), 'col', axis=1, tiled=True)  78.7 us
    scatter-add x2, other arithmetic, per_device(): jnp.zeros((seeds, item_tiles, edge), jnp.float32).at[:, tile_cols, :]  63.2 us
    scatter-add x2, other arithmetic, per_device(): jnp.zeros((seeds, user_tiles, edge), jnp.float32).at[:, tile_rows, :]  63 us
    all_gather x2, blocking collectives, per_device(): lax.all_gather(authority.astype(jnp.bfloat16), 'row', axis=1, tiled=True)  57.4 us
  transfers between devices with their start and end apart: 4, of which 4 were waited for; matrix products, arithmetic and copies ran while one was open for 0% of the time, Pallas kernels for 0%

commit v1 on v0

v1 whole, which is shorter than its diff:
```python
import functools
import jax
import jax.numpy as jnp
import numpy as np
from jax import lax
from jax.experimental import pallas as pl
from jax.experimental.pallas import tpu as pltpu
from jax.sharding import PartitionSpec as P

SEEDK = 16
U_DEV = 512
I_DEV = 256
STEP = 32
SHRINK = 2.0**-16
GROW = 2.0**16


def teleport_tile(seed_ref, base, scale):
    seeds = seed_ref.shape[0]
    ids = base + lax.broadcasted_iota(jnp.int32, (seeds, 128), 1)
    count = jnp.zeros((seeds, 128), jnp.float32)
    for k in range(seed_ref.shape[1]):
        count += (seed_ref[:, k : k + 1] == ids).astype(jnp.float32)
    return count * scale


def teleport_kernel(base_ref, seed_ref, out_ref, *, scale):
    def body(t, carry):
        tile = teleport_tile(seed_ref, base_ref[0] + t * 128, scale)
        out_ref[t] = tile.astype(out_ref.dtype)
        return carry

    lax.fori_loop(0, out_ref.shape[0], body, 0)


def pass_kernel(src_ref, dst_ref, x_ref, w_ref, out_ref, acc_ref, *, contract, factor):
    step = pl.program_id(0)

    @pl.when(step == 0)
    def _():
        acc_ref[...] = jnp.zeros_like(acc_ref)

    for j in range(STEP):
        t = step * STEP + j
        prod = lax.dot_general(
            x_ref[src_ref[t]],
            w_ref[j],
            (((1,), (contract,)), ((), ())),
            preferred_element_type=jnp.float32,
        )
        acc_ref[dst_ref[t]] += prod

    @pl.when(step == pl.num_programs(0) - 1)
    def _():
        out_ref[...] = (acc_ref[...] * factor).astype(out_ref.dtype)


def tile_pass(src, dst, x, w, n_out, contract, factor, out_dtype):
    tiles = w.shape[0]
    seeds = x.shape[1]
    return pl.pallas_call(
        functools.partial(pass_kernel, contract=contract, factor=factor),
        grid_spec=pltpu.PrefetchScalarGridSpec(
            num_scalar_prefetch=2,
            grid=(tiles // STEP,),
            in_specs=[
                pl.BlockSpec(x.shape, lambda i, s, d: (0, 0, 0)),
                pl.BlockSpec((STEP, 128, 128), lambda i, s, d: (i, 0, 0)),
            ],
            out_specs=pl.BlockSpec((n_out, seeds, 128), lambda i, s, d: (0, 0, 0)),
            scratch_shapes=[pltpu.VMEM((n_out, seeds, 128), jnp.float32)],
        ),
        out_shape=jax.ShapeDtypeStruct((n_out, seeds, 128), out_dtype),
        compiler_params=pltpu.CompilerParams(vmem_limit_bytes=24 * 2**20),
    )(src, dst, x, w)


def reduce_shards(part, axis, n):
    tiles, seeds, edge = part.shape
    got = lax.all_to_all(part.reshape(n, tiles // n, seeds, edge), axis, 0, 0)
    return jnp.sum(got.astype(jnp.float32), axis=0)


def gather_shards(shard, axis, n):
    tiles, seeds, edge = shard.shape
    wire = jnp.broadcast_to(shard.astype(jnp.bfloat16)[None], (n, tiles, seeds, edge))
    return lax.all_to_all(wire, axis, 0, 0).reshape(n * tiles, seeds, edge)


def diag_mask(seeds, slot):
    lane = lax.broadcasted_iota(jnp.int32, (seeds, 128), 1)
    sub = lax.broadcasted_iota(jnp.int32, (seeds, 128), 0)
    return lane == sub + slot * seeds


def stat_kernel(x1_ref, y2_ref, got_ref, w2_ref, stat_ref):
    seeds = w2_ref.shape[1]
    w2_ref[...] = jnp.sum(got_ref[...], axis=0)

    def dot(a, b):
        return jnp.sum(jnp.sum(a * b, axis=0), axis=1, keepdims=True)

    x1, y2, w2 = x1_ref[...], y2_ref[...], w2_ref[...]
    spread = jnp.zeros((seeds, 128), jnp.float32)
    for slot, value in enumerate((dot(x1, x1), dot(x1, y2), dot(y2, y2), dot(w2, w2))):
        spread = jnp.where(diag_mask(seeds, slot), value, spread)
    stat_ref[...] = jnp.sum(spread, axis=0, keepdims=True)


def finish_kernel(
    base_ref, seed_ref, stat_ref, x1_ref, u1_ref, y2_ref, w2_ref, hub_ref, auth_ref, *, users, items, scale
):
    seeds = seed_ref.shape[0]

    def stat(slot):
        spread = jnp.where(diag_mask(seeds, slot), stat_ref[...], 0.0)
        return jnp.sum(spread, axis=1, keepdims=True)

    x1_sq, x1_y2, y2_sq, w2_sq = stat(0), stat(1), stat(2), stat(3)
    s_item1 = lax.rsqrt(x1_sq / items + 1e-06)
    gain = s_item1 * GROW
    s_user1 = lax.rsqrt(gain * gain * x1_y2 / users + 1e-06)
    alpha = 0.85 * s_item1 * s_user1 * (GROW * GROW)
    x2_sq = alpha * alpha * y2_sq + 0.3 * alpha * x1_y2 + 0.0225 * x1_sq
    s_item2 = lax.rsqrt(x2_sq / items + 1e-06)
    for t in range(auth_ref.shape[1] // 128):
        auth_ref[:, t * 128 : (t + 1) * 128] = (alpha * y2_ref[t] + 0.15 * x1_ref[t]) * s_item2
    raw_sq = alpha * alpha * w2_sq + 0.3 * alpha * y2_sq + 0.0225 * x1_y2
    out_gain = s_item2 * GROW
    s_user2 = lax.rsqrt(out_gain * out_gain * raw_sq / users + 1e-06)
    for t in range(hub_ref.shape[1] // 128):
        raw = (alpha * w2_ref[t] + 0.15 * u1_ref[t]) * out_gain
        tele = teleport_tile(seed_ref, base_ref[0] + t * 128, scale)
        hub_ref[:, t * 128 : (t + 1) * 128] = 0.85 * raw * s_user2 + 0.15 * tele


def per_device(tile_values, tile_rows, tile_cols, seed_users):
    n_rows = lax.axis_size("row")
    n_cols = lax.axis_size("col")
    row_index = lax.axis_index("row")
    cell = row_index * n_cols + lax.axis_index("col")
    seeds = seed_users.shape[0]
    edge = tile_values.shape[1]
    user_tiles = U_DEV * n_cols // edge
    item_tiles = I_DEV * n_rows // edge
    users = U_DEV * n_rows * n_cols
    items = I_DEV * n_rows * n_cols
    scale = float(np.float32((users / SEEDK) ** 0.5))
    smem = pl.BlockSpec(memory_space=pltpu.SMEM)
    vmem = pl.BlockSpec(memory_space=pltpu.VMEM)

    def to_items(hub, out_dtype, factor):
        return tile_pass(tile_rows, tile_cols, hub, tile_values, item_tiles, 0, factor, out_dtype)

    def to_users(item, out_dtype, factor):
        return tile_pass(tile_cols, tile_rows, item, tile_values, user_tiles, 1, factor, out_dtype)

    row_base = (row_index * (U_DEV * n_cols)).astype(jnp.int32).reshape(1)
    own_base = (cell * U_DEV).astype(jnp.int32).reshape(1)
    tele = pl.pallas_call(
        functools.partial(teleport_kernel, scale=scale),
        in_specs=[smem, vmem],
        out_specs=vmem,
        out_shape=jax.ShapeDtypeStruct((user_tiles, seeds, edge), jnp.bfloat16),
    )(row_base, seed_users)
    x1 = reduce_shards(to_items(tele, jnp.bfloat16, 1.0), "row", n_rows)
    u1 = reduce_shards(
        to_users(gather_shards(x1, "row", n_rows), jnp.bfloat16, SHRINK), "col", n_cols
    )
    y2 = reduce_shards(
        to_items(gather_shards(u1, "col", n_cols), jnp.float32, SHRINK), "row", n_rows
    )
    part = to_users(gather_shards(y2, "row", n_rows), jnp.float32, SHRINK)
    got = lax.all_to_all(part.reshape(n_cols, user_tiles // n_cols, seeds, edge), "col", 0, 0)
    w2, stat = pl.pallas_call(
        stat_kernel,
        in_specs=[vmem] * 3,
        out_specs=[vmem] * 2,
        out_shape=[
            jax.ShapeDtypeStruct((U_DEV // edge, seeds, edge), jnp.float32),
            jax.ShapeDtypeStruct((1, edge), jnp.float32),
        ],
    )(x1, y2, got)
    spread = jnp.broadcast_to(stat[None], (n_rows * n_cols, 1, edge))
    total = jnp.sum(lax.all_to_all(spread, ("row", "col"), 0, 0), axis=0)
    return pl.pallas_call(
        functools.partial(finish_kernel, users=users, items=items, scale=scale),
        in_specs=[smem] + [vmem] * 6,
        out_specs=[vmem] * 2,
        out_shape=[
            jax.ShapeDtypeStruct((seeds, U_DEV), jnp.float32),
            jax.ShapeDtypeStruct((seeds, I_DEV), jnp.float32),
        ],
    )(own_base, seed_users, total, x1, u1, y2, w2)


def solution(mesh):
    return jax.shard_map(
        per_device,
        mesh=mesh,
        in_specs=(P(("row", "col"), None, None), P(("row", "col")), P(("row", "col")), P()),
        out_specs=(P(None, ("row", "col")), P(None, ("col", "row"))),
        check_vma=False,
    )
```

time: 961 us -> 230 us (0.24)
  blocking collectives: 458 us -> 152 us
  waiting for transfers between devices: 298 us -> 12.9 us
  other arithmetic: 136 us -> 0.79 us
  Pallas kernels: 0 us -> 42 us
  matrix products: 36.2 us -> 0 us
  between operations: 13.9 us -> 0.81 us
    psum x4 -> x0, blocking collectives: 321 us -> none  [the longest x2 170 us: per_device(): lax.psum(jnp.sum(user_raw * user_raw, axis=1, keepdims=True), ('row', 'co...]
    reduce_scatter x4 -> x0, waiting for transfers between devices: 298 us -> none  [the longest x2 157 us: per_device(): lax.psum_scatter(item_part, 'row', scatter_dimension=1, tiled=True)]
    all_to_all x0 -> x7, blocking collectives: none -> 152 us  [the longest x3 68.9 us: reduce_shards(): got = lax.all_to_all(part.reshape(n, tiles // n, seeds, edge), axis, 0, 0)]
    all_gather x4 -> x0, blocking collectives: 136 us -> none  [the longest x2 78.7 us: per_device(): lax.all_gather(hub.astype(jnp.bfloat16), 'col', axis=1, tiled=True)]
    scatter-add x4 -> x0, other arithmetic: 126 us -> none  [the longest x2 63.2 us: per_device(): jnp.zeros((seeds, item_tiles, edge), jnp.float32).at[:, tile_cols, :]]
    pallas_call x0 -> x7, Pallas kernels: none -> 42 us  [the longest x4 26.1 us: tile_pass(): pl.pallas_call(functools.partial(pass_kernel, contract=contract, factor=f...]
    dot_general x4 -> x0, matrix products: 36.2 us -> none  [the longest x2 21 us: per_device(): jnp.einsum('stj,tkj->stk', picked, tile_values, preferred_element_type=jn...]
    all_to_all x0 -> x1, waiting for transfers between devices: none -> 12.9 us  [per_device(): total = jnp.sum(lax.all_to_all(spread, ('row', 'col'), 0, 0), axis=0)]
  transfers between devices with their start and end apart: 4 -> 1, of which waited for: 4 -> 1; matrix products, arithmetic and copies ran while one was open for 0% -> 0% of each run, Pallas kernels for 0% -> 0%
where the time goes in v1:
time: 230 us; the launch traced here: 229 us
  blocking collectives  152 us (66%)
  Pallas kernels  42 us (18%)
  local copies, waits for them, and re-layouts  13.9 us (6%)
  waiting for transfers between devices  12.9 us (6%)
  starting transfers between devices  6.86 us (3%)
    all_to_all x3, blocking collectives, reduce_shards(): got = lax.all_to_all(part.reshape(n, tiles // n, seeds, edge), axis, 0, 0)  68.9 us
    all_to_all x3, blocking collectives, gather_shards(): return lax.all_to_all(wire, axis, 0, 0).reshape(n * tiles, seeds, edge)  51.5 us
    all_to_all x1, blocking collectives, per_device(): lax.all_to_all(part.reshape(n_cols, user_tiles // n_cols, seeds, edge), '...  31.2 us
    pallas_call x4, Pallas kernels, tile_pass(): pl.pallas_call(functools.partial(pass_kernel, contract=contract, factor=f...  26.1 us
    all_to_all x1, waiting for transfers between devices, per_device(): total = jnp.sum(lax.all_to_all(spread, ('row', 'col'), 0, 0), axis=0)  12.9 us
    unnamed x23, local copies, waits for them, and re-layouts  12.4 us
    pallas_call x1, Pallas kernels, per_device(): pl.pallas_call(functools.partial(teleport_kernel, scale=scale), in_specs=...  11.8 us
    all_to_all x1, starting transfers between devices, per_device(): total = jnp.sum(lax.all_to_all(spread, ('row', 'col'), 0, 0), axis=0)  6.86 us
  transfers between devices with their start and end apart: 1, of which 1 were waited for; matrix products, arithmetic and copies ran while one was open for 0% of the time, Pallas kernels for 0%

profile of v1, /device:TPU:1, one launch (start us, length us, event | category | flops | bytes accessed | tf_op | source)
XLA Modules:
  0.0 229.0 jit_solution(16581072672925732495)
XLA Ops:
  0.6 1.4 copy.12.seed_ref
  2.0 11.8 %shard_map.59.x_ref = bf16[64,32,128]{2,1,0:T(8,128)(2,1)} custom-call(s32[1]{0:T(128)} %bitcast.1.base_ref, s32[32,16]{1,0:T(8,128)} %copy.12.seed_ref), custom_call_target="tpu_custom_call" | custom-call | tf_op jit(solution)/shard_map/pallas_call | solution.py:160
  13.8 0.0 copy-start
  13.8 4.3 %copy-done = bf16[352,128,128]{2,1,0:T(8,128)(2,1)S(1)} copy-done((bf16[352,128,128]{2,1,0:T(8,128)(2,1)S(1)}, bf16[352,128,128]{2,1,0:T(8,128)(2,1)}, u32[]{:S(2)}) %copy-start) | copy-done | bytes 11534360
  18.1 0.0 copy-start.3
  18.1 1.0 copy-done.3
  19.1 0.0 copy-start.4
  19.1 0.7 copy-done.4
  19.8 0.0 copy-start.6
  19.8 0.7 copy-done.6
  20.5 0.0 copy-start.1
  20.5 5.0 %shard_map.60 = bf16[32,32,128]{2,1,0:T(8,128)(2,1)S(1)} custom-call(s32[352]{0:T(512)S(1)} %copy-done.4, s32[352]{0:T(512)S(1)} %copy-done.6, bf16[64,32,128]{2,1,0:T(8,128)(2,1)S(1)} %copy-done.3, bf16[352,128,128]{2,1,0:T(8,128)(2,1)S(1)} %copy-done), custom_call_target="tpu_custom_call" | custom-call | tf_op jit(solution)/shard_map/pallas_call | solution.py:61
  25.5 0.0 copy-start.5
  25.5 0.0 copy-start.7
  25.5 23.5 %all_to_all.40 = bf16[16,2,32,128]{3,2,1,0:T(8,128)(2,1)S(1)} all-to-all(bf16[16,2,32,128]{3,2,1,0:T(8,128)(2,1)S(1)} %bitcast.16), channel_id=1, replica_groups=mesh['row'=16,'col'=16] {'row'}, dimensions={0} | all-to-all | bytes 524288 | tf_op jit(solution)/shard_map/all_to_all | solution.py:80
  49.1 0.0 copy-start.9
  49.2 15.1 %all_to_all.41 = bf16[16,2,32,128]{3,2,1,0:T(8,128)(2,1)S(1)} all-to-all(bf16[16,2,32,128]{3,2,1,0:T(8,128)(2,1)S(1)} %broadcast_in_dim.10), channel_id=1, replica_groups=mesh['row'=16,'col'=16] {'row'}, dimensions={0} | all-to-all | bytes 524288 | tf_op jit(solution)/shard_map/all_to_all | solution.py:87
  64.2 0.0 copy-done.1
  64.2 8.0 %shard_map.61 = bf16[64,32,128]{2,1,0:T(8,128)(2,1)S(1)} custom-call(s32[352]{0:T(512)S(1)} %copy-done.6, s32[352]{0:T(512)S(1)} %copy-done.4, bf16[32,32,128]{2,1,0:T(8,128)(2,1)S(1)} %bitcast.17, bf16[352,128,128]{2,1,0:T(8,128)(2,1)S(1)} %copy-done.1), custom_call_target="tpu_custom_call" | custom-call | tf_op jit(solution)/shard_map/pallas_call | solution.py:61
  72.3 24.3 %all_to_all.42 = bf16[16,4,32,128]{3,2,1,0:T(8,128)(2,1)S(1)} all-to-all(bf16[16,4,32,128]{3,2,1,0:T(8,128)(2,1)S(1)} %bitcast.13), channel_id=1, replica_groups=mesh['row'=16,'col'=16] {'col'}, dimensions={0} | all-to-all | bytes 1048576 | tf_op jit(solution)/shard_map/all_to_all | solution.py:80
  96.6 0.1 convert_reduce_fusion.u1_ref
  96.7 0.0 copy-start.8
  96.7 0.1 broadcast_in_dim.11
  96.8 19.5 %all_to_all.43 = bf16[16,4,32,128]{3,2,1,0:T(8,128)(2,1)S(1)} all-to-all(bf16[16,4,32,128]{3,2,1,0:T(8,128)(2,1)S(1)} %broadcast_in_dim.11), channel_id=1, replica_groups=mesh['row'=16,'col'=16] {'col'}, dimensions={0} | all-to-all | bytes 1048576 | tf_op jit(solution)/shard_map/all_to_all | solution.py:87
  116.3 0.0 copy-done.5
  116.3 0.0 copy-done.7
  116.4 5.0 %shard_map.62 = f32[32,32,128]{2,1,0:T(8,128)S(1)} custom-call(s32[352]{0:T(512)S(1)} %copy-done.5, s32[352]{0:T(512)S(1)} %copy-done.7, bf16[64,32,128]{2,1,0:T(8,128)(2,1)S(1)} %bitcast.14, bf16[352,128,128]{2,1,0:T(8,128)(2,1)S(1)} %copy-done.1), custom_call_target="tpu_custom_call" | custom-call | tf_op jit(solution)/shard_map/pallas_call | solution.py:61
  121.4 0.0 copy-done.9
  121.4 21.1 %all_to_all.44 = f32[16,2,32,128]{3,2,1,0:T(8,128)S(1)} all-to-all(f32[16,2,32,128]{3,2,1,0:T(8,128)S(1)} %bitcast.15), channel_id=1, replica_groups=mesh['row'=16,'col'=16] {'row'}, dimensions={0} | all-to-all | bytes 1048576 | tf_op jit(solution)/shard_map/all_to_all | solution.py:80
  142.5 0.0 copy-start.10
  142.6 17.0 %all_to_all.45 = bf16[16,2,32,128]{3,2,1,0:T(8,128)(2,1)S(1)} all-to-all(bf16[16,2,32,128]{3,2,1,0:T(8,128)(2,1)S(1)} %broadcast_in_dim.12), channel_id=1, replica_groups=mesh['row'=16,'col'=16] {'row'}, dimensions={0} | all-to-all | bytes 524288 | tf_op jit(solution)/shard_map/all_to_all | solution.py:87
  159.6 0.0 copy-start.2
  159.6 4.3 %copy-done.2 = bf16[352,128,128]{2,1,0:T(8,128)(2,1)S(1)} copy-done((bf16[352,128,128]{2,1,0:T(8,128)(2,1)S(1)}, bf16[352,128,128]{2,1,0:T(8,128)(2,1)}, u32[]{:S(2)}) %copy-start.2) | copy-done | bytes 11534360
  163.8 8.1 %shard_map.63 = f32[64,32,128]{2,1,0:T(8,128)S(1)} custom-call(s32[352]{0:T(512)S(1)} %copy-done.7, s32[352]{0:T(512)S(1)} %copy-done.5, bf16[32,32,128]{2,1,0:T(8,128)(2,1)S(1)} %bitcast.18, bf16[352,128,128]{2,1,0:T(8,128)(2,1)S(1)} %copy-done.2), custom_call_target="tpu_custom_call" | custom-call | tf_op jit(solution)/shard_map/pallas_call | solution.py:61
  171.9 0.0 copy-done.8
  171.9 31.2 %all_to_all.46.got_ref = f32[16,4,32,128]{3,2,1,0:T(8,128)} all-to-all(f32[16,4,32,128]{3,2,1,0:T(8,128)S(1)} %bitcast.12), channel_id=1, replica_groups=mesh['row'=16,'col'=16] {'col'}, dimensions={0} | all-to-all | bytes 2097152 | tf_op jit(solution)/shard_map/all_to_all | solution.py:174
  203.2 0.0 copy-done.10
  203.2 2.0 shard_map.64
  205.1 1.4 broadcast_in_dim.14
  206.5 6.9 %all-to-all-start.7 = ((f32[256,1,128]{2,1,0:T(1,128)}), f32[256,1,128]{2,1,0:T(1,128)S(1)}, u32[]{:S(2)}, u32[]{:S(2)}) async-start(f32[256,1,128]{2,1,0:T(1,128)} %broadcast_in_dim.14), calls=%async_computation.7 | async-start | bytes 262144 | tf_op jit(solution)/shard_map/all_to_all | solution.py:185
  213.4 12.9 %all-to-all-done.7 = f32[256,1,128]{2,1,0:T(1,128)S(1)} async-done(((f32[256,1,128]{2,1,0:T(1,128)}), f32[256,1,128]{2,1,0:T(1,128)S(1)}, u32[]{:S(2)}, u32[]{:S(2)}) %all-to-all-start.7) | async-done | bytes 131104 | tf_op jit(solution)/shard_map/all_to_all | solution.py:185
  226.3 0.6 reduce_sum.41
  226.9 2.0 shard_map.65
  (7 shorter events, 0.2 us)
Async XLA Ops:
  13.8 4.3 %copy-start = (bf16[352,128,128]{2,1,0:T(8,128)(2,1)S(1)}, bf16[352,128,128]{2,1,0:T(8,128)(2,1)}, u32[]{:S(2)}) copy-start(bf16[352,128,128]{2,1,0:T(8,128)(2,1)} %w_ref.7) | copy-start | bytes 34603012
  18.1 1.0 copy-start.3
  19.1 0.7 copy-start.4
  19.8 0.7 copy-start.6
  20.5 43.7 %copy-start.1 = (bf16[352,128,128]{2,1,0:T(8,128)(2,1)S(1)}, bf16[352,128,128]{2,1,0:T(8,128)(2,1)}, u32[]{:S(2)}) copy-start(bf16[352,128,128]{2,1,0:T(8,128)(2,1)} %w_ref.7) | copy-start | bytes 34603012
  25.5 90.8 %copy-start.5 = (s32[352]{0:T(512)S(1)}, s32[352]{0:T(512)}, u32[]{:S(2)}) copy-start(s32[352]{0:T(512)} %dst_ref.7) | copy-start | bytes 4228
  25.5 90.8 %copy-start.7 = (s32[352]{0:T(512)S(1)}, s32[352]{0:T(512)}, u32[]{:S(2)}) copy-start(s32[352]{0:T(512)} %src_ref.7) | copy-start | bytes 4228
  49.1 72.3 %copy-start.9 = (f32[2,32,128]{2,1,0:T(8,128)}, f32[2,32,128]{2,1,0:T(8,128)S(1)}, u32[]{:S(2)}) copy-start(f32[2,32,128]{2,1,0:T(8,128)S(1)} %convert_reduce_fusion.1.x1_ref) | copy-start | bytes 98308
  96.7 75.2 %copy-start.8 = (f32[4,32,128]{2,1,0:T(8,128)}, f32[4,32,128]{2,1,0:T(8,128)S(1)}, u32[]{:S(2)}) copy-start(f32[4,32,128]{2,1,0:T(8,128)S(1)} %convert_reduce_fusion.u1_ref) | copy-start | bytes 196612
  142.5 60.6 %copy-start.10 = (f32[2,32,128]{2,1,0:T(8,128)}, f32[2,32,128]{2,1,0:T(8,128)S(1)}, u32[]{:S(2)}) copy-start(f32[2,32,128]{2,1,0:T(8,128)S(1)} %reduce_sum.40.y2_ref) | copy-start | bytes 98308
  159.6 4.3 %copy-start.2 = (bf16[352,128,128]{2,1,0:T(8,128)(2,1)S(1)}, bf16[352,128,128]{2,1,0:T(8,128)(2,1)}, u32[]{:S(2)}) copy-start(bf16[352,128,128]{2,1,0:T(8,128)(2,1)} %w_ref.7) | copy-start | bytes 34603012
  206.5 19.8 %all-to-all-start.7 = ((f32[256,1,128]{2,1,0:T(1,128)}), f32[256,1,128]{2,1,0:T(1,128)S(1)}, u32[]{:S(2)}, u32[]{:S(2)}) async-start(f32[256,1,128]{2,1,0:T(1,128)} %broadcast_in_dim.14), calls=%async_computation.7 | async-start | bytes 262144 | tf_op jit(solution)/shard_map/all_to_all | solution.py:185

commit v2 on v0

v2 whole, which is shorter than its diff:
```python
import functools
import jax
import jax.numpy as jnp
import numpy as np
from jax import lax
from jax.experimental import pallas as pl
from jax.experimental.pallas import tpu as pltpu
from jax.sharding import PartitionSpec as P

SEEDK = 16
U_DEV = 512
I_DEV = 256
EDGE = 128
UNROLL = 176
STREAM = 88
SHRINK = 2.0**-16
GROW = 2.0**16
MIB = 2**20
F32 = jnp.float32
BF16 = jnp.bfloat16
SMEM = pl.BlockSpec(memory_space=pltpu.SMEM)
VMEM = pl.BlockSpec(memory_space=pltpu.VMEM)

CORE, Y, ZHI = (0, 1), (1, 2), (3, 1)
ZLO, X = (0, 2), (2, 2)


def field(index, part):
    return (index >> part[0]) & ((1 << part[1]) - 1)


def shifted(x, axis, part, by):
    size = 1 << part[1]
    perm = []
    for i in range(16):
        old = field(i, part)
        perm.append((i, i + (((old + by) % size - old) << part[0])))
    return lax.ppermute(x, axis, perm)


def gathered(x, axis, part):
    size = 1 << part[1]
    return [x] + [shifted(x, axis, part, size - by) for by in range(1, size)]


def exchanged(chunks, axis, part):
    return [chunks[0]] + [shifted(c, axis, part, by) for by, c in enumerate(chunks) if by]


def added(parts):
    total = parts[0].astype(F32)
    for p in parts[1:]:
        total = total + p.astype(F32)
    return total


def seed_columns(seed_ref):
    k, seeds = seed_ref.shape
    diag = diag_mask(seeds, seeds, 0)
    rows = seed_ref[...].astype(F32)
    return [
        jnp.sum(jnp.where(diag, rows[i : i + 1], 0.0), axis=1, keepdims=True).astype(jnp.int32)
        for i in range(k)
    ]


def teleport_tile(columns, base, scale):
    seeds = columns[0].shape[0]
    ids = base + lax.broadcasted_iota(jnp.int32, (seeds, EDGE), 1)
    count = jnp.zeros((seeds, EDGE), F32)
    for column in columns:
        count = jnp.where(column == ids, count + 1.0, count)
    return count * scale


def multiply_tiles(src_ref, dst_ref, x_ref, w_ref, acc_ref, contract, first, count):
    for j in range(count):
        prod = lax.dot_general(
            x_ref[src_ref[first + j]],
            w_ref[j] if w_ref.shape[0] == count else w_ref[first + j],
            (((1,), (contract,)), ((), ())),
            preferred_element_type=F32,
        )
        acc_ref[dst_ref[first + j]] += prod


def store_chunks(acc_ref, out_refs, factor):
    start = 0
    for out in out_refs:
        rows = out.shape[0]
        out[...] = (acc_ref[start : start + rows] * factor).astype(out.dtype)
        start += rows


def first_kernel(src_ref, dst_ref, base_ref, seed_ref, w_ref, *rest, scale):
    *out_refs, x_ref, wide_ref, acc_ref = rest
    step = pl.program_id(0)

    @pl.when(step == 0)
    def _():
        acc_ref[...] = jnp.zeros_like(acc_ref)
        for k, column in enumerate(seed_columns(seed_ref)):
            wide_ref[k] = jnp.broadcast_to(column - base_ref[0], wide_ref.shape[1:])

        def body(t, carry):
            ids = t * EDGE + lax.broadcasted_iota(jnp.int32, wide_ref.shape[1:], 1)
            count = jnp.zeros(wide_ref.shape[1:], F32)
            for k in range(wide_ref.shape[0]):
                count = jnp.where(wide_ref[k] == ids, count + 1.0, count)
            x_ref[t] = (count * scale).astype(x_ref.dtype)
            return carry

        lax.fori_loop(0, x_ref.shape[0], body, 0)

    multiply_tiles(src_ref, dst_ref, x_ref, w_ref, acc_ref, 0, step * STREAM, STREAM)

    @pl.when(step == pl.num_programs(0) - 1)
    def _():
        store_chunks(acc_ref, out_refs, 1.0)


def first_pass(src, dst, base, seed_t, w, n_src, outs, scale):
    seeds = seed_t.shape[1]
    n_dst = sum(rows for rows, _ in outs)
    return pl.pallas_call(
        functools.partial(first_kernel, scale=scale),
        grid_spec=pltpu.PrefetchScalarGridSpec(
            num_scalar_prefetch=3,
            grid=(w.shape[0] // STREAM,),
            in_specs=[
                pl.BlockSpec(seed_t.shape, lambda i, *_: (0, 0)),
                pl.BlockSpec((STREAM, EDGE, EDGE), lambda i, *_: (i, 0, 0)),
            ],
            out_specs=[pl.BlockSpec((rows, seeds, EDGE), lambda i, *_: (0, 0, 0)) for rows, _ in outs],
            scratch_shapes=[
                pltpu.VMEM((n_src, seeds, EDGE), BF16),
                pltpu.VMEM((seed_t.shape[0], seeds, EDGE), jnp.int32),
                pltpu.VMEM((n_dst, seeds, EDGE), F32),
            ],
        ),
        out_shape=[jax.ShapeDtypeStruct((rows, seeds, EDGE), dtype) for rows, dtype in outs],
        compiler_params=pltpu.CompilerParams(vmem_limit_bytes=56 * MIB),
    )(src, dst, base, seed_t, w)


def pass_kernel(src_ref, dst_ref, w_ref, *rest, contract, n_in):
    in_refs, (*out_refs, x_ref, acc_ref) = rest[:n_in], rest[n_in:]
    acc_ref[...] = jnp.zeros_like(acc_ref)
    start = 0
    for ref in in_refs:
        x_ref[start : start + ref.shape[0]] = ref[...]
        start += ref.shape[0]

    def body(i, carry):
        multiply_tiles(src_ref, dst_ref, x_ref, w_ref, acc_ref, contract, i * UNROLL, UNROLL)
        return carry

    lax.fori_loop(0, w_ref.shape[0] // UNROLL, body, 0)
    store_chunks(acc_ref, out_refs, SHRINK)


def tile_pass(src, dst, w, parts, contract, outs):
    seeds = parts[0].shape[1]
    n_src = sum(p.shape[0] for p in parts)
    n_dst = sum(rows for rows, _ in outs)
    return pl.pallas_call(
        functools.partial(pass_kernel, contract=contract, n_in=len(parts)),
        in_specs=[SMEM] * 2 + [VMEM] * (1 + len(parts)),
        out_specs=[VMEM] * len(outs),
        scratch_shapes=[
            pltpu.VMEM((n_src, seeds, EDGE), BF16),
            pltpu.VMEM((n_dst, seeds, EDGE), F32),
        ],
        out_shape=[jax.ShapeDtypeStruct((rows, seeds, EDGE), dtype) for rows, dtype in outs],
        compiler_params=pltpu.CompilerParams(vmem_limit_bytes=20 * MIB),
    )(src, dst, w, *parts)


def diag_mask(seeds, width, slot):
    lane = lax.broadcasted_iota(jnp.int32, (seeds, width), 1)
    sub = lax.broadcasted_iota(jnp.int32, (seeds, width), 0)
    return lane == sub + slot * seeds


def stat_kernel(x1_ref, y2_ref, *rest):
    *got_refs, w2_ref, stat_ref = rest
    seeds = w2_ref.shape[1]
    w2_ref[...] = added([ref[...] for ref in got_refs])

    def dot(a, b):
        return jnp.sum(jnp.sum(a * b, axis=0), axis=1, keepdims=True)

    x1, y2, w2 = x1_ref[...], y2_ref[...], w2_ref[...]
    spread = jnp.zeros((seeds, EDGE), F32)
    for slot, value in enumerate((dot(x1, x1), dot(x1, y2), dot(y2, y2), dot(w2, w2))):
        spread = jnp.where(diag_mask(seeds, EDGE, slot), value, spread)
    stat_ref[...] = jnp.broadcast_to(jnp.sum(spread, axis=0, keepdims=True), stat_ref.shape)


def finish_kernel(
    base_ref, seed_ref, stat_ref, x1_ref, u1_ref, y2_ref, w2_ref, hub_ref, auth_ref, *, users, items, scale
):
    seeds = seed_ref.shape[1]
    total = jnp.sum(stat_ref[...], axis=0, keepdims=True)

    def stat(slot):
        return jnp.sum(jnp.where(diag_mask(seeds, EDGE, slot), total, 0.0), axis=1, keepdims=True)

    x1_sq, x1_y2, y2_sq, w2_sq = stat(0), stat(1), stat(2), stat(3)
    s_item1 = lax.rsqrt(x1_sq / items + 1e-06)
    gain = s_item1 * GROW
    s_user1 = lax.rsqrt(gain * gain * x1_y2 / users + 1e-06)
    alpha = 0.85 * s_item1 * s_user1 * (GROW * GROW)
    x2_sq = alpha * alpha * y2_sq + 0.3 * alpha * x1_y2 + 0.0225 * x1_sq
    s_item2 = lax.rsqrt(x2_sq / items + 1e-06)
    for t in range(auth_ref.shape[1] // EDGE):
        auth_ref[:, t * EDGE : (t + 1) * EDGE] = (alpha * y2_ref[t] + 0.15 * x1_ref[t]) * s_item2
    raw_sq = alpha * alpha * w2_sq + 0.3 * alpha * y2_sq + 0.0225 * x1_y2
    out_gain = s_item2 * GROW
    s_user2 = lax.rsqrt(out_gain * out_gain * raw_sq / users + 1e-06)
    columns = seed_columns(seed_ref)
    for t in range(hub_ref.shape[1] // EDGE):
        raw = (alpha * w2_ref[t] + 0.15 * u1_ref[t]) * out_gain
        tele = teleport_tile(columns, base_ref[0] + t * EDGE, scale)
        hub_ref[:, t * EDGE : (t + 1) * EDGE] = 0.85 * raw * s_user2 + 0.15 * tele


def per_device(tile_values, tile_rows, tile_cols, seed_users):
    n_rows = lax.axis_size("row")
    n_cols = lax.axis_size("col")
    row = lax.axis_index("row").astype(jnp.int32)
    col = lax.axis_index("col").astype(jnp.int32)
    seeds = seed_users.shape[0]
    users = U_DEV * n_rows * n_cols
    items = I_DEV * n_rows * n_cols
    scale = float(np.float32((users / SEEDK) ** 0.5))
    seed_t = seed_users.T
    row_base = (row * (U_DEV * n_cols)).reshape(1)
    own_base = ((row * n_cols + col) * U_DEV).reshape(1)
    core, y, zhi = field(row, CORE), field(row, Y), field(row, ZHI)
    zlo, x = field(col, ZLO), field(col, X)

    t_half = (((tile_cols >> 1) & 1) ^ core) * 16
    t_zhi, t_y, t_q = tile_cols >> 4, (tile_cols >> 2) & 3, tile_cols & 1
    item_whole = t_half + t_zhi * 8 + t_y * 2 + t_q
    item_by_y = t_half + ((t_y - y) & 3) * 4 + t_zhi * 2 + t_q
    t_x = ((tile_rows >> 4) - x) & 3
    user_whole = t_x * 16 + (tile_rows & 15)
    user_by_z = t_x * 16 + ((((tile_rows >> 2) & 3) - zlo) & 3) * 4 + (tile_rows & 3)

    keep, send = first_pass(
        tile_rows, item_whole, row_base, seed_t, tile_values, 64, [(16, BF16)] * 2, scale
    )
    part = added(exchanged([keep, send], "row", CORE)).astype(BF16)
    part = added(gathered(part, "row", ZHI)).astype(BF16)
    x1_all = added(gathered(part, "row", Y))
    x1 = lax.dynamic_slice_in_dim(x1_all, (zhi * 4 + y) * 2, 2, 0)

    chunks = tile_pass(
        item_whole, user_whole, tile_values, gathered(x1_all.astype(BF16), "row", CORE), 1, [(16, BF16)] * 4
    )
    part = added(exchanged(chunks, "col", X)).astype(BF16)
    for bit in (1, 0):
        part = added(gathered(part, "col", (bit, 1)))
        u1 = lax.dynamic_slice_in_dim(part, zlo * 4, 4, 0)
        part = part.astype(BF16)

    chunks = tile_pass(
        user_whole, item_by_y, tile_values, gathered(part, "col", X), 0, [(16, F32)] * 2
    )
    part = added(exchanged(chunks, "row", CORE))
    part = added(exchanged([part[i * 4 : i * 4 + 4] for i in range(4)], "row", Y))
    part = added(gathered(part, "row", ZHI))
    y2 = lax.dynamic_slice_in_dim(part, zhi * 2, 2, 0)
    half = jnp.concatenate(gathered(part.astype(BF16), "row", Y), axis=0)

    chunks = tile_pass(
        item_by_y, user_by_z, tile_values, gathered(half, "row", CORE), 1, [(16, F32)] * 4
    )
    part = added(exchanged(chunks, "col", X))
    got = exchanged([part[i * 4 : i * 4 + 4] for i in range(4)], "col", ZLO)
    small = pltpu.CompilerParams(vmem_limit_bytes=8 * MIB)
    w2, stat = pl.pallas_call(
        stat_kernel,
        in_specs=[VMEM] * (2 + len(got)),
        out_specs=[VMEM] * 2,
        out_shape=[
            jax.ShapeDtypeStruct((U_DEV // EDGE, seeds, EDGE), F32),
            jax.ShapeDtypeStruct((n_rows * n_cols, EDGE), F32),
        ],
        compiler_params=small,
    )(x1, y2, *got)
    stats = lax.all_to_all(stat.reshape(n_rows * n_cols, 1, EDGE), ("row", "col"), 0, 0)
    return pl.pallas_call(
        functools.partial(finish_kernel, users=users, items=items, scale=scale),
        in_specs=[SMEM] + [VMEM] * 6,
        out_specs=[VMEM] * 2,
        out_shape=[
            jax.ShapeDtypeStruct((seeds, U_DEV), F32),
            jax.ShapeDtypeStruct((seeds, I_DEV), F32),
        ],
        compiler_params=small,
    )(own_base, seed_t, stats.reshape(n_rows * n_cols, EDGE), x1, u1, y2, w2)


def solution(mesh):
    return jax.shard_map(
        per_device,
        mesh=mesh,
        in_specs=(P(("row", "col"), None, None), P(("row", "col")), P(("row", "col")), P()),
        out_specs=(P(None, ("row", "col")), P(None, ("col", "row"))),
        check_vma=False,
    )
```

time: 961 us -> 179 us (0.19)
  blocking collectives: 458 us -> 0 us
  waiting for transfers between devices: 298 us -> 63 us
  other arithmetic: 136 us -> 2.66 us
  starting transfers between devices: 0.16 us -> 74 us
  matrix products: 36.2 us -> 0 us
  Pallas kernels: 0 us -> 29.9 us
  between operations: 13.9 us -> 0.79 us
    psum x4 -> x0, blocking collectives: 321 us -> none  [the longest x2 170 us: per_device(): lax.psum(jnp.sum(user_raw * user_raw, axis=1, keepdims=True), ('row', 'co...]
    reduce_scatter x4 -> x0, waiting for transfers between devices: 298 us -> none  [the longest x2 157 us: per_device(): lax.psum_scatter(item_part, 'row', scatter_dimension=1, tiled=True)]
    all_gather x4 -> x0, blocking collectives: 136 us -> none  [the longest x2 78.7 us: per_device(): lax.all_gather(hub.astype(jnp.bfloat16), 'col', axis=1, tiled=True)]
    scatter-add x4 -> x0, other arithmetic: 126 us -> none  [the longest x2 63.2 us: per_device(): jnp.zeros((seeds, item_tiles, edge), jnp.float32).at[:, tile_cols, :]]
    ppermute x0 -> x29, starting transfers between devices: none -> 61.3 us  [shifted(): return lax.ppermute(x, axis, perm)]
    ppermute x0 -> x29, waiting for transfers between devices: none -> 50.2 us  [shifted(): return lax.ppermute(x, axis, perm)]
    dot_general x4 -> x0, matrix products: 36.2 us -> none  [the longest x2 21 us: per_device(): jnp.einsum('stj,tkj->stk', picked, tile_values, preferred_element_type=jn...]
    pallas_call x0 -> x6, Pallas kernels: none -> 29.9 us  [the longest x3 17.9 us: tile_pass(): pl.pallas_call(functools.partial(pass_kernel, contract=contract, n_in=len...]
  transfers between devices with their start and end apart: 4 -> 30, of which waited for: 4 -> 26; matrix products, arithmetic and copies ran while one was open for 0% -> 0% of each run, Pallas kernels for 0% -> 0%
where the time goes in v2:
time: 179 us
  starting transfers between devices  74 us (41%)
  waiting for transfers between devices  63 us (35%)
  Pallas kernels  29.9 us (17%)
  local copies, waits for them, and re-layouts  8.62 us (5%)
  other arithmetic  2.66 us (1%)
    ppermute x29, starting transfers between devices, shifted(): return lax.ppermute(x, axis, perm)  61.3 us
    ppermute x29, waiting for transfers between devices, shifted(): return lax.ppermute(x, axis, perm)  50.2 us
    pallas_call x3, Pallas kernels, tile_pass(): pl.pallas_call(functools.partial(pass_kernel, contract=contract, n_in=len...  17.9 us
    all_to_all x1, waiting for transfers between devices, per_device(): lax.all_to_all(stat.reshape(n_rows * n_cols, 1, EDGE), ('row', 'col'), 0, 0)  12.9 us
    all_to_all x1, starting transfers between devices, per_device(): lax.all_to_all(stat.reshape(n_rows * n_cols, 1, EDGE), ('row', 'col'), 0, 0)  12.7 us
    pallas_call x1, Pallas kernels, first_pass(): pl.pallas_call(functools.partial(first_kernel, scale=scale), grid_spec=pl...  10.3 us
    unnamed x10, local copies, waits for them, and re-layouts  8.57 us
  transfers between devices with their start and end apart: 30, of which 26 were waited for; matrix products, arithmetic and copies ran while one was open for 0% of the time, Pallas kernels for 0%

profile of v2, /device:TPU:1, one launch (start us, length us, event | category | flops | bytes accessed | tf_op | source)
XLA Modules:
  0.0 178.9 jit_solution(4778231860948138199)
XLA Ops:
  0.6 1.3 add_add_fusion.1
  1.9 10.3 %shard_map.59 = (bf16[16,32,128]{2,1,0:T(8,128)(2,1)}, bf16[16,32,128]{2,1,0:T(8,128)(2,1)}) custom-call(s32[352]{0:T(512)} %src_ref.1, s32[352]{0:T(512)} %get-tuple-element.46.dst_ref.src_ref, s32[1]{0:T(128)} %bitcast.2.base_ref, s32[16,32]{1,0:T(8,128)} %bitcast.8, bf16[352,128,128]{2,1,0:T(8,128)(2,1)} %w_ref.7), custom_call_target="tpu_custom_call" | custom-call | tf_op jit(solution)/shard_map/pallas_call | solution.py:125
  12.2 3.2 %collective-permute-start = (bf16[16,32,128]{2,1,0:T(8,128)(2,1)}, bf16[16,32,128]{2,1,0:T(8,128)(2,1)S(1)}, u32[]{:S(2)}, u32[]{:S(2)}) collective-permute-start(bf16[16,32,128]{2,1,0:T(8,128)(2,1)} %get-tuple-element.17), channel_id=1, source_target_pairs={{0,16},{16,0},{32,48},{48,32},{64,80},{80,64},{96,112},{112,96},{1... | collective-permute-start | bytes 393224 | tf_op jit(solution)/shard_map/ppermute | solution.py:38
  15.5 1.2 collective-permute-done
  17.6 5.3 %collective-permute-start.1 = (bf16[16,32,128]{2,1,0:T(8,128)(2,1)S(1)}, bf16[16,32,128]{2,1,0:T(8,128)(2,1)S(1)}, u32[]{:S(2)}, u32[]{:S(2)}) collective-permute-start(bf16[16,32,128]{2,1,0:T(8,128)(2,1)S(1)} %add_convert_fusion.3), channel_id=1, source_target_pairs={{0,128},{16,144},{32,160},{48,176},{64,192},{80,208},{96,224},{112... | collective-permute-start | bytes 393224 | tf_op jit(solution)/shard_map/ppermute | solution.py:38
  22.9 3.5 %collective-permute-done.1 = bf16[16,32,128]{2,1,0:T(8,128)(2,1)S(1)} collective-permute-done((bf16[16,32,128]{2,1,0:T(8,128)(2,1)S(1)}, bf16[16,32,128]{2,1,0:T(8,128)(2,1)S(1)}, u32[]{:S(2)}, u32[]{:S(2)}) %collective-permute-start.1) | collective-permute-done | bytes 131104 | tf_op jit(solution)/shard_map/ppermute | solution.py:38
  26.4 1.5 collective-permute-start.4
  27.9 2.6 %collective-permute-start.3 = (bf16[16,32,128]{2,1,0:T(8,128)(2,1)S(1)}, bf16[16,32,128]{2,1,0:T(8,128)(2,1)S(1)}, u32[]{:S(2)}, u32[]{:S(2)}) collective-permute-start(bf16[16,32,128]{2,1,0:T(8,128)(2,1)S(1)} %add_convert_fusion.2), channel_id=1, source_target_pairs={{0,64},{16,80},{32,96},{48,112},{64,0},{80,16},{96,32},{112,48},{1... | collective-permute-start | bytes 393224 | tf_op jit(solution)/shard_map/ppermute | solution.py:38
  30.5 1.1 collective-permute-start.2
  31.7 3.9 %collective-permute-done.3 = bf16[16,32,128]{2,1,0:T(8,128)(2,1)S(1)} collective-permute-done((bf16[16,32,128]{2,1,0:T(8,128)(2,1)S(1)}, bf16[16,32,128]{2,1,0:T(8,128)(2,1)S(1)}, u32[]{:S(2)}, u32[]{:S(2)}) %collective-permute-start.3) | collective-permute-done | bytes 131104 | tf_op jit(solution)/shard_map/ppermute | solution.py:38
  36.1 1.8 %collective-permute-start.5 = (bf16[16,32,128]{2,1,0:T(8,128)(2,1)S(1)}, bf16[16,32,128]{2,1,0:T(8,128)(2,1)S(1)}, u32[]{:S(2)}, u32[]{:S(2)}) collective-permute-start(bf16[16,32,128]{2,1,0:T(8,128)(2,1)S(1)} %get-tuple-element.32.rest_0_), channel_id=1, source_target_pairs={{0,16},{16,0},{32,48},{48,32},{64,80},{80,64},{96,112},{112,96},{1... | collective-permute-start | bytes 393224 | tf_op jit(solution)/shard_map/ppermute | solution.py:38
  38.9 4.3 %copy-done = bf16[352,128,128]{2,1,0:T(8,128)(2,1)S(1)} copy-done((bf16[352,128,128]{2,1,0:T(8,128)(2,1)S(1)}, bf16[352,128,128]{2,1,0:T(8,128)(2,1)}, u32[]{:S(2)}) %copy-start) | copy-done | bytes 11534360
  43.2 7.0 %shard_map.60 = (bf16[16,32,128]{2,1,0:T(8,128)(2,1)S(1)}, bf16[16,32,128]{2,1,0:T(8,128)(2,1)S(1)}, bf16[16,32,128]{2,1,0:T(8,128)(2,1)S(1)}, bf16[16,32,128]{2,1,0:T(8,128)(2,1)S(1)}) custom-call(s32[352]{0:T(512)S(1)} %copy-done.3, s32[352]{0:T(512)S(1)} %get-tuple-element.44.dst_ref.src_ref, bf16[352,128,128]{2,1,0:T(8,128)(2,1)S(1)} %copy-done, ...), custom_call_target="tpu_custom_call" | custom-call | tf_op jit(solution)/shard_map/pallas_call | solution.py:166
  50.2 1.3 collective-permute-start.6
  51.5 2.5 %collective-permute-start.7 = (bf16[16,32,128]{2,1,0:T(8,128)(2,1)S(1)}, bf16[16,32,128]{2,1,0:T(8,128)(2,1)S(1)}, u32[]{:S(2)}, u32[]{:S(2)}) collective-permute-start(bf16[16,32,128]{2,1,0:T(8,128)(2,1)S(1)} %get-tuple-element.20), channel_id=1, source_target_pairs={{0,8},{1,9},{2,10},{3,11},{4,12},{5,13},{6,14},{7,15},{8,0},{9,1},... | collective-permute-start | bytes 393224 | tf_op jit(solution)/shard_map/ppermute | solution.py:38
  53.9 1.2 collective-permute-start.8
  55.1 1.1 collective-permute-done.6
  56.2 3.8 %collective-permute-done.7 = bf16[16,32,128]{2,1,0:T(8,128)(2,1)S(1)} collective-permute-done((bf16[16,32,128]{2,1,0:T(8,128)(2,1)S(1)}, bf16[16,32,128]{2,1,0:T(8,128)(2,1)S(1)}, u32[]{:S(2)}, u32[]{:S(2)}) %collective-permute-start.7) | collective-permute-done | bytes 131104 | tf_op jit(solution)/shard_map/ppermute | solution.py:38
  60.1 4.1 %collective-permute-start.9 = (bf16[16,32,128]{2,1,0:T(8,128)(2,1)S(1)}, bf16[16,32,128]{2,1,0:T(8,128)(2,1)S(1)}, u32[]{:S(2)}, u32[]{:S(2)}) collective-permute-start(bf16[16,32,128]{2,1,0:T(8,128)(2,1)S(1)} %add_convert_fusion.1), channel_id=1, source_target_pairs={{0,2},{1,3},{2,0},{3,1},{4,6},{5,7},{6,4},{7,5},{8,10},{9,11},{10,... | collective-permute-start | bytes 393224 | tf_op jit(solution)/shard_map/ppermute | solution.py:38
  64.2 2.4 %collective-permute-done.9 = bf16[16,32,128]{2,1,0:T(8,128)(2,1)S(1)} collective-permute-done((bf16[16,32,128]{2,1,0:T(8,128)(2,1)S(1)}, bf16[16,32,128]{2,1,0:T(8,128)(2,1)S(1)}, u32[]{:S(2)}, u32[]{:S(2)}) %collective-permute-start.9) | collective-permute-done | bytes 131104 | tf_op jit(solution)/shard_map/ppermute | solution.py:38
  66.6 2.1 %collective-permute-start.10 = (bf16[16,32,128]{2,1,0:T(8,128)(2,1)S(1)}, bf16[16,32,128]{2,1,0:T(8,128)(2,1)S(1)}, u32[]{:S(2)}, u32[]{:S(2)}) collective-permute-start(bf16[16,32,128]{2,1,0:T(8,128)(2,1)S(1)} %add_convert_fusion), channel_id=1, source_target_pairs={{0,1},{1,0},{2,3},{3,2},{4,5},{5,4},{6,7},{7,6},{8,9},{9,8},{10,11... | collective-permute-start | bytes 393224 | tf_op jit(solution)/shard_map/ppermute | solution.py:38
  68.7 3.3 %collective-permute-done.10 = bf16[16,32,128]{2,1,0:T(8,128)(2,1)S(1)} collective-permute-done((bf16[16,32,128]{2,1,0:T(8,128)(2,1)S(1)}, bf16[16,32,128]{2,1,0:T(8,128)(2,1)S(1)}, u32[]{:S(2)}, u32[]{:S(2)}) %collective-permute-start.10) | collective-permute-done | bytes 131104 | tf_op jit(solution)/shard_map/ppermute | solution.py:38
  72.0 1.1 collective-permute-start.13
  73.1 2.3 %collective-permute-start.12 = (bf16[16,32,128]{2,1,0:T(8,128)(2,1)S(1)}, bf16[16,32,128]{2,1,0:T(8,128)(2,1)S(1)}, u32[]{:S(2)}, u32[]{:S(2)}) collective-permute-start(bf16[16,32,128]{2,1,0:T(8,128)(2,1)S(1)} %get-tuple-element.35.rest_0_), channel_id=1, source_target_pairs={{0,8},{1,9},{2,10},{3,11},{4,12},{5,13},{6,14},{7,15},{8,0},{9,1},... | collective-permute-start | bytes 393224 | tf_op jit(solution)/shard_map/ppermute | solution.py:38
  77.1 2.0 %collective-permute-done.12.rest_2_ = bf16[16,32,128]{2,1,0:T(8,128)(2,1)S(1)} collective-permute-done((bf16[16,32,128]{2,1,0:T(8,128)(2,1)S(1)}, bf16[16,32,128]{2,1,0:T(8,128)(2,1)S(1)}, u32[]{:S(2)}, u32[]{:S(2)}) %collective-permute-start.12) | collective-permute-done | bytes 131104 | tf_op jit(solution)/shard_map/ppermute | solution.py:38
  79.2 4.3 %copy-done.1 = bf16[352,128,128]{2,1,0:T(8,128)(2,1)S(1)} copy-done((bf16[352,128,128]{2,1,0:T(8,128)(2,1)S(1)}, bf16[352,128,128]{2,1,0:T(8,128)(2,1)}, u32[]{:S(2)}) %copy-start.1) | copy-done | bytes 11534360
  83.5 3.9 %shard_map.61 = (f32[16,32,128]{2,1,0:T(8,128)S(1)}, f32[16,32,128]{2,1,0:T(8,128)S(1)}) custom-call(s32[352]{0:T(512)S(1)} %get-tuple-element.44.dst_ref.src_ref, s32[352]{0:T(512)S(1)} %get-tuple-element.45.dst_ref.src_ref, bf16[352,128,128]{2,1,0:T(8,128)(2,1)S(1)} %copy-done.1, bf16[16,32,128]{2,1,0:T(8,128)(2,1)S(1)} %get-tuple-element.35.rest_0_, ...), custom_call_target="tpu_custom_call" | custom-call | tf_op jit(solution)/shard_map/pallas_call | solution.py:166
  87.4 6.4 %collective-permute-start.14 = (f32[16,32,128]{2,1,0:T(8,128)S(1)}, f32[16,32,128]{2,1,0:T(8,128)S(1)}, u32[]{:S(2)}, u32[]{:S(2)}) collective-permute-start(f32[16,32,128]{2,1,0:T(8,128)S(1)} %get-tuple-element.23), channel_id=1, source_target_pairs={{0,16},{16,0},{32,48},{48,32},{64,80},{80,64},{96,112},{112,96},{1... | collective-permute-start | bytes 786440 | tf_op jit(solution)/shard_map/ppermute | solution.py:38
  93.8 1.2 collective-permute-done.14
  95.1 1.0 collective-permute-start.15
  96.1 1.7 collective-permute-start.17
  97.8 1.1 collective-permute-start.16
  99.5 3.0 %collective-permute-done.16 = f32[4,32,128]{2,1,0:T(8,128)S(1)} collective-permute-done((f32[4,32,128]{2,1,0:T(8,128)S(1)}, f32[4,32,128]{2,1,0:T(8,128)S(1)}, u32[]{:S(2)}, u32[]{:S(2)}) %collective-permute-start.16) | collective-permute-done | bytes 65568 | tf_op jit(solution)/shard_map/ppermute | solution.py:38
  102.5 5.2 %collective-permute-start.18 = (f32[4,32,128]{2,1,0:T(8,128)S(1)}, f32[4,32,128]{2,1,0:T(8,128)S(1)}, u32[]{:S(2)}, u32[]{:S(2)}) collective-permute-start(f32[4,32,128]{2,1,0:T(8,128)S(1)} %fusion.1), channel_id=1, source_target_pairs={{0,128},{16,144},{32,160},{48,176},{64,192},{80,208},{96,224},{112... | collective-permute-start | bytes 196616 | tf_op jit(solution)/shard_map/ppermute | solution.py:38
  107.7 1.9 %collective-permute-done.18 = f32[4,32,128]{2,1,0:T(8,128)S(1)} collective-permute-done((f32[4,32,128]{2,1,0:T(8,128)S(1)}, f32[4,32,128]{2,1,0:T(8,128)S(1)}, u32[]{:S(2)}, u32[]{:S(2)}) %collective-permute-start.18) | collective-permute-done | bytes 65568 | tf_op jit(solution)/shard_map/ppermute | solution.py:38
  110.1 1.8 %collective-permute-start.20 = (bf16[4,32,128]{2,1,0:T(8,128)(2,1)S(1)}, bf16[4,32,128]{2,1,0:T(8,128)(2,1)S(1)}, u32[]{:S(2)}, u32[]{:S(2)}) collective-permute-start(bf16[4,32,128]{2,1,0:T(8,128)(2,1)S(1)} %get-tuple-element.30), channel_id=1, source_target_pairs={{0,64},{16,80},{32,96},{48,112},{64,0},{80,16},{96,32},{112,48},{1... | collective-permute-start | bytes 98312 | tf_op jit(solution)/shard_map/ppermute | solution.py:38
  114.7 5.6 %collective-permute-start.22 = (bf16[16,32,128]{2,1,0:T(8,128)(2,1)S(1)}, bf16[16,32,128]{2,1,0:T(8,128)(2,1)S(1)}, u32[]{:S(2)}, u32[]{:S(2)}) collective-permute-start(bf16[16,32,128]{2,1,0:T(8,128)(2,1)S(1)} %pad_maximum_fusion.rest_0_), channel_id=1, source_target_pairs={{0,16},{16,0},{32,48},{48,32},{64,80},{80,64},{96,112},{112,96},{1... | collective-permute-start | bytes 393224 | tf_op jit(solution)/shard_map/ppermute | solution.py:38
  120.3 1.0 collective-permute-done.22.rest_1_
  121.3 7.0 %shard_map.62 = (f32[16,32,128]{2,1,0:T(8,128)S(1)}, f32[16,32,128]{2,1,0:T(8,128)S(1)}, f32[16,32,128]{2,1,0:T(8,128)S(1)}, f32[16,32,128]{2,1,0:T(8,128)S(1)}) custom-call(s32[352]{0:T(512)S(1)} %get-tuple-element.45.dst_ref.src_ref, s32[352]{0:T(512)S(1)} %get-tuple-element.43.dst_ref, bf16[352,128,128]{2,1,0:T(8,128)(2,1)S(1)} %copy-done.1, ...), custom_call_target="tpu_custom_call" | custom-call | tf_op jit(solution)/shard_map/pallas_call | solution.py:166
  128.3 1.4 collective-permute-start.23
  129.6 2.2 %collective-permute-start.24 = (f32[16,32,128]{2,1,0:T(8,128)S(1)}, f32[16,32,128]{2,1,0:T(8,128)S(1)}, u32[]{:S(2)}, u32[]{:S(2)}) collective-permute-start(f32[16,32,128]{2,1,0:T(8,128)S(1)} %get-tuple-element.26), channel_id=1, source_target_pairs={{0,8},{1,9},{2,10},{3,11},{4,12},{5,13},{6,14},{7,15},{8,0},{9,1},... | collective-permute-start | bytes 786440 | tf_op jit(solution)/shard_map/ppermute | solution.py:38
  132.3 4.8 %collective-permute-done.23 = f32[16,32,128]{2,1,0:T(8,128)S(1)} collective-permute-done((f32[16,32,128]{2,1,0:T(8,128)S(1)}, f32[16,32,128]{2,1,0:T(8,128)S(1)}, u32[]{:S(2)}, u32[]{:S(2)}) %collective-permute-start.23) | collective-permute-done | bytes 262176 | tf_op jit(solution)/shard_map/ppermute | solution.py:38
  137.1 6.4 %collective-permute-done.24 = f32[16,32,128]{2,1,0:T(8,128)S(1)} collective-permute-done((f32[16,32,128]{2,1,0:T(8,128)S(1)}, f32[16,32,128]{2,1,0:T(8,128)S(1)}, u32[]{:S(2)}, u32[]{:S(2)}) %collective-permute-start.24) | collective-permute-done | bytes 262176 | tf_op jit(solution)/shard_map/ppermute | solution.py:38
  143.6 1.8 %collective-permute-start.28 = (f32[4,32,128]{2,1,0:T(8,128)S(1)}, f32[4,32,128]{2,1,0:T(8,128)S(1)}, u32[]{:S(2)}, u32[]{:S(2)}) collective-permute-start(f32[4,32,128]{2,1,0:T(8,128)S(1)} %get-tuple-element.36), channel_id=1, source_target_pairs={{0,3},{1,0},{2,1},{3,2},{4,7},{5,4},{6,5},{7,6},{8,11},{9,8},{10,9... | collective-permute-start | bytes 196616 | tf_op jit(solution)/shard_map/ppermute | solution.py:38
  145.8 1.2 collective-permute-done.28.rest_3_
  147.0 4.7 %collective-permute-done.27.rest_2_ = f32[4,32,128]{2,1,0:T(8,128)S(1)} collective-permute-done((f32[4,32,128]{2,1,0:T(8,128)S(1)}, f32[4,32,128]{2,1,0:T(8,128)S(1)}, u32[]{:S(2)}, u32[]{:S(2)}) %collective-permute-start.27) | collective-permute-done | bytes 65568 | tf_op jit(solution)/shard_map/ppermute | solution.py:38
  152.4 12.7 %all-to-all-start = ((f32[256,1,128]{2,1,0:T(1,128)}), f32[256,1,128]{2,1,0:T(1,128)S(1)}, u32[]{:S(2)}, u32[]{:S(2)}) async-start(f32[256,1,128]{2,1,0:T(1,128)} %bitcast.4), calls=%async_computation | async-start | bytes 262144 | tf_op jit(solution)/shard_map/all_to_all | solution.py:293
  165.2 12.9 %all-to-all-done = f32[256,1,128]{2,1,0:T(1,128)S(1)} async-done(((f32[256,1,128]{2,1,0:T(1,128)}), f32[256,1,128]{2,1,0:T(1,128)S(1)}, u32[]{:S(2)}, u32[]{:S(2)}) %all-to-all-start) | async-done | bytes 131104 | tf_op jit(solution)/shard_map/all_to_all | solution.py:293
  (46 shorter events, 11.2 us)
Async XLA Ops:
  0.6 37.3 %copy-start.4 = (s32[352]{0:T(512)S(1)}, s32[352]{0:T(512)}, u32[]{:S(2)}) copy-start(s32[352]{0:T(512)} %src_ref.1) | copy-start | bytes 4228
  1.9 37.0 %copy-start.3 = (s32[352]{0:T(512)S(1)}, s32[352]{0:T(512)}, u32[]{:S(2)}) copy-start(s32[352]{0:T(512)} %get-tuple-element.46.dst_ref.src_ref) | copy-start | bytes 4228
  12.2 4.4 %collective-permute-start = (bf16[16,32,128]{2,1,0:T(8,128)(2,1)}, bf16[16,32,128]{2,1,0:T(8,128)(2,1)S(1)}, u32[]{:S(2)}, u32[]{:S(2)}) collective-permute-start(bf16[16,32,128]{2,1,0:T(8,128)(2,1)} %get-tuple-element.17), channel_id=1, source_target_pairs={{0,16},{16,0},{32,48},{48,32},{64,80},{80,64},{96,112},{112,96},{1... | collective-permute-start | bytes 393224 | tf_op jit(solution)/shard_map/ppermute | solution.py:38
  17.6 8.7 %collective-permute-start.1 = (bf16[16,32,128]{2,1,0:T(8,128)(2,1)S(1)}, bf16[16,32,128]{2,1,0:T(8,128)(2,1)S(1)}, u32[]{:S(2)}, u32[]{:S(2)}) collective-permute-start(bf16[16,32,128]{2,1,0:T(8,128)(2,1)S(1)} %add_convert_fusion.3), channel_id=1, source_target_pairs={{0,128},{16,144},{32,160},{48,176},{64,192},{80,208},{96,224},{112... | collective-permute-start | bytes 393224 | tf_op jit(solution)/shard_map/ppermute | solution.py:38
  26.4 5.3 %collective-permute-start.4 = (bf16[16,32,128]{2,1,0:T(8,128)(2,1)S(1)}, bf16[16,32,128]{2,1,0:T(8,128)(2,1)S(1)}, u32[]{:S(2)}, u32[]{:S(2)}) collective-permute-start(bf16[16,32,128]{2,1,0:T(8,128)(2,1)S(1)} %add_convert_fusion.2), channel_id=1, source_target_pairs={{0,32},{16,48},{32,64},{48,80},{64,96},{80,112},{96,0},{112,16},{1... | collective-permute-start | bytes 393224 | tf_op jit(solution)/shard_map/ppermute | solution.py:38
  27.9 7.7 %collective-permute-start.3 = (bf16[16,32,128]{2,1,0:T(8,128)(2,1)S(1)}, bf16[16,32,128]{2,1,0:T(8,128)(2,1)S(1)}, u32[]{:S(2)}, u32[]{:S(2)}) collective-permute-start(bf16[16,32,128]{2,1,0:T(8,128)(2,1)S(1)} %add_convert_fusion.2), channel_id=1, source_target_pairs={{0,64},{16,80},{32,96},{48,112},{64,0},{80,16},{96,32},{112,48},{1... | collective-permute-start | bytes 393224 | tf_op jit(solution)/shard_map/ppermute | solution.py:38
  30.5 5.5 %collective-permute-start.2 = (bf16[16,32,128]{2,1,0:T(8,128)(2,1)S(1)}, bf16[16,32,128]{2,1,0:T(8,128)(2,1)S(1)}, u32[]{:S(2)}, u32[]{:S(2)}) collective-permute-start(bf16[16,32,128]{2,1,0:T(8,128)(2,1)S(1)} %add_convert_fusion.2), channel_id=1, source_target_pairs={{0,96},{16,112},{32,0},{48,16},{64,32},{80,48},{96,64},{112,80},{1... | collective-permute-start | bytes 393224 | tf_op jit(solution)/shard_map/ppermute | solution.py:38
  36.1 2.8 %collective-permute-start.5 = (bf16[16,32,128]{2,1,0:T(8,128)(2,1)S(1)}, bf16[16,32,128]{2,1,0:T(8,128)(2,1)S(1)}, u32[]{:S(2)}, u32[]{:S(2)}) collective-permute-start(bf16[16,32,128]{2,1,0:T(8,128)(2,1)S(1)} %get-tuple-element.32.rest_0_), channel_id=1, source_target_pairs={{0,16},{16,0},{32,48},{48,32},{64,80},{80,64},{96,112},{112,96},{1... | collective-permute-start | bytes 393224 | tf_op jit(solution)/shard_map/ppermute | solution.py:38
  38.9 4.3 %copy-start = (bf16[352,128,128]{2,1,0:T(8,128)(2,1)S(1)}, bf16[352,128,128]{2,1,0:T(8,128)(2,1)}, u32[]{:S(2)}) copy-start(bf16[352,128,128]{2,1,0:T(8,128)(2,1)} %w_ref.7) | copy-start | bytes 34603012
  50.2 6.0 %collective-permute-start.6 = (bf16[16,32,128]{2,1,0:T(8,128)(2,1)S(1)}, bf16[16,32,128]{2,1,0:T(8,128)(2,1)S(1)}, u32[]{:S(2)}, u32[]{:S(2)}) collective-permute-start(bf16[16,32,128]{2,1,0:T(8,128)(2,1)S(1)} %get-tuple-element.19), channel_id=1, source_target_pairs={{0,4},{1,5},{2,6},{3,7},{4,8},{5,9},{6,10},{7,11},{8,12},{9,13},{1... | collective-permute-start | bytes 393224 | tf_op jit(solution)/shard_map/ppermute | solution.py:38
  51.5 8.5 %collective-permute-start.7 = (bf16[16,32,128]{2,1,0:T(8,128)(2,1)S(1)}, bf16[16,32,128]{2,1,0:T(8,128)(2,1)S(1)}, u32[]{:S(2)}, u32[]{:S(2)}) collective-permute-start(bf16[16,32,128]{2,1,0:T(8,128)(2,1)S(1)} %get-tuple-element.20), channel_id=1, source_target_pairs={{0,8},{1,9},{2,10},{3,11},{4,12},{5,13},{6,14},{7,15},{8,0},{9,1},... | collective-permute-start | bytes 393224 | tf_op jit(solution)/shard_map/ppermute | solution.py:38
  53.9 6.1 %collective-permute-start.8 = (bf16[16,32,128]{2,1,0:T(8,128)(2,1)S(1)}, bf16[16,32,128]{2,1,0:T(8,128)(2,1)S(1)}, u32[]{:S(2)}, u32[]{:S(2)}) collective-permute-start(bf16[16,32,128]{2,1,0:T(8,128)(2,1)S(1)} %get-tuple-element.21), channel_id=1, source_target_pairs={{0,12},{1,13},{2,14},{3,15},{4,0},{5,1},{6,2},{7,3},{8,4},{9,5},{1... | collective-permute-start | bytes 393224 | tf_op jit(solution)/shard_map/ppermute | solution.py:38
  60.1 6.5 %collective-permute-start.9 = (bf16[16,32,128]{2,1,0:T(8,128)(2,1)S(1)}, bf16[16,32,128]{2,1,0:T(8,128)(2,1)S(1)}, u32[]{:S(2)}, u32[]{:S(2)}) collective-permute-start(bf16[16,32,128]{2,1,0:T(8,128)(2,1)S(1)} %add_convert_fusion.1), channel_id=1, source_target_pairs={{0,2},{1,3},{2,0},{3,1},{4,6},{5,7},{6,4},{7,5},{8,10},{9,11},{10,... | collective-permute-start | bytes 393224 | tf_op jit(solution)/shard_map/ppermute | solution.py:38
  66.6 5.4 %collective-permute-start.10 = (bf16[16,32,128]{2,1,0:T(8,128)(2,1)S(1)}, bf16[16,32,128]{2,1,0:T(8,128)(2,1)S(1)}, u32[]{:S(2)}, u32[]{:S(2)}) collective-permute-start(bf16[16,32,128]{2,1,0:T(8,128)(2,1)S(1)} %add_convert_fusion), channel_id=1, source_target_pairs={{0,1},{1,0},{2,3},{3,2},{4,5},{5,4},{6,7},{7,6},{8,9},{9,8},{10,11... | collective-permute-start | bytes 393224 | tf_op jit(solution)/shard_map/ppermute | solution.py:38
  72.0 5.1 %collective-permute-start.13 = (bf16[16,32,128]{2,1,0:T(8,128)(2,1)S(1)}, bf16[16,32,128]{2,1,0:T(8,128)(2,1)S(1)}, u32[]{:S(2)}, u32[]{:S(2)}) collective-permute-start(bf16[16,32,128]{2,1,0:T(8,128)(2,1)S(1)} %get-tuple-element.35.rest_0_), channel_id=1, source_target_pairs={{0,4},{1,5},{2,6},{3,7},{4,8},{5,9},{6,10},{7,11},{8,12},{9,13},{1... | collective-permute-start | bytes 393224 | tf_op jit(solution)/shard_map/ppermute | solution.py:38
  73.1 6.0 %collective-permute-start.12 = (bf16[16,32,128]{2,1,0:T(8,128)(2,1)S(1)}, bf16[16,32,128]{2,1,0:T(8,128)(2,1)S(1)}, u32[]{:S(2)}, u32[]{:S(2)}) collective-permute-start(bf16[16,32,128]{2,1,0:T(8,128)(2,1)S(1)} %get-tuple-element.35.rest_0_), channel_id=1, source_target_pairs={{0,8},{1,9},{2,10},{3,11},{4,12},{5,13},{6,14},{7,15},{8,0},{9,1},... | collective-permute-start | bytes 393224 | tf_op jit(solution)/shard_map/ppermute | solution.py:38
  75.4 3.8 %collective-permute-start.11 = (bf16[16,32,128]{2,1,0:T(8,128)(2,1)S(1)}, bf16[16,32,128]{2,1,0:T(8,128)(2,1)S(1)}, u32[]{:S(2)}, u32[]{:S(2)}) collective-permute-start(bf16[16,32,128]{2,1,0:T(8,128)(2,1)S(1)} %get-tuple-element.35.rest_0_), channel_id=1, source_target_pairs={{0,12},{1,13},{2,14},{3,15},{4,0},{5,1},{6,2},{7,3},{8,4},{9,5},{1... | collective-permute-start | bytes 393224 | tf_op jit(solution)/shard_map/ppermute | solution.py:38
  79.2 4.3 %copy-start.1 = (bf16[352,128,128]{2,1,0:T(8,128)(2,1)S(1)}, bf16[352,128,128]{2,1,0:T(8,128)(2,1)}, u32[]{:S(2)}) copy-start(bf16[352,128,128]{2,1,0:T(8,128)(2,1)} %w_ref.7) | copy-start | bytes 34603012
  83.5 94.6 %copy-start.2 = (s32[32,16]{0,1:T(8,128)S(1)}, s32[32,16]{0,1:T(8,128)}, u32[]{:S(2)}) copy-start(s32[32,16]{0,1:T(8,128)} %param.7) | copy-start | bytes 6148
  87.4 7.6 %collective-permute-start.14 = (f32[16,32,128]{2,1,0:T(8,128)S(1)}, f32[16,32,128]{2,1,0:T(8,128)S(1)}, u32[]{:S(2)}, u32[]{:S(2)}) collective-permute-start(f32[16,32,128]{2,1,0:T(8,128)S(1)} %get-tuple-element.23), channel_id=1, source_target_pairs={{0,16},{16,0},{32,48},{48,32},{64,80},{80,64},{96,112},{112,96},{1... | collective-permute-start | bytes 786440 | tf_op jit(solution)/shard_map/ppermute | solution.py:38
  95.1 4.4 %collective-permute-start.15 = (f32[4,32,128]{2,1,0:T(8,128)S(1)}, f32[4,32,128]{2,1,0:T(8,128)S(1)}, u32[]{:S(2)}, u32[]{:S(2)}) collective-permute-start(f32[4,32,128]{2,1,0:T(8,128)S(1)} %get-tuple-element.40), channel_id=1, source_target_pairs={{0,32},{16,48},{32,64},{48,80},{64,96},{80,112},{96,0},{112,16},{1... | collective-permute-start | bytes 196616 | tf_op jit(solution)/shard_map/ppermute | solution.py:38
  96.1 3.4 %collective-permute-start.17 = (f32[4,32,128]{2,1,0:T(8,128)S(1)}, f32[4,32,128]{2,1,0:T(8,128)S(1)}, u32[]{:S(2)}, u32[]{:S(2)}) collective-permute-start(f32[4,32,128]{2,1,0:T(8,128)S(1)} %get-tuple-element.41), channel_id=1, source_target_pairs={{0,96},{16,112},{32,0},{48,16},{64,32},{80,48},{96,64},{112,80},{1... | collective-permute-start | bytes 196616 | tf_op jit(solution)/shard_map/ppermute | solution.py:38
  97.8 4.6 %collective-permute-start.16 = (f32[4,32,128]{2,1,0:T(8,128)S(1)}, f32[4,32,128]{2,1,0:T(8,128)S(1)}, u32[]{:S(2)}, u32[]{:S(2)}) collective-permute-start(f32[4,32,128]{2,1,0:T(8,128)S(1)} %get-tuple-element.42), channel_id=1, source_target_pairs={{0,64},{16,80},{32,96},{48,112},{64,0},{80,16},{96,32},{112,48},{1... | collective-permute-start | bytes 196616 | tf_op jit(solution)/shard_map/ppermute | solution.py:38
  102.5 7.1 %collective-permute-start.18 = (f32[4,32,128]{2,1,0:T(8,128)S(1)}, f32[4,32,128]{2,1,0:T(8,128)S(1)}, u32[]{:S(2)}, u32[]{:S(2)}) collective-permute-start(f32[4,32,128]{2,1,0:T(8,128)S(1)} %fusion.1), channel_id=1, source_target_pairs={{0,128},{16,144},{32,160},{48,176},{64,192},{80,208},{96,224},{112... | collective-permute-start | bytes 196616 | tf_op jit(solution)/shard_map/ppermute | solution.py:38
  109.6 4.1 %collective-permute-start.21 = (bf16[4,32,128]{2,1,0:T(8,128)(2,1)S(1)}, bf16[4,32,128]{2,1,0:T(8,128)(2,1)S(1)}, u32[]{:S(2)}, u32[]{:S(2)}) collective-permute-start(bf16[4,32,128]{2,1,0:T(8,128)(2,1)S(1)} %get-tuple-element.30), channel_id=1, source_target_pairs={{0,32},{16,48},{32,64},{48,80},{64,96},{80,112},{96,0},{112,16},{1... | collective-permute-start | bytes 98312 | tf_op jit(solution)/shard_map/ppermute | solution.py:38
  110.1 4.3 %collective-permute-start.20 = (bf16[4,32,128]{2,1,0:T(8,128)(2,1)S(1)}, bf16[4,32,128]{2,1,0:T(8,128)(2,1)S(1)}, u32[]{:S(2)}, u32[]{:S(2)}) collective-permute-start(bf16[4,32,128]{2,1,0:T(8,128)(2,1)S(1)} %get-tuple-element.30), channel_id=1, source_target_pairs={{0,64},{16,80},{32,96},{48,112},{64,0},{80,16},{96,32},{112,48},{1... | collective-permute-start | bytes 98312 | tf_op jit(solution)/shard_map/ppermute | solution.py:38
  111.9 2.8 %collective-permute-start.19 = (bf16[4,32,128]{2,1,0:T(8,128)(2,1)S(1)}, bf16[4,32,128]{2,1,0:T(8,128)(2,1)S(1)}, u32[]{:S(2)}, u32[]{:S(2)}) collective-permute-start(bf16[4,32,128]{2,1,0:T(8,128)(2,1)S(1)} %get-tuple-element.30), channel_id=1, source_target_pairs={{0,96},{16,112},{32,0},{48,16},{64,32},{80,48},{96,64},{112,80},{1... | collective-permute-start | bytes 98312 | tf_op jit(solution)/shard_map/ppermute | solution.py:38
  114.7 6.6 %collective-permute-start.22 = (bf16[16,32,128]{2,1,0:T(8,128)(2,1)S(1)}, bf16[16,32,128]{2,1,0:T(8,128)(2,1)S(1)}, u32[]{:S(2)}, u32[]{:S(2)}) collective-permute-start(bf16[16,32,128]{2,1,0:T(8,128)(2,1)S(1)} %pad_maximum_fusion.rest_0_), channel_id=1, source_target_pairs={{0,16},{16,0},{32,48},{48,32},{64,80},{80,64},{96,112},{112,96},{1... | collective-permute-start | bytes 393224 | tf_op jit(solution)/shard_map/ppermute | solution.py:38
  128.3 8.8 %collective-permute-start.23 = (f32[16,32,128]{2,1,0:T(8,128)S(1)}, f32[16,32,128]{2,1,0:T(8,128)S(1)}, u32[]{:S(2)}, u32[]{:S(2)}) collective-permute-start(f32[16,32,128]{2,1,0:T(8,128)S(1)} %get-tuple-element.25), channel_id=1, source_target_pairs={{0,4},{1,5},{2,6},{3,7},{4,8},{5,9},{6,10},{7,11},{8,12},{9,13},{1... | collective-permute-start | bytes 786440 | tf_op jit(solution)/shard_map/ppermute | solution.py:38
  129.6 13.8 %collective-permute-start.24 = (f32[16,32,128]{2,1,0:T(8,128)S(1)}, f32[16,32,128]{2,1,0:T(8,128)S(1)}, u32[]{:S(2)}, u32[]{:S(2)}) collective-permute-start(f32[16,32,128]{2,1,0:T(8,128)S(1)} %get-tuple-element.26), channel_id=1, source_target_pairs={{0,8},{1,9},{2,10},{3,11},{4,12},{5,13},{6,14},{7,15},{8,0},{9,1},... | collective-permute-start | bytes 786440 | tf_op jit(solution)/shard_map/ppermute | solution.py:38
  131.8 11.7 %collective-permute-start.25 = (f32[16,32,128]{2,1,0:T(8,128)S(1)}, f32[16,32,128]{2,1,0:T(8,128)S(1)}, u32[]{:S(2)}, u32[]{:S(2)}) collective-permute-start(f32[16,32,128]{2,1,0:T(8,128)S(1)} %get-tuple-element.27), channel_id=1, source_target_pairs={{0,12},{1,13},{2,14},{3,15},{4,0},{5,1},{6,2},{7,3},{8,4},{9,5},{1... | collective-permute-start | bytes 786440 | tf_op jit(solution)/shard_map/ppermute | solution.py:38
  143.6 3.4 %collective-permute-start.28 = (f32[4,32,128]{2,1,0:T(8,128)S(1)}, f32[4,32,128]{2,1,0:T(8,128)S(1)}, u32[]{:S(2)}, u32[]{:S(2)}) collective-permute-start(f32[4,32,128]{2,1,0:T(8,128)S(1)} %get-tuple-element.36), channel_id=1, source_target_pairs={{0,3},{1,0},{2,1},{3,2},{4,7},{5,4},{6,5},{7,6},{8,11},{9,8},{10,9... | collective-permute-start | bytes 196616 | tf_op jit(solution)/shard_map/ppermute | solution.py:38
  145.4 6.3 %collective-permute-start.27 = (f32[4,32,128]{2,1,0:T(8,128)S(1)}, f32[4,32,128]{2,1,0:T(8,128)S(1)}, u32[]{:S(2)}, u32[]{:S(2)}) collective-permute-start(f32[4,32,128]{2,1,0:T(8,128)S(1)} %get-tuple-element.37), channel_id=1, source_target_pairs={{0,2},{1,3},{2,0},{3,1},{4,6},{5,7},{6,4},{7,5},{8,10},{9,11},{10,... | collective-permute-start | bytes 196616 | tf_op jit(solution)/shard_map/ppermute | solution.py:38
  145.4 6.3 %collective-permute-start.26 = (f32[4,32,128]{2,1,0:T(8,128)S(1)}, f32[4,32,128]{2,1,0:T(8,128)S(1)}, u32[]{:S(2)}, u32[]{:S(2)}) collective-permute-start(f32[4,32,128]{2,1,0:T(8,128)S(1)} %get-tuple-element.38), channel_id=1, source_target_pairs={{0,1},{1,2},{2,3},{3,0},{4,5},{5,6},{6,7},{7,4},{8,9},{9,10},{10,1... | collective-permute-start | bytes 196616 | tf_op jit(solution)/shard_map/ppermute | solution.py:38
  152.4 25.6 %all-to-all-start = ((f32[256,1,128]{2,1,0:T(1,128)}), f32[256,1,128]{2,1,0:T(1,128)S(1)}, u32[]{:S(2)}, u32[]{:S(2)}) async-start(f32[256,1,128]{2,1,0:T(1,128)} %bitcast.4), calls=%async_computation | async-start | bytes 262144 | tf_op jit(solution)/shard_map/all_to_all | solution.py:293

commit v3 on v2

--- a/solution.py
+++ b/solution.py
@@ -29,22 +29,16 @@
     return (index >> part[0]) & ((1 << part[1]) - 1)
 
 
-def shifted(x, axis, part, by):
-    size = 1 << part[1]
-    perm = []
-    for i in range(16):
-        old = field(i, part)
-        perm.append((i, i + (((old + by) % size - old) << part[0])))
-    return lax.ppermute(x, axis, perm)
+def swapped(x, axis, part, by):
+    return lax.ppermute(x, axis, [(i, i ^ (by << part[0])) for i in range(16)])
 
 
 def gathered(x, axis, part):
-    size = 1 << part[1]
-    return [x] + [shifted(x, axis, part, size - by) for by in range(1, size)]
+    return [x] + [swapped(x, axis, part, by) for by in range(1, 1 << part[1])]
 
 
 def exchanged(chunks, axis, part):
-    return [chunks[0]] + [shifted(c, axis, part, by) for by, c in enumerate(chunks) if by]
+    return [chunks[0]] + [swapped(c, axis, part, by) for by, c in enumerate(chunks) if by]
 
 
 def added(parts):
@@ -52,6 +46,22 @@
     for p in parts[1:]:
         total = total + p.astype(F32)
     return total
+
+
+def add_kernel(held_ref, *refs, n_in):
+    total = added([ref[...] for ref in refs[:n_in]])
+    for out in refs[n_in:]:
+        out[...] = total.astype(out.dtype)
+
+
+def add_parts(held, parts, dtypes):
+    return pl.pallas_call(
+        functools.partial(add_kernel, n_in=len(parts)),
+        in_specs=[VMEM] * (1 + len(parts)),
+        out_specs=[VMEM] * len(dtypes),
+        out_shape=[jax.ShapeDtypeStruct(parts[0].shape, dtype) for dtype in dtypes],
+        compiler_params=pltpu.CompilerParams(vmem_limit_bytes=8 * MIB),
+    )(held, *parts)
 
 
 def seed_columns(seed_ref):
@@ -77,7 +87,7 @@
     for j in range(count):
         prod = lax.dot_general(
             x_ref[src_ref[first + j]],
-            w_ref[j] if w_ref.shape[0] == count else w_ref[first + j],
+            w_ref[first + j],
             (((1,), (contract,)), ((), ())),
             preferred_element_type=F32,
         )
@@ -92,31 +102,36 @@
         start += rows
 
 
-def first_kernel(src_ref, dst_ref, base_ref, seed_ref, w_ref, *rest, scale):
-    *out_refs, x_ref, wide_ref, acc_ref = rest
-    step = pl.program_id(0)
-
-    @pl.when(step == 0)
-    def _():
-        acc_ref[...] = jnp.zeros_like(acc_ref)
-        for k, column in enumerate(seed_columns(seed_ref)):
-            wide_ref[k] = jnp.broadcast_to(column - base_ref[0], wide_ref.shape[1:])
-
-        def body(t, carry):
-            ids = t * EDGE + lax.broadcasted_iota(jnp.int32, wide_ref.shape[1:], 1)
-            count = jnp.zeros(wide_ref.shape[1:], F32)
-            for k in range(wide_ref.shape[0]):
-                count = jnp.where(wide_ref[k] == ids, count + 1.0, count)
-            x_ref[t] = (count * scale).astype(x_ref.dtype)
-            return carry
-
-        lax.fori_loop(0, x_ref.shape[0], body, 0)
-
-    multiply_tiles(src_ref, dst_ref, x_ref, w_ref, acc_ref, 0, step * STREAM, STREAM)
-
-    @pl.when(step == pl.num_programs(0) - 1)
-    def _():
-        store_chunks(acc_ref, out_refs, 1.0)
+def first_kernel(src_ref, dst_ref, base_ref, seed_ref, w_ref, held_ref, *rest, scale):
+    *out_refs, x_ref, wide_ref, acc_ref, sem = rest
+    copies = []
+    for i in range(held_ref.shape[0] // STREAM):
+        part = pl.ds(i * STREAM, STREAM)
+        copies.append(pltpu.make_async_copy(w_ref.at[part], held_ref.at[part], sem.at[i]))
+        copies[-1].start()
+    acc_ref[...] = jnp.zeros_like(acc_ref)
+    last = x_ref.shape[0] * EDGE
+    for k, column in enumerate(seed_columns(seed_ref)):
+        local = column - base_ref[0]
+        local = jnp.where((local >= 0) & (local < last), local, -1)
+        wide_ref[k] = jnp.broadcast_to(local, wide_ref.shape[1:]).astype(wide_ref.dtype)
+
+    lanes = lax.broadcasted_iota(jnp.int32, wide_ref.shape[1:], 1)
+
+    def body(t, carry):
+        ids = (t * EDGE + lanes).astype(wide_ref.dtype)
+        count = jnp.zeros(ids.shape, ids.dtype)
+        one = jnp.ones(ids.shape, ids.dtype)
+        for k in range(wide_ref.shape[0]):
+            count = count + jnp.where(wide_ref[k] == ids, one, jnp.zeros_like(one))
+        x_ref[t ^ base_ref[1]] = (count.astype(F32) * scale).astype(x_ref.dtype)
+        return carry
+
+    lax.fori_loop(0, x_ref.shape[0], body, 0, unroll=4)
+    for i, copy in enumerate(copies):
+        copy.wait()
+        multiply_tiles(src_ref, dst_ref, x_ref, held_ref, acc_ref, 0, i * STREAM, STREAM)
+    store_chunks(acc_ref, out_refs, 1.0)
 
 
 def first_pass(src, dst, base, seed_t, w, n_src, outs, scale):
@@ -124,22 +139,17 @@
     n_dst = sum(rows for rows, _ in outs)
     return pl.pallas_call(
         functools.partial(first_kernel, scale=scale),
-        grid_spec=pltpu.PrefetchScalarGridSpec(
-            num_scalar_prefetch=3,
-            grid=(w.shape[0] // STREAM,),
-            in_specs=[
-                pl.BlockSpec(seed_t.shape, lambda i, *_: (0, 0)),
-                pl.BlockSpec((STREAM, EDGE, EDGE), lambda i, *_: (i, 0, 0)),
-            ],
-            out_specs=[pl.BlockSpec((rows, seeds, EDGE), lambda i, *_: (0, 0, 0)) for rows, _ in outs],
-            scratch_shapes=[
-                pltpu.VMEM((n_src, seeds, EDGE), BF16),
-                pltpu.VMEM((seed_t.shape[0], seeds, EDGE), jnp.int32),
-                pltpu.VMEM((n_dst, seeds, EDGE), F32),
-            ],
-        ),
-        out_shape=[jax.ShapeDtypeStruct((rows, seeds, EDGE), dtype) for rows, dtype in outs],
-        compiler_params=pltpu.CompilerParams(vmem_limit_bytes=56 * MIB),
+        in_specs=[SMEM] * 3 + [VMEM, pl.BlockSpec(memory_space=pltpu.HBM)],
+        out_specs=[VMEM] * (1 + len(outs)),
+        scratch_shapes=[
+            pltpu.VMEM((n_src, seeds, EDGE), BF16),
+            pltpu.VMEM((seed_t.shape[0], seeds, EDGE), jnp.int16),
+            pltpu.VMEM((n_dst, seeds, EDGE), F32),
+            pltpu.SemaphoreType.DMA((w.shape[0] // STREAM,)),
+        ],
+        out_shape=[pltpu.VMEM(w.shape, w.dtype)]
+        + [jax.ShapeDtypeStruct((rows, seeds, EDGE), dtype) for rows, dtype in outs],
+        compiler_params=pltpu.CompilerParams(vmem_limit_bytes=49 * MIB),
     )(src, dst, base, seed_t, w)
 
 
@@ -235,7 +245,7 @@
     items = I_DEV * n_rows * n_cols
     scale = float(np.float32((users / SEEDK) ** 0.5))
     seed_t = seed_users.T
-    row_base = (row * (U_DEV * n_cols)).reshape(1)
+    row_base = jnp.stack([row * (U_DEV * n_cols), field(col, X) * 16])
     own_base = ((row * n_cols + col) * U_DEV).reshape(1)
     core, y, zhi = field(row, CORE), field(row, Y), field(row, ZHI)
     zlo, x = field(col, ZLO), field(col, X)
@@ -243,39 +253,38 @@
     t_half = (((tile_cols >> 1) & 1) ^ core) * 16
     t_zhi, t_y, t_q = tile_cols >> 4, (tile_cols >> 2) & 3, tile_cols & 1
     item_whole = t_half + t_zhi * 8 + t_y * 2 + t_q
-    item_by_y = t_half + ((t_y - y) & 3) * 4 + t_zhi * 2 + t_q
-    t_x = ((tile_rows >> 4) - x) & 3
+    item_by_y = t_half + (t_y ^ y) * 4 + t_zhi * 2 + t_q
+    t_x = (tile_rows >> 4) ^ x
     user_whole = t_x * 16 + (tile_rows & 15)
-    user_by_z = t_x * 16 + ((((tile_rows >> 2) & 3) - zlo) & 3) * 4 + (tile_rows & 3)
-
-    keep, send = first_pass(
-        tile_rows, item_whole, row_base, seed_t, tile_values, 64, [(16, BF16)] * 2, scale
-    )
-    part = added(exchanged([keep, send], "row", CORE)).astype(BF16)
-    part = added(gathered(part, "row", ZHI)).astype(BF16)
-    x1_all = added(gathered(part, "row", Y))
+    user_by_z = t_x * 16 + (((tile_rows >> 2) & 3) ^ zlo) * 4 + (tile_rows & 3)
+
+    held, keep, send = first_pass(
+        user_whole, item_whole, row_base, seed_t, tile_values, 64, [(16, BF16)] * 2, scale
+    )
+    (part,) = add_parts(held, exchanged([keep, send], "row", CORE), [BF16])
+    (part,) = add_parts(held, gathered(part, "row", ZHI), [BF16])
+    x1_all, part = add_parts(held, gathered(part, "row", Y), [F32, BF16])
     x1 = lax.dynamic_slice_in_dim(x1_all, (zhi * 4 + y) * 2, 2, 0)
 
     chunks = tile_pass(
-        item_whole, user_whole, tile_values, gathered(x1_all.astype(BF16), "row", CORE), 1, [(16, BF16)] * 4
-    )
-    part = added(exchanged(chunks, "col", X)).astype(BF16)
-    for bit in (1, 0):
-        part = added(gathered(part, "col", (bit, 1)))
-        u1 = lax.dynamic_slice_in_dim(part, zlo * 4, 4, 0)
-        part = part.astype(BF16)
+        item_whole, user_whole, held, gathered(part, "row", CORE), 1, [(16, BF16)] * 4
+    )
+    (part,) = add_parts(held, exchanged(chunks, "col", X), [BF16])
+    (part,) = add_parts(held, gathered(part, "col", (1, 1)), [BF16])
+    u1_all, part = add_parts(held, gathered(part, "col", (0, 1)), [F32, BF16])
+    u1 = lax.dynamic_slice_in_dim(u1_all, zlo * 4, 4, 0)
 
     chunks = tile_pass(
-        user_whole, item_by_y, tile_values, gathered(part, "col", X), 0, [(16, F32)] * 2
-    )
-    part = added(exchanged(chunks, "row", CORE))
-    part = added(exchanged([part[i * 4 : i * 4 + 4] for i in range(4)], "row", Y))
-    part = added(gathered(part, "row", ZHI))
-    y2 = lax.dynamic_slice_in_dim(part, zhi * 2, 2, 0)
-    half = jnp.concatenate(gathered(part.astype(BF16), "row", Y), axis=0)
+        user_whole, item_by_y, held, gathered(part, "col", X), 0, [(16, F32)] * 2
+    )
+    (part,) = add_parts(held, exchanged(chunks, "row", CORE), [F32])
+    (part,) = add_parts(held, exchanged([part[i * 4 : i * 4 + 4] for i in range(4)], "row", Y), [F32])
+    y2_all, part = add_parts(held, gathered(part, "row", ZHI), [F32, BF16])
+    y2 = lax.dynamic_slice_in_dim(y2_all, zhi * 2, 2, 0)
+    half = jnp.concatenate(gathered(part, "row", Y), axis=0)
 
     chunks = tile_pass(
-        item_by_y, user_by_z, tile_values, gathered(half, "row", CORE), 1, [(16, F32)] * 4
+        item_by_y, user_by_z, held, gathered(half, "row", CORE), 1, [(16, F32)] * 4
     )
     part = added(exchanged(chunks, "col", X))
     got = exchanged([part[i * 4 : i * 4 + 4] for i in range(4)], "col", ZLO)

time: 179 us -> 169 us (0.944)
  local copies, waits for them, and re-layouts: 8.62 us -> 1.01 us
  waiting for transfers between devices: 63 us -> 69.5 us
  starting transfers between devices: 74 us -> 68.8 us
  Pallas kernels: 29.9 us -> 26.9 us
    unnamed x10 -> x11, local copies, waits for them, and re-layouts: 8.57 us -> 0.94 us
    ppermute x29, waiting for transfers between devices: 50.2 us -> 56.6 us  [swapped(): return lax.ppermute(x, axis, [(i, i ^ by << part[0]) for i in range(16)])]
    ppermute x29, starting transfers between devices: 61.3 us -> 58.1 us  [swapped(): return lax.ppermute(x, axis, [(i, i ^ by << part[0]) for i in range(16)])]
    pallas_call x1 -> x10, Pallas kernels: 10.3 us -> 7.36 us  [the longest x1 7.03 us: first_pass(): pl.pallas_call(functools.partial(first_kernel, scale=scale), in_specs=[SM...]
    all_to_all x1, starting transfers between devices: 12.7 us -> 10.6 us  [per_device(): lax.all_to_all(stat.reshape(n_rows * n_cols, 1, EDGE), ('row', 'col'), 0, 0)]
  transfers between devices with their start and end apart: 30 -> 30, of which waited for: 26 -> 25; matrix products, arithmetic and copies ran while one was open for 0% -> 0% of each run, Pallas kernels for 0% -> 0%
where the time goes in v3:
time: 169 us
  waiting for transfers between devices  69.5 us (41%)
  starting transfers between devices  68.8 us (41%)
  Pallas kernels  26.9 us (16%)
  other arithmetic  1.96 us (1%)
    ppermute x29, starting transfers between devices, swapped(): return lax.ppermute(x, axis, [(i, i ^ by << part[0]) for i in range(16)])  58.1 us
    ppermute x29, waiting for transfers between devices, swapped(): return lax.ppermute(x, axis, [(i, i ^ by << part[0]) for i in range(16)])  56.6 us
    pallas_call x3, Pallas kernels, tile_pass(): pl.pallas_call(functools.partial(pass_kernel, contract=contract, n_in=len...  17.9 us
    all_to_all x1, waiting for transfers between devices, per_device(): lax.all_to_all(stat.reshape(n_rows * n_cols, 1, EDGE), ('row', 'col'), 0, 0)  12.9 us
    all_to_all x1, starting transfers between devices, per_device(): lax.all_to_all(stat.reshape(n_rows * n_cols, 1, EDGE), ('row', 'col'), 0, 0)  10.6 us
    pallas_call x1, Pallas kernels, first_pass(): pl.pallas_call(functools.partial(first_kernel, scale=scale), in_specs=[SM...  7.03 us
  transfers between devices with their start and end apart: 30, of which 25 were waited for; matrix products, arithmetic and copies ran while one was open for 0% of the time, Pallas kernels for 0%

profile of v3, /device:TPU:1, one launch (start us, length us, event | category | flops | bytes accessed | tf_op | source)
XLA Modules:
  0.0 168.9 jit_solution(10784172664381364748)
XLA Ops:
  1.2 1.3 and_add_fusion
  2.5 7.0 %shard_map.59 = (bf16[352,128,128]{2,1,0:T(8,128)(2,1)S(1)}, bf16[16,32,128]{2,1,0:T(8,128)(2,1)}, bf16[16,32,128]{2,1,0:T(8,128)(2,1)}) custom-call(s32[352]{0:T(512)} %get-tuple-element.53.src_ref.dst_ref, s32[352]{0:T(512)} %get-tuple-element.56.dst_ref.src_ref, s32[2]{0:T(128)} %pad_add_fusion.base_ref, s32[16,32]{1,0:T(8,128)} %bitcast.9, ...), custom_call_target="tpu_custom_call" | custom-call | tf_op jit(solution)/shard_map/pallas_call | solution.py:140
  9.5 3.3 %collective-permute-start = (bf16[16,32,128]{2,1,0:T(8,128)(2,1)}, bf16[16,32,128]{2,1,0:T(8,128)(2,1)S(1)}, u32[]{:S(2)}, u32[]{:S(2)}) collective-permute-start(bf16[16,32,128]{2,1,0:T(8,128)(2,1)} %get-tuple-element.25), channel_id=1, source_target_pairs={{0,16},{16,0},{32,48},{48,32},{64,80},{80,64},{96,112},{112,96},{1... | collective-permute-start | bytes 393224 | tf_op jit(solution)/shard_map/ppermute | solution.py:33
  12.9 1.2 collective-permute-done.refs_1_
  15.0 5.3 %collective-permute-start.1 = (bf16[16,32,128]{2,1,0:T(8,128)(2,1)S(1)}, bf16[16,32,128]{2,1,0:T(8,128)(2,1)S(1)}, u32[]{:S(2)}, u32[]{:S(2)}) collective-permute-start(bf16[16,32,128]{2,1,0:T(8,128)(2,1)S(1)} %shard_map.60.refs_0_), channel_id=1, source_target_pairs={{0,128},{16,144},{32,160},{48,176},{64,192},{80,208},{96,224},{112... | collective-permute-start | bytes 393224 | tf_op jit(solution)/shard_map/ppermute | solution.py:33
  20.3 3.5 %collective-permute-done.1.refs_1_ = bf16[16,32,128]{2,1,0:T(8,128)(2,1)S(1)} collective-permute-done((bf16[16,32,128]{2,1,0:T(8,128)(2,1)S(1)}, bf16[16,32,128]{2,1,0:T(8,128)(2,1)S(1)}, u32[]{:S(2)}, u32[]{:S(2)}) %collective-permute-start.1) | collective-permute-done | bytes 131104 | tf_op jit(solution)/shard_map/ppermute | solution.py:33
  23.8 2.9 %collective-permute-start.4 = (bf16[16,32,128]{2,1,0:T(8,128)(2,1)S(1)}, bf16[16,32,128]{2,1,0:T(8,128)(2,1)S(1)}, u32[]{:S(2)}, u32[]{:S(2)}) collective-permute-start(bf16[16,32,128]{2,1,0:T(8,128)(2,1)S(1)} %shard_map.61.refs_0_), channel_id=1, source_target_pairs={{0,96},{16,112},{32,64},{48,80},{64,32},{80,48},{96,0},{112,16},{1... | collective-permute-start | bytes 393224 | tf_op jit(solution)/shard_map/ppermute | solution.py:33
  27.4 4.8 %collective-permute-done.4.refs_3_ = bf16[16,32,128]{2,1,0:T(8,128)(2,1)S(1)} collective-permute-done((bf16[16,32,128]{2,1,0:T(8,128)(2,1)S(1)}, bf16[16,32,128]{2,1,0:T(8,128)(2,1)S(1)}, u32[]{:S(2)}, u32[]{:S(2)}) %collective-permute-start.4) | collective-permute-done | bytes 131104 | tf_op jit(solution)/shard_map/ppermute | solution.py:33
  32.3 3.4 %collective-permute-start.5 = (bf16[16,32,128]{2,1,0:T(8,128)(2,1)S(1)}, bf16[16,32,128]{2,1,0:T(8,128)(2,1)S(1)}, u32[]{:S(2)}, u32[]{:S(2)}) collective-permute-start(bf16[16,32,128]{2,1,0:T(8,128)(2,1)S(1)} %get-tuple-element.27.rest_0_), channel_id=1, source_target_pairs={{0,16},{16,0},{32,48},{48,32},{64,80},{80,64},{96,112},{112,96},{1... | collective-permute-start | bytes 393224 | tf_op jit(solution)/shard_map/ppermute | solution.py:33
  35.7 1.0 collective-permute-done.5.rest_1_
  36.7 7.0 %shard_map.63 = (bf16[16,32,128]{2,1,0:T(8,128)(2,1)S(1)}, bf16[16,32,128]{2,1,0:T(8,128)(2,1)S(1)}, bf16[16,32,128]{2,1,0:T(8,128)(2,1)S(1)}, bf16[16,32,128]{2,1,0:T(8,128)(2,1)S(1)}) custom-call(s32[352]{0:T(512)S(1)} %copy-done.3, s32[352]{0:T(512)S(1)} %copy-done.2, bf16[352,128,128]{2,1,0:T(8,128)(2,1)S(1)} %get-tuple-element.23.held_ref.w_ref, ...), custom_call_target="tpu_custom_call" | custom-call | tf_op jit(solution)/shard_map/pallas_call | solution.py:176
  43.7 1.3 collective-permute-start.6
  45.0 2.5 %collective-permute-start.7 = (bf16[16,32,128]{2,1,0:T(8,128)(2,1)S(1)}, bf16[16,32,128]{2,1,0:T(8,128)(2,1)S(1)}, u32[]{:S(2)}, u32[]{:S(2)}) collective-permute-start(bf16[16,32,128]{2,1,0:T(8,128)(2,1)S(1)} %get-tuple-element.30), channel_id=1, source_target_pairs={{0,8},{1,9},{2,10},{3,11},{4,12},{5,13},{6,14},{7,15},{8,0},{9,1},... | collective-permute-start | bytes 393224 | tf_op jit(solution)/shard_map/ppermute | solution.py:33
  48.5 5.1 %collective-permute-done.7.refs_2_ = bf16[16,32,128]{2,1,0:T(8,128)(2,1)S(1)} collective-permute-done((bf16[16,32,128]{2,1,0:T(8,128)(2,1)S(1)}, bf16[16,32,128]{2,1,0:T(8,128)(2,1)S(1)}, u32[]{:S(2)}, u32[]{:S(2)}) %collective-permute-start.7) | collective-permute-done | bytes 131104 | tf_op jit(solution)/shard_map/ppermute | solution.py:33
  53.5 2.5 %collective-permute-done.8.refs_3_ = bf16[16,32,128]{2,1,0:T(8,128)(2,1)S(1)} collective-permute-done((bf16[16,32,128]{2,1,0:T(8,128)(2,1)S(1)}, bf16[16,32,128]{2,1,0:T(8,128)(2,1)S(1)}, u32[]{:S(2)}, u32[]{:S(2)}) %collective-permute-start.8) | collective-permute-done | bytes 131104 | tf_op jit(solution)/shard_map/ppermute | solution.py:33
  56.1 4.1 %collective-permute-start.9 = (bf16[16,32,128]{2,1,0:T(8,128)(2,1)S(1)}, bf16[16,32,128]{2,1,0:T(8,128)(2,1)S(1)}, u32[]{:S(2)}, u32[]{:S(2)}) collective-permute-start(bf16[16,32,128]{2,1,0:T(8,128)(2,1)S(1)} %shard_map.64.refs_0_), channel_id=1, source_target_pairs={{0,2},{1,3},{2,0},{3,1},{4,6},{5,7},{6,4},{7,5},{8,10},{9,11},{10,... | collective-permute-start | bytes 393224 | tf_op jit(solution)/shard_map/ppermute | solution.py:33
  60.2 2.9 %collective-permute-done.9.refs_1_ = bf16[16,32,128]{2,1,0:T(8,128)(2,1)S(1)} collective-permute-done((bf16[16,32,128]{2,1,0:T(8,128)(2,1)S(1)}, bf16[16,32,128]{2,1,0:T(8,128)(2,1)S(1)}, u32[]{:S(2)}, u32[]{:S(2)}) %collective-permute-start.9) | collective-permute-done | bytes 131104 | tf_op jit(solution)/shard_map/ppermute | solution.py:33
  63.1 1.7 %collective-permute-start.10 = (bf16[16,32,128]{2,1,0:T(8,128)(2,1)S(1)}, bf16[16,32,128]{2,1,0:T(8,128)(2,1)S(1)}, u32[]{:S(2)}, u32[]{:S(2)}) collective-permute-start(bf16[16,32,128]{2,1,0:T(8,128)(2,1)S(1)} %shard_map.65.refs_0_), channel_id=1, source_target_pairs={{0,1},{1,0},{2,3},{3,2},{4,5},{5,4},{6,7},{7,6},{8,9},{9,8},{10,11... | collective-permute-start | bytes 393224 | tf_op jit(solution)/shard_map/ppermute | solution.py:33
  64.8 3.4 %collective-permute-done.10.refs_1_ = bf16[16,32,128]{2,1,0:T(8,128)(2,1)S(1)} collective-permute-done((bf16[16,32,128]{2,1,0:T(8,128)(2,1)S(1)}, bf16[16,32,128]{2,1,0:T(8,128)(2,1)S(1)}, u32[]{:S(2)}, u32[]{:S(2)}) %collective-permute-start.10) | collective-permute-done | bytes 131104 | tf_op jit(solution)/shard_map/ppermute | solution.py:33
  68.3 2.4 %collective-permute-start.13 = (bf16[16,32,128]{2,1,0:T(8,128)(2,1)S(1)}, bf16[16,32,128]{2,1,0:T(8,128)(2,1)S(1)}, u32[]{:S(2)}, u32[]{:S(2)}) collective-permute-start(bf16[16,32,128]{2,1,0:T(8,128)(2,1)S(1)} %get-tuple-element.32.rest_0_), channel_id=1, source_target_pairs={{0,12},{1,13},{2,14},{3,15},{4,8},{5,9},{6,10},{7,11},{8,4},{9,5},... | collective-permute-start | bytes 393224 | tf_op jit(solution)/shard_map/ppermute | solution.py:33
  71.6 2.3 %collective-permute-done.13.rest_3_ = bf16[16,32,128]{2,1,0:T(8,128)(2,1)S(1)} collective-permute-done((bf16[16,32,128]{2,1,0:T(8,128)(2,1)S(1)}, bf16[16,32,128]{2,1,0:T(8,128)(2,1)S(1)}, u32[]{:S(2)}, u32[]{:S(2)}) %collective-permute-start.13) | collective-permute-done | bytes 131104 | tf_op jit(solution)/shard_map/ppermute | solution.py:33
  73.9 2.0 %collective-permute-done.12.rest_2_ = bf16[16,32,128]{2,1,0:T(8,128)(2,1)S(1)} collective-permute-done((bf16[16,32,128]{2,1,0:T(8,128)(2,1)S(1)}, bf16[16,32,128]{2,1,0:T(8,128)(2,1)S(1)}, u32[]{:S(2)}, u32[]{:S(2)}) %collective-permute-start.12) | collective-permute-done | bytes 131104 | tf_op jit(solution)/shard_map/ppermute | solution.py:33
  75.9 3.9 %shard_map.67 = (f32[16,32,128]{2,1,0:T(8,128)S(1)}, f32[16,32,128]{2,1,0:T(8,128)S(1)}) custom-call(s32[352]{0:T(512)S(1)} %copy-done.2, s32[352]{0:T(512)S(1)} %get-tuple-element.57.dst_ref.src_ref, bf16[352,128,128]{2,1,0:T(8,128)(2,1)S(1)} %get-tuple-element.23.held_ref.w_ref, bf16[16,32,128]{2,1,0:T(8,128)(2,1)S(1)} %get-tuple-element.32.rest_0_, ...), custom_call_target="tpu_custom_call" | custom-call | tf_op jit(solution)/shard_map/pallas_call | solution.py:176
  79.9 5.6 %collective-permute-start.14 = (f32[16,32,128]{2,1,0:T(8,128)S(1)}, f32[16,32,128]{2,1,0:T(8,128)S(1)}, u32[]{:S(2)}, u32[]{:S(2)}) collective-permute-start(f32[16,32,128]{2,1,0:T(8,128)S(1)} %get-tuple-element.34), channel_id=1, source_target_pairs={{0,16},{16,0},{32,48},{48,32},{64,80},{80,64},{96,112},{112,96},{1... | collective-permute-start | bytes 786440 | tf_op jit(solution)/shard_map/ppermute | solution.py:33
  85.5 1.2 collective-permute-done.14.refs_1_
  86.7 1.7 %collective-permute-start.17 = (f32[4,32,128]{2,1,0:T(8,128)S(1)}, f32[4,32,128]{2,1,0:T(8,128)S(1)}, u32[]{:S(2)}, u32[]{:S(2)}) collective-permute-start(f32[4,32,128]{2,1,0:T(8,128)S(1)} %get-tuple-element.48), channel_id=1, source_target_pairs={{0,96},{16,112},{32,64},{48,80},{64,32},{80,48},{96,0},{112,16},{1... | collective-permute-start | bytes 196616 | tf_op jit(solution)/shard_map/ppermute | solution.py:33
  88.8 1.3 collective-permute-start.15
  90.0 1.1 collective-permute-done.17.refs_3_
  91.1 2.0 %collective-permute-done.16.refs_2_ = f32[4,32,128]{2,1,0:T(8,128)S(1)} collective-permute-done((f32[4,32,128]{2,1,0:T(8,128)S(1)}, f32[4,32,128]{2,1,0:T(8,128)S(1)}, u32[]{:S(2)}, u32[]{:S(2)}) %collective-permute-start.16) | collective-permute-done | bytes 65568 | tf_op jit(solution)/shard_map/ppermute | solution.py:33
  93.1 5.0 %collective-permute-start.18 = (f32[4,32,128]{2,1,0:T(8,128)S(1)}, f32[4,32,128]{2,1,0:T(8,128)S(1)}, u32[]{:S(2)}, u32[]{:S(2)}) collective-permute-start(f32[4,32,128]{2,1,0:T(8,128)S(1)} %shard_map.69.refs_0_), channel_id=1, source_target_pairs={{0,128},{16,144},{32,160},{48,176},{64,192},{80,208},{96,224},{112... | collective-permute-start | bytes 196616 | tf_op jit(solution)/shard_map/ppermute | solution.py:33
  98.1 2.1 %collective-permute-done.18.refs_1_ = f32[4,32,128]{2,1,0:T(8,128)S(1)} collective-permute-done((f32[4,32,128]{2,1,0:T(8,128)S(1)}, f32[4,32,128]{2,1,0:T(8,128)S(1)}, u32[]{:S(2)}, u32[]{:S(2)}) %collective-permute-start.18) | collective-permute-done | bytes 65568 | tf_op jit(solution)/shard_map/ppermute | solution.py:33
  100.2 1.7 collective-permute-start.21
  101.9 1.2 collective-permute-start.20
  103.6 2.3 %collective-permute-done.19 = bf16[4,32,128]{2,1,0:T(8,128)(2,1)S(1)} collective-permute-done((bf16[4,32,128]{2,1,0:T(8,128)(2,1)S(1)}, bf16[4,32,128]{2,1,0:T(8,128)(2,1)S(1)}, u32[]{:S(2)}, u32[]{:S(2)}) %collective-permute-start.19) | collective-permute-done | bytes 32800 | tf_op jit(solution)/shard_map/ppermute | solution.py:33
  106.2 4.5 %collective-permute-start.22 = (bf16[16,32,128]{2,1,0:T(8,128)(2,1)S(1)}, bf16[16,32,128]{2,1,0:T(8,128)(2,1)S(1)}, u32[]{:S(2)}, u32[]{:S(2)}) collective-permute-start(bf16[16,32,128]{2,1,0:T(8,128)(2,1)S(1)} %constant_dynamic-update-slice_fusion.rest_0_), channel_id=1, source_target_pairs={{0,16},{16,0},{32,48},{48,32},{64,80},{80,64},{96,112},{112,96},{1... | collective-permute-start | bytes 393224 | tf_op jit(solution)/shard_map/ppermute | solution.py:33
  110.7 1.0 collective-permute-done.22.rest_1_
  111.7 7.0 %shard_map.71 = (f32[16,32,128]{2,1,0:T(8,128)S(1)}, f32[16,32,128]{2,1,0:T(8,128)S(1)}, f32[16,32,128]{2,1,0:T(8,128)S(1)}, f32[16,32,128]{2,1,0:T(8,128)S(1)}) custom-call(s32[352]{0:T(512)S(1)} %get-tuple-element.57.dst_ref.src_ref, s32[352]{0:T(512)S(1)} %get-tuple-element.52.dst_ref, bf16[352,128,128]{2,1,0:T(8,128)(2,1)S(1)} %get-tuple-element.23.held_ref.w_ref, ...), custom_call_target="tpu_custom_call" | custom-call | tf_op jit(solution)/shard_map/pallas_call | solution.py:176
  119.1 1.8 %collective-permute-start.24 = (f32[16,32,128]{2,1,0:T(8,128)S(1)}, f32[16,32,128]{2,1,0:T(8,128)S(1)}, u32[]{:S(2)}, u32[]{:S(2)}) collective-permute-start(f32[16,32,128]{2,1,0:T(8,128)S(1)} %get-tuple-element.39), channel_id=1, source_target_pairs={{0,8},{1,9},{2,10},{3,11},{4,12},{5,13},{6,14},{7,15},{8,0},{9,1},... | collective-permute-start | bytes 786440 | tf_op jit(solution)/shard_map/ppermute | solution.py:33
  121.0 1.7 collective-permute-start.25
  122.7 3.7 %collective-permute-done.23 = f32[16,32,128]{2,1,0:T(8,128)S(1)} collective-permute-done((f32[16,32,128]{2,1,0:T(8,128)S(1)}, f32[16,32,128]{2,1,0:T(8,128)S(1)}, u32[]{:S(2)}, u32[]{:S(2)}) %collective-permute-start.23) | collective-permute-done | bytes 262176 | tf_op jit(solution)/shard_map/ppermute | solution.py:33
  126.3 6.4 %collective-permute-done.24 = f32[16,32,128]{2,1,0:T(8,128)S(1)} collective-permute-done((f32[16,32,128]{2,1,0:T(8,128)S(1)}, f32[16,32,128]{2,1,0:T(8,128)S(1)}, u32[]{:S(2)}, u32[]{:S(2)}) %collective-permute-start.24) | collective-permute-done | bytes 262176 | tf_op jit(solution)/shard_map/ppermute | solution.py:33
  132.7 2.0 %collective-permute-done.25 = f32[16,32,128]{2,1,0:T(8,128)S(1)} collective-permute-done((f32[16,32,128]{2,1,0:T(8,128)S(1)}, f32[16,32,128]{2,1,0:T(8,128)S(1)}, u32[]{:S(2)}, u32[]{:S(2)}) %collective-permute-start.25) | collective-permute-done | bytes 262176 | tf_op jit(solution)/shard_map/ppermute | solution.py:33
  134.8 1.6 collective-permute-start.28
  136.5 2.0 %collective-permute-start.26 = (f32[4,32,128]{2,1,0:T(8,128)S(1)}, f32[4,32,128]{2,1,0:T(8,128)S(1)}, u32[]{:S(2)}, u32[]{:S(2)}) collective-permute-start(f32[4,32,128]{2,1,0:T(8,128)S(1)} %get-tuple-element.46), channel_id=1, source_target_pairs={{0,1},{1,0},{2,3},{3,2},{4,5},{5,4},{6,7},{7,6},{8,9},{9,8},{10,11... | collective-permute-start | bytes 196616 | tf_op jit(solution)/shard_map/ppermute | solution.py:33
  138.5 1.5 collective-permute-done.28.rest_3_
  139.9 3.7 %collective-permute-done.27.rest_2_ = f32[4,32,128]{2,1,0:T(8,128)S(1)} collective-permute-done((f32[4,32,128]{2,1,0:T(8,128)S(1)}, f32[4,32,128]{2,1,0:T(8,128)S(1)}, u32[]{:S(2)}, u32[]{:S(2)}) %collective-permute-start.27) | collective-permute-done | bytes 65568 | tf_op jit(solution)/shard_map/ppermute | solution.py:33
  144.4 10.6 %all-to-all-start = ((f32[256,1,128]{2,1,0:T(1,128)}), f32[256,1,128]{2,1,0:T(1,128)S(1)}, u32[]{:S(2)}, u32[]{:S(2)}) async-start(f32[256,1,128]{2,1,0:T(1,128)} %bitcast.5), calls=%async_computation | async-start | bytes 262144 | tf_op jit(solution)/shard_map/all_to_all | solution.py:302
  155.1 12.9 %all-to-all-done = f32[256,1,128]{2,1,0:T(1,128)S(1)} async-done(((f32[256,1,128]{2,1,0:T(1,128)}), f32[256,1,128]{2,1,0:T(1,128)S(1)}, u32[]{:S(2)}, u32[]{:S(2)}) %all-to-all-start) | async-done | bytes 131104 | tf_op jit(solution)/shard_map/all_to_all | solution.py:302
  (47 shorter events, 8.0 us)
Async XLA Ops:
  9.5 4.5 %collective-permute-start = (bf16[16,32,128]{2,1,0:T(8,128)(2,1)}, bf16[16,32,128]{2,1,0:T(8,128)(2,1)S(1)}, u32[]{:S(2)}, u32[]{:S(2)}) collective-permute-start(bf16[16,32,128]{2,1,0:T(8,128)(2,1)} %get-tuple-element.25), channel_id=1, source_target_pairs={{0,16},{16,0},{32,48},{48,32},{64,80},{80,64},{96,112},{112,96},{1... | collective-permute-start | bytes 393224 | tf_op jit(solution)/shard_map/ppermute | solution.py:33
  14.1 0.9 copy-start
  15.0 21.7 %copy-start.2 = (s32[352]{0:T(512)S(1)}, s32[352]{0:T(512)}, u32[]{:S(2)}) copy-start(s32[352]{0:T(512)} %get-tuple-element.53.src_ref.dst_ref) | copy-start | bytes 4228
  15.0 21.7 %copy-start.3 = (s32[352]{0:T(512)S(1)}, s32[352]{0:T(512)}, u32[]{:S(2)}) copy-start(s32[352]{0:T(512)} %get-tuple-element.56.dst_ref.src_ref) | copy-start | bytes 4228
  15.0 8.7 %collective-permute-start.1 = (bf16[16,32,128]{2,1,0:T(8,128)(2,1)S(1)}, bf16[16,32,128]{2,1,0:T(8,128)(2,1)S(1)}, u32[]{:S(2)}, u32[]{:S(2)}) collective-permute-start(bf16[16,32,128]{2,1,0:T(8,128)(2,1)S(1)} %shard_map.60.refs_0_), channel_id=1, source_target_pairs={{0,128},{16,144},{32,160},{48,176},{64,192},{80,208},{96,224},{112... | collective-permute-start | bytes 393224 | tf_op jit(solution)/shard_map/ppermute | solution.py:33
  23.8 8.4 %collective-permute-start.4 = (bf16[16,32,128]{2,1,0:T(8,128)(2,1)S(1)}, bf16[16,32,128]{2,1,0:T(8,128)(2,1)S(1)}, u32[]{:S(2)}, u32[]{:S(2)}) collective-permute-start(bf16[16,32,128]{2,1,0:T(8,128)(2,1)S(1)} %shard_map.61.refs_0_), channel_id=1, source_target_pairs={{0,96},{16,112},{32,64},{48,80},{64,32},{80,48},{96,0},{112,16},{1... | collective-permute-start | bytes 393224 | tf_op jit(solution)/shard_map/ppermute | solution.py:33
  26.7 5.4 %collective-permute-start.3 = (bf16[16,32,128]{2,1,0:T(8,128)(2,1)S(1)}, bf16[16,32,128]{2,1,0:T(8,128)(2,1)S(1)}, u32[]{:S(2)}, u32[]{:S(2)}) collective-permute-start(bf16[16,32,128]{2,1,0:T(8,128)(2,1)S(1)} %shard_map.61.refs_0_), channel_id=1, source_target_pairs={{0,64},{16,80},{32,96},{48,112},{64,0},{80,16},{96,32},{112,48},{1... | collective-permute-start | bytes 393224 | tf_op jit(solution)/shard_map/ppermute | solution.py:33
  27.1 5.2 %collective-permute-start.2 = (bf16[16,32,128]{2,1,0:T(8,128)(2,1)S(1)}, bf16[16,32,128]{2,1,0:T(8,128)(2,1)S(1)}, u32[]{:S(2)}, u32[]{:S(2)}) collective-permute-start(bf16[16,32,128]{2,1,0:T(8,128)(2,1)S(1)} %shard_map.61.refs_0_), channel_id=1, source_target_pairs={{0,32},{16,48},{32,0},{48,16},{64,96},{80,112},{96,64},{112,80},{1... | collective-permute-start | bytes 393224 | tf_op jit(solution)/shard_map/ppermute | solution.py:33
  32.3 4.4 %collective-permute-start.5 = (bf16[16,32,128]{2,1,0:T(8,128)(2,1)S(1)}, bf16[16,32,128]{2,1,0:T(8,128)(2,1)S(1)}, u32[]{:S(2)}, u32[]{:S(2)}) collective-permute-start(bf16[16,32,128]{2,1,0:T(8,128)(2,1)S(1)} %get-tuple-element.27.rest_0_), channel_id=1, source_target_pairs={{0,16},{16,0},{32,48},{48,32},{64,80},{80,64},{96,112},{112,96},{1... | collective-permute-start | bytes 393224 | tf_op jit(solution)/shard_map/ppermute | solution.py:33
  43.7 4.8 %collective-permute-start.6 = (bf16[16,32,128]{2,1,0:T(8,128)(2,1)S(1)}, bf16[16,32,128]{2,1,0:T(8,128)(2,1)S(1)}, u32[]{:S(2)}, u32[]{:S(2)}) collective-permute-start(bf16[16,32,128]{2,1,0:T(8,128)(2,1)S(1)} %get-tuple-element.29), channel_id=1, source_target_pairs={{0,4},{1,5},{2,6},{3,7},{4,0},{5,1},{6,2},{7,3},{8,12},{9,13},{10,... | collective-permute-start | bytes 393224 | tf_op jit(solution)/shard_map/ppermute | solution.py:33
  45.0 8.6 %collective-permute-start.7 = (bf16[16,32,128]{2,1,0:T(8,128)(2,1)S(1)}, bf16[16,32,128]{2,1,0:T(8,128)(2,1)S(1)}, u32[]{:S(2)}, u32[]{:S(2)}) collective-permute-start(bf16[16,32,128]{2,1,0:T(8,128)(2,1)S(1)} %get-tuple-element.30), channel_id=1, source_target_pairs={{0,8},{1,9},{2,10},{3,11},{4,12},{5,13},{6,14},{7,15},{8,0},{9,1},... | collective-permute-start | bytes 393224 | tf_op jit(solution)/shard_map/ppermute | solution.py:33
  47.4 8.6 %collective-permute-start.8 = (bf16[16,32,128]{2,1,0:T(8,128)(2,1)S(1)}, bf16[16,32,128]{2,1,0:T(8,128)(2,1)S(1)}, u32[]{:S(2)}, u32[]{:S(2)}) collective-permute-start(bf16[16,32,128]{2,1,0:T(8,128)(2,1)S(1)} %get-tuple-element.31), channel_id=1, source_target_pairs={{0,12},{1,13},{2,14},{3,15},{4,8},{5,9},{6,10},{7,11},{8,4},{9,5},... | collective-permute-start | bytes 393224 | tf_op jit(solution)/shard_map/ppermute | solution.py:33
  56.1 7.0 %collective-permute-start.9 = (bf16[16,32,128]{2,1,0:T(8,128)(2,1)S(1)}, bf16[16,32,128]{2,1,0:T(8,128)(2,1)S(1)}, u32[]{:S(2)}, u32[]{:S(2)}) collective-permute-start(bf16[16,32,128]{2,1,0:T(8,128)(2,1)S(1)} %shard_map.64.refs_0_), channel_id=1, source_target_pairs={{0,2},{1,3},{2,0},{3,1},{4,6},{5,7},{6,4},{7,5},{8,10},{9,11},{10,... | collective-permute-start | bytes 393224 | tf_op jit(solution)/shard_map/ppermute | solution.py:33
  63.1 5.1 %collective-permute-start.10 = (bf16[16,32,128]{2,1,0:T(8,128)(2,1)S(1)}, bf16[16,32,128]{2,1,0:T(8,128)(2,1)S(1)}, u32[]{:S(2)}, u32[]{:S(2)}) collective-permute-start(bf16[16,32,128]{2,1,0:T(8,128)(2,1)S(1)} %shard_map.65.refs_0_), channel_id=1, source_target_pairs={{0,1},{1,0},{2,3},{3,2},{4,5},{5,4},{6,7},{7,6},{8,9},{9,8},{10,11... | collective-permute-start | bytes 393224 | tf_op jit(solution)/shard_map/ppermute | solution.py:33
  68.3 5.7 %collective-permute-start.13 = (bf16[16,32,128]{2,1,0:T(8,128)(2,1)S(1)}, bf16[16,32,128]{2,1,0:T(8,128)(2,1)S(1)}, u32[]{:S(2)}, u32[]{:S(2)}) collective-permute-start(bf16[16,32,128]{2,1,0:T(8,128)(2,1)S(1)} %get-tuple-element.32.rest_0_), channel_id=1, source_target_pairs={{0,12},{1,13},{2,14},{3,15},{4,8},{5,9},{6,10},{7,11},{8,4},{9,5},... | collective-permute-start | bytes 393224 | tf_op jit(solution)/shard_map/ppermute | solution.py:33
  70.6 5.3 %collective-permute-start.12 = (bf16[16,32,128]{2,1,0:T(8,128)(2,1)S(1)}, bf16[16,32,128]{2,1,0:T(8,128)(2,1)S(1)}, u32[]{:S(2)}, u32[]{:S(2)}) collective-permute-start(bf16[16,32,128]{2,1,0:T(8,128)(2,1)S(1)} %get-tuple-element.32.rest_0_), channel_id=1, source_target_pairs={{0,8},{1,9},{2,10},{3,11},{4,12},{5,13},{6,14},{7,15},{8,0},{9,1},... | collective-permute-start | bytes 393224 | tf_op jit(solution)/shard_map/ppermute | solution.py:33
  70.6 5.3 %collective-permute-start.11 = (bf16[16,32,128]{2,1,0:T(8,128)(2,1)S(1)}, bf16[16,32,128]{2,1,0:T(8,128)(2,1)S(1)}, u32[]{:S(2)}, u32[]{:S(2)}) collective-permute-start(bf16[16,32,128]{2,1,0:T(8,128)(2,1)S(1)} %get-tuple-element.32.rest_0_), channel_id=1, source_target_pairs={{0,4},{1,5},{2,6},{3,7},{4,0},{5,1},{6,2},{7,3},{8,12},{9,13},{10,... | collective-permute-start | bytes 393224 | tf_op jit(solution)/shard_map/ppermute | solution.py:33
  79.9 6.8 %collective-permute-start.14 = (f32[16,32,128]{2,1,0:T(8,128)S(1)}, f32[16,32,128]{2,1,0:T(8,128)S(1)}, u32[]{:S(2)}, u32[]{:S(2)}) collective-permute-start(f32[16,32,128]{2,1,0:T(8,128)S(1)} %get-tuple-element.34), channel_id=1, source_target_pairs={{0,16},{16,0},{32,48},{48,32},{64,80},{80,64},{96,112},{112,96},{1... | collective-permute-start | bytes 786440 | tf_op jit(solution)/shard_map/ppermute | solution.py:33
  86.7 4.4 %collective-permute-start.17 = (f32[4,32,128]{2,1,0:T(8,128)S(1)}, f32[4,32,128]{2,1,0:T(8,128)S(1)}, u32[]{:S(2)}, u32[]{:S(2)}) collective-permute-start(f32[4,32,128]{2,1,0:T(8,128)S(1)} %get-tuple-element.48), channel_id=1, source_target_pairs={{0,96},{16,112},{32,64},{48,80},{64,32},{80,48},{96,0},{112,16},{1... | collective-permute-start | bytes 196616 | tf_op jit(solution)/shard_map/ppermute | solution.py:33
  88.5 4.6 %collective-permute-start.16 = (f32[4,32,128]{2,1,0:T(8,128)S(1)}, f32[4,32,128]{2,1,0:T(8,128)S(1)}, u32[]{:S(2)}, u32[]{:S(2)}) collective-permute-start(f32[4,32,128]{2,1,0:T(8,128)S(1)} %get-tuple-element.49), channel_id=1, source_target_pairs={{0,64},{16,80},{32,96},{48,112},{64,0},{80,16},{96,32},{112,48},{1... | collective-permute-start | bytes 196616 | tf_op jit(solution)/shard_map/ppermute | solution.py:33
  88.8 4.3 %collective-permute-start.15 = (f32[4,32,128]{2,1,0:T(8,128)S(1)}, f32[4,32,128]{2,1,0:T(8,128)S(1)}, u32[]{:S(2)}, u32[]{:S(2)}) collective-permute-start(f32[4,32,128]{2,1,0:T(8,128)S(1)} %get-tuple-element.50), channel_id=1, source_target_pairs={{0,32},{16,48},{32,0},{48,16},{64,96},{80,112},{96,64},{112,80},{1... | collective-permute-start | bytes 196616 | tf_op jit(solution)/shard_map/ppermute | solution.py:33
  93.1 74.9 %copy-start.1 = (s32[32,16]{0,1:T(8,128)S(1)}, s32[32,16]{0,1:T(8,128)}, u32[]{:S(2)}) copy-start(s32[32,16]{0,1:T(8,128)} %param.7) | copy-start | bytes 6148
  93.1 7.1 %collective-permute-start.18 = (f32[4,32,128]{2,1,0:T(8,128)S(1)}, f32[4,32,128]{2,1,0:T(8,128)S(1)}, u32[]{:S(2)}, u32[]{:S(2)}) collective-permute-start(f32[4,32,128]{2,1,0:T(8,128)S(1)} %shard_map.69.refs_0_), channel_id=1, source_target_pairs={{0,128},{16,144},{32,160},{48,176},{64,192},{80,208},{96,224},{112... | collective-permute-start | bytes 196616 | tf_op jit(solution)/shard_map/ppermute | solution.py:33
  100.2 6.0 %collective-permute-start.21 = (bf16[4,32,128]{2,1,0:T(8,128)(2,1)S(1)}, bf16[4,32,128]{2,1,0:T(8,128)(2,1)S(1)}, u32[]{:S(2)}, u32[]{:S(2)}) collective-permute-start(bf16[4,32,128]{2,1,0:T(8,128)(2,1)S(1)} %get-tuple-element.36), channel_id=1, source_target_pairs={{0,96},{16,112},{32,64},{48,80},{64,32},{80,48},{96,0},{112,16},{1... | collective-permute-start | bytes 98312 | tf_op jit(solution)/shard_map/ppermute | solution.py:33
  101.9 4.3 %collective-permute-start.20 = (bf16[4,32,128]{2,1,0:T(8,128)(2,1)S(1)}, bf16[4,32,128]{2,1,0:T(8,128)(2,1)S(1)}, u32[]{:S(2)}, u32[]{:S(2)}) collective-permute-start(bf16[4,32,128]{2,1,0:T(8,128)(2,1)S(1)} %get-tuple-element.36), channel_id=1, source_target_pairs={{0,64},{16,80},{32,96},{48,112},{64,0},{80,16},{96,32},{112,48},{1... | collective-permute-start | bytes 98312 | tf_op jit(solution)/shard_map/ppermute | solution.py:33
  103.1 2.8 %collective-permute-start.19 = (bf16[4,32,128]{2,1,0:T(8,128)(2,1)S(1)}, bf16[4,32,128]{2,1,0:T(8,128)(2,1)S(1)}, u32[]{:S(2)}, u32[]{:S(2)}) collective-permute-start(bf16[4,32,128]{2,1,0:T(8,128)(2,1)S(1)} %get-tuple-element.36), channel_id=1, source_target_pairs={{0,32},{16,48},{32,0},{48,16},{64,96},{80,112},{96,64},{112,80},{1... | collective-permute-start | bytes 98312 | tf_op jit(solution)/shard_map/ppermute | solution.py:33
  106.2 5.5 %collective-permute-start.22 = (bf16[16,32,128]{2,1,0:T(8,128)(2,1)S(1)}, bf16[16,32,128]{2,1,0:T(8,128)(2,1)S(1)}, u32[]{:S(2)}, u32[]{:S(2)}) collective-permute-start(bf16[16,32,128]{2,1,0:T(8,128)(2,1)S(1)} %constant_dynamic-update-slice_fusion.rest_0_), channel_id=1, source_target_pairs={{0,16},{16,0},{32,48},{48,32},{64,80},{80,64},{96,112},{112,96},{1... | collective-permute-start | bytes 393224 | tf_op jit(solution)/shard_map/ppermute | solution.py:33
  118.7 7.6 %collective-permute-start.23 = (f32[16,32,128]{2,1,0:T(8,128)S(1)}, f32[16,32,128]{2,1,0:T(8,128)S(1)}, u32[]{:S(2)}, u32[]{:S(2)}) collective-permute-start(f32[16,32,128]{2,1,0:T(8,128)S(1)} %get-tuple-element.38), channel_id=1, source_target_pairs={{0,4},{1,5},{2,6},{3,7},{4,0},{5,1},{6,2},{7,3},{8,12},{9,13},{10,... | collective-permute-start | bytes 786440 | tf_op jit(solution)/shard_map/ppermute | solution.py:33
  119.1 13.6 %collective-permute-start.24 = (f32[16,32,128]{2,1,0:T(8,128)S(1)}, f32[16,32,128]{2,1,0:T(8,128)S(1)}, u32[]{:S(2)}, u32[]{:S(2)}) collective-permute-start(f32[16,32,128]{2,1,0:T(8,128)S(1)} %get-tuple-element.39), channel_id=1, source_target_pairs={{0,8},{1,9},{2,10},{3,11},{4,12},{5,13},{6,14},{7,15},{8,0},{9,1},... | collective-permute-start | bytes 786440 | tf_op jit(solution)/shard_map/ppermute | solution.py:33
  121.0 13.7 %collective-permute-start.25 = (f32[16,32,128]{2,1,0:T(8,128)S(1)}, f32[16,32,128]{2,1,0:T(8,128)S(1)}, u32[]{:S(2)}, u32[]{:S(2)}) collective-permute-start(f32[16,32,128]{2,1,0:T(8,128)S(1)} %get-tuple-element.40), channel_id=1, source_target_pairs={{0,12},{1,13},{2,14},{3,15},{4,8},{5,9},{6,10},{7,11},{8,4},{9,5},... | collective-permute-start | bytes 786440 | tf_op jit(solution)/shard_map/ppermute | solution.py:33
  134.8 5.1 %collective-permute-start.28 = (f32[4,32,128]{2,1,0:T(8,128)S(1)}, f32[4,32,128]{2,1,0:T(8,128)S(1)}, u32[]{:S(2)}, u32[]{:S(2)}) collective-permute-start(f32[4,32,128]{2,1,0:T(8,128)S(1)} %get-tuple-element.44), channel_id=1, source_target_pairs={{0,3},{1,2},{2,1},{3,0},{4,7},{5,6},{6,5},{7,4},{8,11},{9,10},{10,... | collective-permute-start | bytes 196616 | tf_op jit(solution)/shard_map/ppermute | solution.py:33
  136.5 7.2 %collective-permute-start.27 = (f32[4,32,128]{2,1,0:T(8,128)S(1)}, f32[4,32,128]{2,1,0:T(8,128)S(1)}, u32[]{:S(2)}, u32[]{:S(2)}) collective-permute-start(f32[4,32,128]{2,1,0:T(8,128)S(1)} %get-tuple-element.45), channel_id=1, source_target_pairs={{0,2},{1,3},{2,0},{3,1},{4,6},{5,7},{6,4},{7,5},{8,10},{9,11},{10,... | collective-permute-start | bytes 196616 | tf_op jit(solution)/shard_map/ppermute | solution.py:33
  136.5 7.2 %collective-permute-start.26 = (f32[4,32,128]{2,1,0:T(8,128)S(1)}, f32[4,32,128]{2,1,0:T(8,128)S(1)}, u32[]{:S(2)}, u32[]{:S(2)}) collective-permute-start(f32[4,32,128]{2,1,0:T(8,128)S(1)} %get-tuple-element.46), channel_id=1, source_target_pairs={{0,1},{1,0},{2,3},{3,2},{4,5},{5,4},{6,7},{7,6},{8,9},{9,8},{10,11... | collective-permute-start | bytes 196616 | tf_op jit(solution)/shard_map/ppermute | solution.py:33
  144.4 23.5 %all-to-all-start = ((f32[256,1,128]{2,1,0:T(1,128)}), f32[256,1,128]{2,1,0:T(1,128)S(1)}, u32[]{:S(2)}, u32[]{:S(2)}) async-start(f32[256,1,128]{2,1,0:T(1,128)} %bitcast.5), calls=%async_computation | async-start | bytes 262144 | tf_op jit(solution)/shard_map/all_to_all | solution.py:302

commit v4 on v3

--- a/solution.py
+++ b/solution.py
@@ -16,13 +16,21 @@
 SHRINK = 2.0**-16
 GROW = 2.0**16
 MIB = 2**20
+LIGHT = pl.CostEstimate(flops=10**6, bytes_accessed=10**5, transcendentals=0)
 F32 = jnp.float32
 BF16 = jnp.bfloat16
+F16 = jnp.float16
+WIRE = F32
 SMEM = pl.BlockSpec(memory_space=pltpu.SMEM)
 VMEM = pl.BlockSpec(memory_space=pltpu.VMEM)
 
 CORE, Y, ZHI = (0, 1), (1, 2), (3, 1)
 ZLO, X = (0, 2), (2, 2)
+
+
+HALVES_ZY = [[z * 16 + y * 4 + h * 2 + q for z in range(2) for y in range(4) for q in range(2)] for h in range(2)]
+HALVES_YZ = [[z * 16 + y * 4 + h * 2 + q for y in range(4) for z in range(2) for q in range(2)] for h in range(2)]
+QUARTERS = [list(range(c * 16, c * 16 + 16)) for c in range(4)]
 
 
 def field(index, part):
@@ -48,9 +56,9 @@
     return total
 
 
-def add_kernel(held_ref, *refs, n_in):
-    total = added([ref[...] for ref in refs[:n_in]])
-    for out in refs[n_in:]:
+def add_kernel(*refs, n_in):
+    total = added([ref[...] for ref in refs[1 : 1 + n_in]])
+    for out in refs[1 + n_in :]:
         out[...] = total.astype(out.dtype)
 
 
@@ -61,7 +69,16 @@
         out_specs=[VMEM] * len(dtypes),
         out_shape=[jax.ShapeDtypeStruct(parts[0].shape, dtype) for dtype in dtypes],
         compiler_params=pltpu.CompilerParams(vmem_limit_bytes=8 * MIB),
+        cost_estimate=LIGHT,
     )(held, *parts)
+
+
+def add_scaled(own, others):
+    total = own
+    for other in others:
+        wide = other.astype(F32)
+        total = total + wide[:-1] * jnp.exp2(wide[-1:])
+    return total
 
 
 def seed_columns(seed_ref):
@@ -83,36 +100,38 @@
     return count * scale
 
 
-def multiply_tiles(src_ref, dst_ref, x_ref, w_ref, acc_ref, contract, first, count):
+def multiply_tiles(src_ref, dst_ref, masks, x_ref, w_ref, acc_ref, first, count, base, flip=0):
     for j in range(count):
+        tile = w_ref[base + first + j]
         prod = lax.dot_general(
             x_ref[src_ref[first + j]],
-            w_ref[first + j],
-            (((1,), (contract,)), ((), ())),
+            tile,
+            (((1,), (0,)), ((), ())),
             preferred_element_type=F32,
         )
         acc_ref[dst_ref[first + j]] += prod
-
-
-def store_chunks(acc_ref, out_refs, factor):
-    start = 0
-    for out in out_refs:
-        rows = out.shape[0]
-        out[...] = (acc_ref[start : start + rows] * factor).astype(out.dtype)
-        start += rows
-
-
-def first_kernel(src_ref, dst_ref, base_ref, seed_ref, w_ref, held_ref, *rest, scale):
+        if flip:
+            w_ref[flip + first + j] = tile.T
+
+
+def store_chunks(acc_ref, out_refs, orders, factor):
+    for out, order in zip(out_refs, orders):
+        for i, tile in enumerate(order):
+            out[i] = (acc_ref[tile] * factor).astype(out.dtype)
+
+
+def first_kernel(src_ref, dst_ref, plan_ref, seed_ref, w_ref, held_ref, *rest, orders, scale):
     *out_refs, x_ref, wide_ref, acc_ref, sem = rest
     copies = []
-    for i in range(held_ref.shape[0] // STREAM):
+    tiles = w_ref.shape[0]
+    for i in range(tiles // STREAM):
         part = pl.ds(i * STREAM, STREAM)
         copies.append(pltpu.make_async_copy(w_ref.at[part], held_ref.at[part], sem.at[i]))
         copies[-1].start()
     acc_ref[...] = jnp.zeros_like(acc_ref)
     last = x_ref.shape[0] * EDGE
     for k, column in enumerate(seed_columns(seed_ref)):
-        local = column - base_ref[0]
+        local = column - plan_ref[2]
         local = jnp.where((local >= 0) & (local < last), local, -1)
         wide_ref[k] = jnp.broadcast_to(local, wide_ref.shape[1:]).astype(wide_ref.dtype)
 
@@ -124,66 +143,91 @@
         one = jnp.ones(ids.shape, ids.dtype)
         for k in range(wide_ref.shape[0]):
             count = count + jnp.where(wide_ref[k] == ids, one, jnp.zeros_like(one))
-        x_ref[t ^ base_ref[1]] = (count.astype(F32) * scale).astype(x_ref.dtype)
+        x_ref[t ^ plan_ref[0]] = (count.astype(F32) * scale).astype(x_ref.dtype)
         return carry
 
     lax.fori_loop(0, x_ref.shape[0], body, 0, unroll=4)
     for i, copy in enumerate(copies):
         copy.wait()
-        multiply_tiles(src_ref, dst_ref, x_ref, held_ref, acc_ref, 0, i * STREAM, STREAM)
-    store_chunks(acc_ref, out_refs, 1.0)
-
-
-def first_pass(src, dst, base, seed_t, w, n_src, outs, scale):
+        multiply_tiles(
+            src_ref, dst_ref, None, x_ref, held_ref, acc_ref, i * STREAM, STREAM, 0, tiles
+        )
+    store_chunks(acc_ref, out_refs, orders, 1.0)
+
+
+def first_pass(src, dst, plan, seed_t, w, n_src, orders, scale):
     seeds = seed_t.shape[1]
-    n_dst = sum(rows for rows, _ in outs)
+    sizes = [len(order) for order in orders]
     return pl.pallas_call(
-        functools.partial(first_kernel, scale=scale),
+        functools.partial(first_kernel, orders=orders, scale=scale),
         in_specs=[SMEM] * 3 + [VMEM, pl.BlockSpec(memory_space=pltpu.HBM)],
-        out_specs=[VMEM] * (1 + len(outs)),
+        out_specs=[VMEM] * (1 + len(sizes)),
         scratch_shapes=[
             pltpu.VMEM((n_src, seeds, EDGE), BF16),
             pltpu.VMEM((seed_t.shape[0], seeds, EDGE), jnp.int16),
-            pltpu.VMEM((n_dst, seeds, EDGE), F32),
+            pltpu.VMEM((sum(sizes), seeds, EDGE), F32),
             pltpu.SemaphoreType.DMA((w.shape[0] // STREAM,)),
         ],
-        out_shape=[pltpu.VMEM(w.shape, w.dtype)]
-        + [jax.ShapeDtypeStruct((rows, seeds, EDGE), dtype) for rows, dtype in outs],
-        compiler_params=pltpu.CompilerParams(vmem_limit_bytes=49 * MIB),
-    )(src, dst, base, seed_t, w)
-
-
-def pass_kernel(src_ref, dst_ref, w_ref, *rest, contract, n_in):
+        out_shape=[pltpu.VMEM((2 * w.shape[0], EDGE, EDGE), w.dtype)]
+        + [jax.ShapeDtypeStruct((rows, seeds, EDGE), BF16) for rows in sizes],
+        compiler_params=pltpu.CompilerParams(vmem_limit_bytes=37 * MIB),
+        cost_estimate=LIGHT,
+    )(src, dst, plan, seed_t, w)
+
+
+def pass_kernel(src_ref, dst_ref, w_ref, *rest, flipped, in_orders, out_orders, wire):
+    n_in = len(in_orders)
     in_refs, (*out_refs, x_ref, acc_ref) = rest[:n_in], rest[n_in:]
     acc_ref[...] = jnp.zeros_like(acc_ref)
-    start = 0
-    for ref in in_refs:
-        x_ref[start : start + ref.shape[0]] = ref[...]
-        start += ref.shape[0]
+    for ref, order in zip(in_refs, in_orders):
+        for i, tile in enumerate(order):
+            x_ref[tile] = ref[i]
+
+    masks = None
+    tiles = w_ref.shape[0] // 2
+    base = tiles if flipped else 0
 
     def body(i, carry):
-        multiply_tiles(src_ref, dst_ref, x_ref, w_ref, acc_ref, contract, i * UNROLL, UNROLL)
+        multiply_tiles(src_ref, dst_ref, masks, x_ref, w_ref, acc_ref, i * UNROLL, UNROLL, base)
         return carry
 
-    lax.fori_loop(0, w_ref.shape[0] // UNROLL, body, 0)
-    store_chunks(acc_ref, out_refs, SHRINK)
-
-
-def tile_pass(src, dst, w, parts, contract, outs):
+    lax.fori_loop(0, tiles // UNROLL, body, 0)
+    if not wire:
+        store_chunks(acc_ref, out_refs, out_orders, SHRINK)
+        return
+    store_chunks(acc_ref, out_refs[:1], out_orders[:1], SHRINK)
+    for out, order in zip(out_refs[1:], out_orders[1:]):
+        top = acc_ref[order[0]]
+        for tile in order[1:]:
+            top = jnp.maximum(top, acc_ref[tile])
+        top = jnp.max(top, axis=1, keepdims=True) * SHRINK
+        power = jnp.ceil(jnp.log2(jnp.maximum(top, 1e-30))) - 14.0
+        factor = jnp.exp2(-power) * SHRINK
+        for i, tile in enumerate(order):
+            out[i] = (acc_ref[tile] * factor).astype(out.dtype)
+        out[len(order)] = jnp.broadcast_to(power, out.shape[1:]).astype(out.dtype)
+
+
+def tile_pass(src, dst, held, flipped, parts, in_orders, out_orders, dtype, wire=None):
     seeds = parts[0].shape[1]
-    n_src = sum(p.shape[0] for p in parts)
-    n_dst = sum(rows for rows, _ in outs)
+    sizes = [len(order) for order in out_orders]
+    out_shape = [jax.ShapeDtypeStruct((rows, seeds, EDGE), dtype) for rows in sizes]
+    if wire is not None:
+        out_shape[1:] = [jax.ShapeDtypeStruct((rows + 1, seeds, EDGE), wire) for rows in sizes[1:]]
     return pl.pallas_call(
-        functools.partial(pass_kernel, contract=contract, n_in=len(parts)),
+        functools.partial(
+            pass_kernel, flipped=flipped, in_orders=in_orders, out_orders=out_orders, wire=wire is not None
+        ),
         in_specs=[SMEM] * 2 + [VMEM] * (1 + len(parts)),
-        out_specs=[VMEM] * len(outs),
+        out_specs=[VMEM] * len(sizes),
         scratch_shapes=[
-            pltpu.VMEM((n_src, seeds, EDGE), BF16),
-            pltpu.VMEM((n_dst, seeds, EDGE), F32),
+            pltpu.VMEM((sum(p.shape[0] for p in parts), seeds, EDGE), BF16),
+            pltpu.VMEM((sum(sizes), seeds, EDGE), F32),
         ],
-        out_shape=[jax.ShapeDtypeStruct((rows, seeds, EDGE), dtype) for rows, dtype in outs],
-        compiler_params=pltpu.CompilerParams(vmem_limit_bytes=20 * MIB),
-    )(src, dst, w, *parts)
+        out_shape=out_shape,
+        compiler_params=pltpu.CompilerParams(vmem_limit_bytes=16 * MIB),
+        cost_estimate=LIGHT,
+    )(src, dst, held, *parts)
 
 
 def diag_mask(seeds, width, slot):
@@ -245,21 +289,17 @@
     items = I_DEV * n_rows * n_cols
     scale = float(np.float32((users / SEEDK) ** 0.5))
     seed_t = seed_users.T
-    row_base = jnp.stack([row * (U_DEV * n_cols), field(col, X) * 16])
-    own_base = ((row * n_cols + col) * U_DEV).reshape(1)
     core, y, zhi = field(row, CORE), field(row, Y), field(row, ZHI)
     zlo, x = field(col, ZLO), field(col, X)
-
-    t_half = (((tile_cols >> 1) & 1) ^ core) * 16
-    t_zhi, t_y, t_q = tile_cols >> 4, (tile_cols >> 2) & 3, tile_cols & 1
-    item_whole = t_half + t_zhi * 8 + t_y * 2 + t_q
-    item_by_y = t_half + (t_y ^ y) * 4 + t_zhi * 2 + t_q
-    t_x = (tile_rows >> 4) ^ x
-    user_whole = t_x * 16 + (tile_rows & 15)
-    user_by_z = t_x * 16 + (((tile_rows >> 2) & 3) ^ zlo) * 4 + (tile_rows & 3)
-
+    own_base = ((row * n_cols + col) * U_DEV).reshape(1)
+    zero = jnp.zeros((), jnp.int32)
+    item_core, item_core_y = core << 1, (core << 1) | (y << 2)
+    user_x, user_x_z = x << 4, (x << 4) | (zlo << 2)
+    plan = jnp.stack([user_x, zero, row * (U_DEV * n_cols)])
+    cols1, cols2 = tile_cols ^ item_core, tile_cols ^ item_core_y
+    rows1, rows2 = tile_rows ^ user_x, tile_rows ^ user_x_z
     held, keep, send = first_pass(
-        user_whole, item_whole, row_base, seed_t, tile_values, 64, [(16, BF16)] * 2, scale
+        rows1, cols1, plan, seed_t, tile_values, 64, HALVES_ZY, scale
     )
     (part,) = add_parts(held, exchanged([keep, send], "row", CORE), [BF16])
     (part,) = add_parts(held, gathered(part, "row", ZHI), [BF16])
@@ -267,7 +307,7 @@
     x1 = lax.dynamic_slice_in_dim(x1_all, (zhi * 4 + y) * 2, 2, 0)
 
     chunks = tile_pass(
-        item_whole, user_whole, held, gathered(part, "row", CORE), 1, [(16, BF16)] * 4
+        cols1, rows1, held, True, gathered(part, "row", CORE), HALVES_ZY, QUARTERS, BF16
     )
     (part,) = add_parts(held, exchanged(chunks, "col", X), [BF16])
     (part,) = add_parts(held, gathered(part, "col", (1, 1)), [BF16])
@@ -275,7 +315,7 @@
     u1 = lax.dynamic_slice_in_dim(u1_all, zlo * 4, 4, 0)
 
     chunks = tile_pass(
-        user_whole, item_by_y, held, gathered(part, "col", X), 0, [(16, F32)] * 2
+        rows1, cols2, held, False, gathered(part, "col", X), QUARTERS, HALVES_YZ, F32
     )
     (part,) = add_parts(held, exchanged(chunks, "row", CORE), [F32])
     (part,) = add_parts(held, exchanged([part[i * 4 : i * 4 + 4] for i in range(4)], "row", Y), [F32])
@@ -283,10 +323,10 @@
     y2 = lax.dynamic_slice_in_dim(y2_all, zhi * 2, 2, 0)
     half = jnp.concatenate(gathered(part, "row", Y), axis=0)
 
-    chunks = tile_pass(
-        item_by_y, user_by_z, held, gathered(half, "row", CORE), 1, [(16, F32)] * 4
-    )
-    part = added(exchanged(chunks, "col", X))
+    own, *others = tile_pass(
+        cols2, rows2, held, True, gathered(half, "row", CORE), HALVES_YZ, QUARTERS, F32, WIRE
+    )
+    part = add_scaled(own, exchanged([own] + [o.astype(F16) for o in others], "col", X)[1:])
     got = exchanged([part[i * 4 : i * 4 + 4] for i in range(4)], "col", ZLO)
     small = pltpu.CompilerParams(vmem_limit_bytes=8 * MIB)
     w2, stat = pl.pallas_call(

time: 169 us -> 156 us (0.923)
  waiting for transfers between devices: 69.5 us -> 63.5 us
  Pallas kernels: 26.9 us -> 21.2 us
    ppermute x29, waiting for transfers between devices: 56.6 us -> 50.6 us  [swapped(): return lax.ppermute(x, axis, [(i, i ^ by << part[0]) for i in range(16)])]
    pallas_call x4, Pallas kernels: 24.9 us -> 19.2 us  [the longest x3 12.1 us: tile_pass(): pl.pallas_call(functools.partial(pass_kernel, flipped=flipped, in_orders=...]
  transfers between devices with their start and end apart: 30 -> 30, of which waited for: 25 -> 24; matrix products, arithmetic and copies ran while one was open for 0% -> 0% of each run, Pallas kernels for 0% -> 0%
where the time goes in v4:
time: 156 us
  starting transfers between devices  67.6 us (43%)
  waiting for transfers between devices  63.5 us (41%)
  Pallas kernels  21.2 us (14%)
  other arithmetic  2.14 us (1%)
    ppermute x29, starting transfers between devices, swapped(): return lax.ppermute(x, axis, [(i, i ^ by << part[0]) for i in range(16)])  57.6 us
    ppermute x29, waiting for transfers between devices, swapped(): return lax.ppermute(x, axis, [(i, i ^ by << part[0]) for i in range(16)])  50.6 us
    all_to_all x1, waiting for transfers between devices, per_device(): lax.all_to_all(stat.reshape(n_rows * n_cols, 1, EDGE), ('row', 'col'), 0, 0)  12.9 us
    pallas_call x3, Pallas kernels, tile_pass(): pl.pallas_call(functools.partial(pass_kernel, flipped=flipped, in_orders=...  12.1 us
    all_to_all x1, starting transfers between devices, per_device(): lax.all_to_all(stat.reshape(n_rows * n_cols, 1, EDGE), ('row', 'col'), 0, 0)  10 us
    pallas_call x1, Pallas kernels, first_pass(): pl.pallas_call(functools.partial(first_kernel, orders=orders, scale=scale...  7.08 us
  transfers between devices with their start and end apart: 30, of which 24 were waited for; matrix products, arithmetic and copies ran while one was open for 0% of the time, Pallas kernels for 0%

profile of v4, /device:TPU:1, one launch (start us, length us, event | category | flops | bytes accessed | tf_op | source)
XLA Modules:
  0.0 156.2 jit_solution(8584328446170016105)
XLA Ops:
  1.2 1.3 broadcast_xor_fusion
  2.5 7.1 %shard_map.59 = (bf16[704,128,128]{2,1,0:T(8,128)(2,1)S(1)}, bf16[16,32,128]{2,1,0:T(8,128)(2,1)}, bf16[16,32,128]{2,1,0:T(8,128)(2,1)}) custom-call(s32[352]{0:T(512)} %get-tuple-element.53.src_ref.dst_ref, s32[352]{0:T(512)} %get-tuple-element.56.dst_ref.src_ref, s32[3]{0:T(128)} %pad_add_fusion.plan_ref, s32[16,32]{1,0:T(8,128)} %bitcast.15, ...), custom_call_target="tpu_custom_call" | custom-call | flops 1000000 | bytes 100000 | tf_op jit(solution)/shard_map/pallas_call | solution.py:161
  9.6 3.3 %collective-permute-start = (bf16[16,32,128]{2,1,0:T(8,128)(2,1)}, bf16[16,32,128]{2,1,0:T(8,128)(2,1)S(1)}, u32[]{:S(2)}, u32[]{:S(2)}) collective-permute-start(bf16[16,32,128]{2,1,0:T(8,128)(2,1)} %get-tuple-element.25), channel_id=1, source_target_pairs={{0,16},{16,0},{32,48},{48,32},{64,80},{80,64},{96,112},{112,96},{1... | collective-permute-start | bytes 393224 | tf_op jit(solution)/shard_map/ppermute | solution.py:41
  12.9 1.2 collective-permute-done.refs_2_
  15.1 5.3 %collective-permute-start.1 = (bf16[16,32,128]{2,1,0:T(8,128)(2,1)S(1)}, bf16[16,32,128]{2,1,0:T(8,128)(2,1)S(1)}, u32[]{:S(2)}, u32[]{:S(2)}) collective-permute-start(bf16[16,32,128]{2,1,0:T(8,128)(2,1)S(1)} %shard_map.60.refs_1_), channel_id=1, source_target_pairs={{0,128},{16,144},{32,160},{48,176},{64,192},{80,208},{96,224},{112... | collective-permute-start | bytes 393224 | tf_op jit(solution)/shard_map/ppermute | solution.py:41
  20.3 3.5 %collective-permute-done.1.refs_2_ = bf16[16,32,128]{2,1,0:T(8,128)(2,1)S(1)} collective-permute-done((bf16[16,32,128]{2,1,0:T(8,128)(2,1)S(1)}, bf16[16,32,128]{2,1,0:T(8,128)(2,1)S(1)}, u32[]{:S(2)}, u32[]{:S(2)}) %collective-permute-start.1) | collective-permute-done | bytes 131104 | tf_op jit(solution)/shard_map/ppermute | solution.py:41
  23.8 2.9 %collective-permute-start.4 = (bf16[16,32,128]{2,1,0:T(8,128)(2,1)S(1)}, bf16[16,32,128]{2,1,0:T(8,128)(2,1)S(1)}, u32[]{:S(2)}, u32[]{:S(2)}) collective-permute-start(bf16[16,32,128]{2,1,0:T(8,128)(2,1)S(1)} %shard_map.61.refs_1_), channel_id=1, source_target_pairs={{0,96},{16,112},{32,64},{48,80},{64,32},{80,48},{96,0},{112,16},{1... | collective-permute-start | bytes 393224 | tf_op jit(solution)/shard_map/ppermute | solution.py:41
  27.5 4.8 %collective-permute-done.4.refs_4_ = bf16[16,32,128]{2,1,0:T(8,128)(2,1)S(1)} collective-permute-done((bf16[16,32,128]{2,1,0:T(8,128)(2,1)S(1)}, bf16[16,32,128]{2,1,0:T(8,128)(2,1)S(1)}, u32[]{:S(2)}, u32[]{:S(2)}) %collective-permute-start.4) | collective-permute-done | bytes 131104 | tf_op jit(solution)/shard_map/ppermute | solution.py:41
  32.4 3.4 %collective-permute-start.5 = (bf16[16,32,128]{2,1,0:T(8,128)(2,1)S(1)}, bf16[16,32,128]{2,1,0:T(8,128)(2,1)S(1)}, u32[]{:S(2)}, u32[]{:S(2)}) collective-permute-start(bf16[16,32,128]{2,1,0:T(8,128)(2,1)S(1)} %get-tuple-element.27.rest_0_), channel_id=1, source_target_pairs={{0,16},{16,0},{32,48},{48,32},{64,80},{80,64},{96,112},{112,96},{1... | collective-permute-start | bytes 393224 | tf_op jit(solution)/shard_map/ppermute | solution.py:41
  35.8 1.0 collective-permute-done.5.rest_1_
  36.8 4.0 %shard_map.63 = (bf16[16,32,128]{2,1,0:T(8,128)(2,1)S(1)}, bf16[16,32,128]{2,1,0:T(8,128)(2,1)S(1)}, bf16[16,32,128]{2,1,0:T(8,128)(2,1)S(1)}, bf16[16,32,128]{2,1,0:T(8,128)(2,1)S(1)}) custom-call(s32[352]{0:T(512)S(1)} %copy-done.3, s32[352]{0:T(512)S(1)} %copy-done.1, bf16[704,128,128]{2,1,0:T(8,128)(2,1)S(1)} %get-tuple-element.23.refs_0_.w_ref, ...), custom_call_target="tpu_custom_call" | custom-call | flops 1000000 | bytes 100000 | tf_op jit(solution)/shard_map/pallas_call | solution.py:217
  40.8 1.3 collective-permute-start.6
  42.1 2.4 %collective-permute-start.7 = (bf16[16,32,128]{2,1,0:T(8,128)(2,1)S(1)}, bf16[16,32,128]{2,1,0:T(8,128)(2,1)S(1)}, u32[]{:S(2)}, u32[]{:S(2)}) collective-permute-start(bf16[16,32,128]{2,1,0:T(8,128)(2,1)S(1)} %get-tuple-element.30), channel_id=1, source_target_pairs={{0,8},{1,9},{2,10},{3,11},{4,12},{5,13},{6,14},{7,15},{8,0},{9,1},... | collective-permute-start | bytes 393224 | tf_op jit(solution)/shard_map/ppermute | solution.py:41
  45.6 5.1 %collective-permute-done.7.refs_3_ = bf16[16,32,128]{2,1,0:T(8,128)(2,1)S(1)} collective-permute-done((bf16[16,32,128]{2,1,0:T(8,128)(2,1)S(1)}, bf16[16,32,128]{2,1,0:T(8,128)(2,1)S(1)}, u32[]{:S(2)}, u32[]{:S(2)}) %collective-permute-start.7) | collective-permute-done | bytes 131104 | tf_op jit(solution)/shard_map/ppermute | solution.py:41
  50.6 2.5 %collective-permute-done.8.refs_4_ = bf16[16,32,128]{2,1,0:T(8,128)(2,1)S(1)} collective-permute-done((bf16[16,32,128]{2,1,0:T(8,128)(2,1)S(1)}, bf16[16,32,128]{2,1,0:T(8,128)(2,1)S(1)}, u32[]{:S(2)}, u32[]{:S(2)}) %collective-permute-start.8) | collective-permute-done | bytes 131104 | tf_op jit(solution)/shard_map/ppermute | solution.py:41
  53.2 4.1 %collective-permute-start.9 = (bf16[16,32,128]{2,1,0:T(8,128)(2,1)S(1)}, bf16[16,32,128]{2,1,0:T(8,128)(2,1)S(1)}, u32[]{:S(2)}, u32[]{:S(2)}) collective-permute-start(bf16[16,32,128]{2,1,0:T(8,128)(2,1)S(1)} %shard_map.64.refs_1_), channel_id=1, source_target_pairs={{0,2},{1,3},{2,0},{3,1},{4,6},{5,7},{6,4},{7,5},{8,10},{9,11},{10,... | collective-permute-start | bytes 393224 | tf_op jit(solution)/shard_map/ppermute | solution.py:41
  57.3 2.8 %collective-permute-done.9.refs_2_ = bf16[16,32,128]{2,1,0:T(8,128)(2,1)S(1)} collective-permute-done((bf16[16,32,128]{2,1,0:T(8,128)(2,1)S(1)}, bf16[16,32,128]{2,1,0:T(8,128)(2,1)S(1)}, u32[]{:S(2)}, u32[]{:S(2)}) %collective-permute-start.9) | collective-permute-done | bytes 131104 | tf_op jit(solution)/shard_map/ppermute | solution.py:41
  60.2 1.8 %collective-permute-start.10 = (bf16[16,32,128]{2,1,0:T(8,128)(2,1)S(1)}, bf16[16,32,128]{2,1,0:T(8,128)(2,1)S(1)}, u32[]{:S(2)}, u32[]{:S(2)}) collective-permute-start(bf16[16,32,128]{2,1,0:T(8,128)(2,1)S(1)} %shard_map.65.refs_1_), channel_id=1, source_target_pairs={{0,1},{1,0},{2,3},{3,2},{4,5},{5,4},{6,7},{7,6},{8,9},{9,8},{10,11... | collective-permute-start | bytes 393224 | tf_op jit(solution)/shard_map/ppermute | solution.py:41
  62.0 3.3 %collective-permute-done.10.refs_2_ = bf16[16,32,128]{2,1,0:T(8,128)(2,1)S(1)} collective-permute-done((bf16[16,32,128]{2,1,0:T(8,128)(2,1)S(1)}, bf16[16,32,128]{2,1,0:T(8,128)(2,1)S(1)}, u32[]{:S(2)}, u32[]{:S(2)}) %collective-permute-start.10) | collective-permute-done | bytes 131104 | tf_op jit(solution)/shard_map/ppermute | solution.py:41
  65.3 2.4 %collective-permute-start.13 = (bf16[16,32,128]{2,1,0:T(8,128)(2,1)S(1)}, bf16[16,32,128]{2,1,0:T(8,128)(2,1)S(1)}, u32[]{:S(2)}, u32[]{:S(2)}) collective-permute-start(bf16[16,32,128]{2,1,0:T(8,128)(2,1)S(1)} %get-tuple-element.32.rest_0_), channel_id=1, source_target_pairs={{0,12},{1,13},{2,14},{3,15},{4,8},{5,9},{6,10},{7,11},{8,4},{9,5},... | collective-permute-start | bytes 393224 | tf_op jit(solution)/shard_map/ppermute | solution.py:41
  67.7 0.9 collective-permute-start.11
  68.7 2.4 %collective-permute-done.13.rest_3_ = bf16[16,32,128]{2,1,0:T(8,128)(2,1)S(1)} collective-permute-done((bf16[16,32,128]{2,1,0:T(8,128)(2,1)S(1)}, bf16[16,32,128]{2,1,0:T(8,128)(2,1)S(1)}, u32[]{:S(2)}, u32[]{:S(2)}) %collective-permute-start.13) | collective-permute-done | bytes 131104 | tf_op jit(solution)/shard_map/ppermute | solution.py:41
  71.1 2.0 %collective-permute-done.12.rest_2_ = bf16[16,32,128]{2,1,0:T(8,128)(2,1)S(1)} collective-permute-done((bf16[16,32,128]{2,1,0:T(8,128)(2,1)S(1)}, bf16[16,32,128]{2,1,0:T(8,128)(2,1)S(1)}, u32[]{:S(2)}, u32[]{:S(2)}) %collective-permute-start.12) | collective-permute-done | bytes 131104 | tf_op jit(solution)/shard_map/ppermute | solution.py:41
  73.1 4.0 %shard_map.67 = (f32[16,32,128]{2,1,0:T(8,128)S(1)}, f32[16,32,128]{2,1,0:T(8,128)S(1)}) custom-call(s32[352]{0:T(512)S(1)} %copy-done.1, s32[352]{0:T(512)S(1)} %get-tuple-element.57.dst_ref.src_ref, bf16[704,128,128]{2,1,0:T(8,128)(2,1)S(1)} %get-tuple-element.23.refs_0_.w_ref, bf16[16,32,128]{2,1,0:T(8,128)(2,1)S(1)} %get-tuple-element.32.rest_0_, ...), custom_call_target="tpu_custom_call" | custom-call | flops 1000000 | bytes 100000 | tf_op jit(solution)/shard_map/pallas_call | solution.py:217
  77.1 5.5 %collective-permute-start.14 = (f32[16,32,128]{2,1,0:T(8,128)S(1)}, f32[16,32,128]{2,1,0:T(8,128)S(1)}, u32[]{:S(2)}, u32[]{:S(2)}) collective-permute-start(f32[16,32,128]{2,1,0:T(8,128)S(1)} %get-tuple-element.34), channel_id=1, source_target_pairs={{0,16},{16,0},{32,48},{48,32},{64,80},{80,64},{96,112},{112,96},{1... | collective-permute-start | bytes 786440 | tf_op jit(solution)/shard_map/ppermute | solution.py:41
  82.6 1.2 collective-permute-done.14.refs_2_
  83.8 1.8 %collective-permute-start.17 = (f32[4,32,128]{2,1,0:T(8,128)S(1)}, f32[4,32,128]{2,1,0:T(8,128)S(1)}, u32[]{:S(2)}, u32[]{:S(2)}) collective-permute-start(f32[4,32,128]{2,1,0:T(8,128)S(1)} %get-tuple-element.48), channel_id=1, source_target_pairs={{0,96},{16,112},{32,64},{48,80},{64,32},{80,48},{96,0},{112,16},{1... | collective-permute-start | bytes 196616 | tf_op jit(solution)/shard_map/ppermute | solution.py:41
  85.9 1.2 collective-permute-start.15
  87.1 1.1 collective-permute-done.17.refs_4_
  88.2 2.0 %collective-permute-done.16.refs_3_ = f32[4,32,128]{2,1,0:T(8,128)S(1)} collective-permute-done((f32[4,32,128]{2,1,0:T(8,128)S(1)}, f32[4,32,128]{2,1,0:T(8,128)S(1)}, u32[]{:S(2)}, u32[]{:S(2)}) %collective-permute-start.16) | collective-permute-done | bytes 65568 | tf_op jit(solution)/shard_map/ppermute | solution.py:41
  90.2 5.0 %collective-permute-start.18 = (f32[4,32,128]{2,1,0:T(8,128)S(1)}, f32[4,32,128]{2,1,0:T(8,128)S(1)}, u32[]{:S(2)}, u32[]{:S(2)}) collective-permute-start(f32[4,32,128]{2,1,0:T(8,128)S(1)} %shard_map.69.refs_1_), channel_id=1, source_target_pairs={{0,128},{16,144},{32,160},{48,176},{64,192},{80,208},{96,224},{112... | collective-permute-start | bytes 196616 | tf_op jit(solution)/shard_map/ppermute | solution.py:41
  95.2 2.1 %collective-permute-done.18.refs_2_ = f32[4,32,128]{2,1,0:T(8,128)S(1)} collective-permute-done((f32[4,32,128]{2,1,0:T(8,128)S(1)}, f32[4,32,128]{2,1,0:T(8,128)S(1)}, u32[]{:S(2)}, u32[]{:S(2)}) %collective-permute-start.18) | collective-permute-done | bytes 65568 | tf_op jit(solution)/shard_map/ppermute | solution.py:41
  97.4 1.7 %collective-permute-start.21 = (bf16[4,32,128]{2,1,0:T(8,128)(2,1)S(1)}, bf16[4,32,128]{2,1,0:T(8,128)(2,1)S(1)}, u32[]{:S(2)}, u32[]{:S(2)}) collective-permute-start(bf16[4,32,128]{2,1,0:T(8,128)(2,1)S(1)} %get-tuple-element.36), channel_id=1, source_target_pairs={{0,96},{16,112},{32,64},{48,80},{64,32},{80,48},{96,0},{112,16},{1... | collective-permute-start | bytes 98312 | tf_op jit(solution)/shard_map/ppermute | solution.py:41
  99.0 1.2 collective-permute-start.20
  100.7 2.3 %collective-permute-done.19 = bf16[4,32,128]{2,1,0:T(8,128)(2,1)S(1)} collective-permute-done((bf16[4,32,128]{2,1,0:T(8,128)(2,1)S(1)}, bf16[4,32,128]{2,1,0:T(8,128)(2,1)S(1)}, u32[]{:S(2)}, u32[]{:S(2)}) %collective-permute-start.19) | collective-permute-done | bytes 32800 | tf_op jit(solution)/shard_map/ppermute | solution.py:41
  103.3 4.5 %collective-permute-start.22 = (bf16[16,32,128]{2,1,0:T(8,128)(2,1)S(1)}, bf16[16,32,128]{2,1,0:T(8,128)(2,1)S(1)}, u32[]{:S(2)}, u32[]{:S(2)}) collective-permute-start(bf16[16,32,128]{2,1,0:T(8,128)(2,1)S(1)} %constant_dynamic-update-slice_fusion.rest_0_), channel_id=1, source_target_pairs={{0,16},{16,0},{32,48},{48,32},{64,80},{80,64},{96,112},{112,96},{1... | collective-permute-start | bytes 393224 | tf_op jit(solution)/shard_map/ppermute | solution.py:41
  107.9 1.0 collective-permute-done.22.rest_1_
  108.9 4.1 %shard_map.71 = (f32[16,32,128]{2,1,0:T(8,128)S(1)}, f32[17,32,128]{2,1,0:T(8,128)S(1)}, f32[17,32,128]{2,1,0:T(8,128)S(1)}, f32[17,32,128]{2,1,0:T(8,128)S(1)}) custom-call(s32[352]{0:T(512)S(1)} %get-tuple-element.57.dst_ref.src_ref, s32[352]{0:T(512)S(1)} %get-tuple-element.52.dst_ref, bf16[704,128,128]{2,1,0:T(8,128)(2,1)S(1)} %get-tuple-element.23.refs_0_.w_ref, ...), custom_call_target="tpu_custom_call" | custom-call | flops 1000000 | bytes 100000 | tf_op jit(solution)/shard_map/pallas_call | solution.py:217
  113.0 1.1 collective-permute-start.25
  114.2 1.2 collective-permute-start.24
  115.4 1.1 collective-permute-start.23
  116.5 5.3 %collective-permute-done.25 = f16[17,32,128]{2,1,0:T(8,128)(2,1)S(1)} collective-permute-done((f16[17,32,128]{2,1,0:T(8,128)(2,1)S(1)}, f16[17,32,128]{2,1,0:T(8,128)(2,1)S(1)}, u32[]{:S(2)}, u32[]{:S(2)}) %collective-permute-start.25) | collective-permute-done | bytes 139296 | tf_op jit(solution)/shard_map/ppermute | solution.py:41
  122.9 1.7 %collective-permute-start.28 = (f32[4,32,128]{2,1,0:T(8,128)S(1)}, f32[4,32,128]{2,1,0:T(8,128)S(1)}, u32[]{:S(2)}, u32[]{:S(2)}) collective-permute-start(f32[4,32,128]{2,1,0:T(8,128)S(1)} %get-tuple-element.44), channel_id=1, source_target_pairs={{0,3},{1,2},{2,1},{3,0},{4,7},{5,6},{6,5},{7,4},{8,11},{9,10},{10,... | collective-permute-start | bytes 196616 | tf_op jit(solution)/shard_map/ppermute | solution.py:41
  124.5 2.0 %collective-permute-start.26 = (f32[4,32,128]{2,1,0:T(8,128)S(1)}, f32[4,32,128]{2,1,0:T(8,128)S(1)}, u32[]{:S(2)}, u32[]{:S(2)}) collective-permute-start(f32[4,32,128]{2,1,0:T(8,128)S(1)} %get-tuple-element.46), channel_id=1, source_target_pairs={{0,1},{1,0},{2,3},{3,2},{4,5},{5,4},{6,7},{7,6},{8,9},{9,8},{10,11... | collective-permute-start | bytes 196616 | tf_op jit(solution)/shard_map/ppermute | solution.py:41
  126.5 1.5 collective-permute-done.28.rest_3_
  128.0 3.6 %collective-permute-done.27.rest_2_ = f32[4,32,128]{2,1,0:T(8,128)S(1)} collective-permute-done((f32[4,32,128]{2,1,0:T(8,128)S(1)}, f32[4,32,128]{2,1,0:T(8,128)S(1)}, u32[]{:S(2)}, u32[]{:S(2)}) %collective-permute-start.27) | collective-permute-done | bytes 65568 | tf_op jit(solution)/shard_map/ppermute | solution.py:41
  132.4 10.0 %all-to-all-start = ((f32[256,1,128]{2,1,0:T(1,128)}), f32[256,1,128]{2,1,0:T(1,128)S(1)}, u32[]{:S(2)}, u32[]{:S(2)}) async-start(f32[256,1,128]{2,1,0:T(1,128)} %bitcast.8), calls=%async_computation | async-start | bytes 262144 | tf_op jit(solution)/shard_map/all_to_all | solution.py:342
  142.5 12.9 %all-to-all-done = f32[256,1,128]{2,1,0:T(1,128)S(1)} async-done(((f32[256,1,128]{2,1,0:T(1,128)}), f32[256,1,128]{2,1,0:T(1,128)S(1)}, u32[]{:S(2)}, u32[]{:S(2)}) %all-to-all-start) | async-done | bytes 131104 | tf_op jit(solution)/shard_map/all_to_all | solution.py:342
  (56 shorter events, 7.5 us)
Async XLA Ops:
  9.6 4.5 %collective-permute-start = (bf16[16,32,128]{2,1,0:T(8,128)(2,1)}, bf16[16,32,128]{2,1,0:T(8,128)(2,1)S(1)}, u32[]{:S(2)}, u32[]{:S(2)}) collective-permute-start(bf16[16,32,128]{2,1,0:T(8,128)(2,1)} %get-tuple-element.25), channel_id=1, source_target_pairs={{0,16},{16,0},{32,48},{48,32},{64,80},{80,64},{96,112},{112,96},{1... | collective-permute-start | bytes 393224 | tf_op jit(solution)/shard_map/ppermute | solution.py:41
  14.1 0.9 copy-start
  15.1 21.7 %copy-start.1 = (s32[352]{0:T(512)S(1)}, s32[352]{0:T(512)}, u32[]{:S(2)}) copy-start(s32[352]{0:T(512)} %get-tuple-element.53.src_ref.dst_ref) | copy-start | bytes 4228
  15.1 21.7 %copy-start.3 = (s32[352]{0:T(512)S(1)}, s32[352]{0:T(512)}, u32[]{:S(2)}) copy-start(s32[352]{0:T(512)} %get-tuple-element.56.dst_ref.src_ref) | copy-start | bytes 4228
  15.1 8.7 %collective-permute-start.1 = (bf16[16,32,128]{2,1,0:T(8,128)(2,1)S(1)}, bf16[16,32,128]{2,1,0:T(8,128)(2,1)S(1)}, u32[]{:S(2)}, u32[]{:S(2)}) collective-permute-start(bf16[16,32,128]{2,1,0:T(8,128)(2,1)S(1)} %shard_map.60.refs_1_), channel_id=1, source_target_pairs={{0,128},{16,144},{32,160},{48,176},{64,192},{80,208},{96,224},{112... | collective-permute-start | bytes 393224 | tf_op jit(solution)/shard_map/ppermute | solution.py:41
  23.8 8.4 %collective-permute-start.4 = (bf16[16,32,128]{2,1,0:T(8,128)(2,1)S(1)}, bf16[16,32,128]{2,1,0:T(8,128)(2,1)S(1)}, u32[]{:S(2)}, u32[]{:S(2)}) collective-permute-start(bf16[16,32,128]{2,1,0:T(8,128)(2,1)S(1)} %shard_map.61.refs_1_), channel_id=1, source_target_pairs={{0,96},{16,112},{32,64},{48,80},{64,32},{80,48},{96,0},{112,16},{1... | collective-permute-start | bytes 393224 | tf_op jit(solution)/shard_map/ppermute | solution.py:41
  26.8 5.4 %collective-permute-start.3 = (bf16[16,32,128]{2,1,0:T(8,128)(2,1)S(1)}, bf16[16,32,128]{2,1,0:T(8,128)(2,1)S(1)}, u32[]{:S(2)}, u32[]{:S(2)}) collective-permute-start(bf16[16,32,128]{2,1,0:T(8,128)(2,1)S(1)} %shard_map.61.refs_1_), channel_id=1, source_target_pairs={{0,64},{16,80},{32,96},{48,112},{64,0},{80,16},{96,32},{112,48},{1... | collective-permute-start | bytes 393224 | tf_op jit(solution)/shard_map/ppermute | solution.py:41
  27.1 5.2 %collective-permute-start.2 = (bf16[16,32,128]{2,1,0:T(8,128)(2,1)S(1)}, bf16[16,32,128]{2,1,0:T(8,128)(2,1)S(1)}, u32[]{:S(2)}, u32[]{:S(2)}) collective-permute-start(bf16[16,32,128]{2,1,0:T(8,128)(2,1)S(1)} %shard_map.61.refs_1_), channel_id=1, source_target_pairs={{0,32},{16,48},{32,0},{48,16},{64,96},{80,112},{96,64},{112,80},{1... | collective-permute-start | bytes 393224 | tf_op jit(solution)/shard_map/ppermute | solution.py:41
  32.4 4.4 %collective-permute-start.5 = (bf16[16,32,128]{2,1,0:T(8,128)(2,1)S(1)}, bf16[16,32,128]{2,1,0:T(8,128)(2,1)S(1)}, u32[]{:S(2)}, u32[]{:S(2)}) collective-permute-start(bf16[16,32,128]{2,1,0:T(8,128)(2,1)S(1)} %get-tuple-element.27.rest_0_), channel_id=1, source_target_pairs={{0,16},{16,0},{32,48},{48,32},{64,80},{80,64},{96,112},{112,96},{1... | collective-permute-start | bytes 393224 | tf_op jit(solution)/shard_map/ppermute | solution.py:41
  40.8 4.8 %collective-permute-start.6 = (bf16[16,32,128]{2,1,0:T(8,128)(2,1)S(1)}, bf16[16,32,128]{2,1,0:T(8,128)(2,1)S(1)}, u32[]{:S(2)}, u32[]{:S(2)}) collective-permute-start(bf16[16,32,128]{2,1,0:T(8,128)(2,1)S(1)} %get-tuple-element.29), channel_id=1, source_target_pairs={{0,4},{1,5},{2,6},{3,7},{4,0},{5,1},{6,2},{7,3},{8,12},{9,13},{10,... | collective-permute-start | bytes 393224 | tf_op jit(solution)/shard_map/ppermute | solution.py:41
  42.1 8.5 %collective-permute-start.7 = (bf16[16,32,128]{2,1,0:T(8,128)(2,1)S(1)}, bf16[16,32,128]{2,1,0:T(8,128)(2,1)S(1)}, u32[]{:S(2)}, u32[]{:S(2)}) collective-permute-start(bf16[16,32,128]{2,1,0:T(8,128)(2,1)S(1)} %get-tuple-element.30), channel_id=1, source_target_pairs={{0,8},{1,9},{2,10},{3,11},{4,12},{5,13},{6,14},{7,15},{8,0},{9,1},... | collective-permute-start | bytes 393224 | tf_op jit(solution)/shard_map/ppermute | solution.py:41
  44.5 8.6 %collective-permute-start.8 = (bf16[16,32,128]{2,1,0:T(8,128)(2,1)S(1)}, bf16[16,32,128]{2,1,0:T(8,128)(2,1)S(1)}, u32[]{:S(2)}, u32[]{:S(2)}) collective-permute-start(bf16[16,32,128]{2,1,0:T(8,128)(2,1)S(1)} %get-tuple-element.31), channel_id=1, source_target_pairs={{0,12},{1,13},{2,14},{3,15},{4,8},{5,9},{6,10},{7,11},{8,4},{9,5},... | collective-permute-start | bytes 393224 | tf_op jit(solution)/shard_map/ppermute | solution.py:41
  53.2 7.0 %collective-permute-start.9 = (bf16[16,32,128]{2,1,0:T(8,128)(2,1)S(1)}, bf16[16,32,128]{2,1,0:T(8,128)(2,1)S(1)}, u32[]{:S(2)}, u32[]{:S(2)}) collective-permute-start(bf16[16,32,128]{2,1,0:T(8,128)(2,1)S(1)} %shard_map.64.refs_1_), channel_id=1, source_target_pairs={{0,2},{1,3},{2,0},{3,1},{4,6},{5,7},{6,4},{7,5},{8,10},{9,11},{10,... | collective-permute-start | bytes 393224 | tf_op jit(solution)/shard_map/ppermute | solution.py:41
  60.2 5.1 %collective-permute-start.10 = (bf16[16,32,128]{2,1,0:T(8,128)(2,1)S(1)}, bf16[16,32,128]{2,1,0:T(8,128)(2,1)S(1)}, u32[]{:S(2)}, u32[]{:S(2)}) collective-permute-start(bf16[16,32,128]{2,1,0:T(8,128)(2,1)S(1)} %shard_map.65.refs_1_), channel_id=1, source_target_pairs={{0,1},{1,0},{2,3},{3,2},{4,5},{5,4},{6,7},{7,6},{8,9},{9,8},{10,11... | collective-permute-start | bytes 393224 | tf_op jit(solution)/shard_map/ppermute | solution.py:41
  65.3 5.7 %collective-permute-start.13 = (bf16[16,32,128]{2,1,0:T(8,128)(2,1)S(1)}, bf16[16,32,128]{2,1,0:T(8,128)(2,1)S(1)}, u32[]{:S(2)}, u32[]{:S(2)}) collective-permute-start(bf16[16,32,128]{2,1,0:T(8,128)(2,1)S(1)} %get-tuple-element.32.rest_0_), channel_id=1, source_target_pairs={{0,12},{1,13},{2,14},{3,15},{4,8},{5,9},{6,10},{7,11},{8,4},{9,5},... | collective-permute-start | bytes 393224 | tf_op jit(solution)/shard_map/ppermute | solution.py:41
  67.7 5.3 %collective-permute-start.12 = (bf16[16,32,128]{2,1,0:T(8,128)(2,1)S(1)}, bf16[16,32,128]{2,1,0:T(8,128)(2,1)S(1)}, u32[]{:S(2)}, u32[]{:S(2)}) collective-permute-start(bf16[16,32,128]{2,1,0:T(8,128)(2,1)S(1)} %get-tuple-element.32.rest_0_), channel_id=1, source_target_pairs={{0,8},{1,9},{2,10},{3,11},{4,12},{5,13},{6,14},{7,15},{8,0},{9,1},... | collective-permute-start | bytes 393224 | tf_op jit(solution)/shard_map/ppermute | solution.py:41
  67.7 5.3 %collective-permute-start.11 = (bf16[16,32,128]{2,1,0:T(8,128)(2,1)S(1)}, bf16[16,32,128]{2,1,0:T(8,128)(2,1)S(1)}, u32[]{:S(2)}, u32[]{:S(2)}) collective-permute-start(bf16[16,32,128]{2,1,0:T(8,128)(2,1)S(1)} %get-tuple-element.32.rest_0_), channel_id=1, source_target_pairs={{0,4},{1,5},{2,6},{3,7},{4,0},{5,1},{6,2},{7,3},{8,12},{9,13},{10,... | collective-permute-start | bytes 393224 | tf_op jit(solution)/shard_map/ppermute | solution.py:41
  77.1 6.7 %collective-permute-start.14 = (f32[16,32,128]{2,1,0:T(8,128)S(1)}, f32[16,32,128]{2,1,0:T(8,128)S(1)}, u32[]{:S(2)}, u32[]{:S(2)}) collective-permute-start(f32[16,32,128]{2,1,0:T(8,128)S(1)} %get-tuple-element.34), channel_id=1, source_target_pairs={{0,16},{16,0},{32,48},{48,32},{64,80},{80,64},{96,112},{112,96},{1... | collective-permute-start | bytes 786440 | tf_op jit(solution)/shard_map/ppermute | solution.py:41
  83.8 4.4 %collective-permute-start.17 = (f32[4,32,128]{2,1,0:T(8,128)S(1)}, f32[4,32,128]{2,1,0:T(8,128)S(1)}, u32[]{:S(2)}, u32[]{:S(2)}) collective-permute-start(f32[4,32,128]{2,1,0:T(8,128)S(1)} %get-tuple-element.48), channel_id=1, source_target_pairs={{0,96},{16,112},{32,64},{48,80},{64,32},{80,48},{96,0},{112,16},{1... | collective-permute-start | bytes 196616 | tf_op jit(solution)/shard_map/ppermute | solution.py:41
  85.6 4.6 %collective-permute-start.16 = (f32[4,32,128]{2,1,0:T(8,128)S(1)}, f32[4,32,128]{2,1,0:T(8,128)S(1)}, u32[]{:S(2)}, u32[]{:S(2)}) collective-permute-start(f32[4,32,128]{2,1,0:T(8,128)S(1)} %get-tuple-element.49), channel_id=1, source_target_pairs={{0,64},{16,80},{32,96},{48,112},{64,0},{80,16},{96,32},{112,48},{1... | collective-permute-start | bytes 196616 | tf_op jit(solution)/shard_map/ppermute | solution.py:41
  85.9 4.3 %collective-permute-start.15 = (f32[4,32,128]{2,1,0:T(8,128)S(1)}, f32[4,32,128]{2,1,0:T(8,128)S(1)}, u32[]{:S(2)}, u32[]{:S(2)}) collective-permute-start(f32[4,32,128]{2,1,0:T(8,128)S(1)} %get-tuple-element.50), channel_id=1, source_target_pairs={{0,32},{16,48},{32,0},{48,16},{64,96},{80,112},{96,64},{112,80},{1... | collective-permute-start | bytes 196616 | tf_op jit(solution)/shard_map/ppermute | solution.py:41
  90.2 65.1 %copy-start.2 = (s32[32,16]{0,1:T(8,128)S(1)}, s32[32,16]{0,1:T(8,128)}, u32[]{:S(2)}) copy-start(s32[32,16]{0,1:T(8,128)} %param.7) | copy-start | bytes 6148
  90.2 7.1 %collective-permute-start.18 = (f32[4,32,128]{2,1,0:T(8,128)S(1)}, f32[4,32,128]{2,1,0:T(8,128)S(1)}, u32[]{:S(2)}, u32[]{:S(2)}) collective-permute-start(f32[4,32,128]{2,1,0:T(8,128)S(1)} %shard_map.69.refs_1_), channel_id=1, source_target_pairs={{0,128},{16,144},{32,160},{48,176},{64,192},{80,208},{96,224},{112... | collective-permute-start | bytes 196616 | tf_op jit(solution)/shard_map/ppermute | solution.py:41
  97.4 6.0 %collective-permute-start.21 = (bf16[4,32,128]{2,1,0:T(8,128)(2,1)S(1)}, bf16[4,32,128]{2,1,0:T(8,128)(2,1)S(1)}, u32[]{:S(2)}, u32[]{:S(2)}) collective-permute-start(bf16[4,32,128]{2,1,0:T(8,128)(2,1)S(1)} %get-tuple-element.36), channel_id=1, source_target_pairs={{0,96},{16,112},{32,64},{48,80},{64,32},{80,48},{96,0},{112,16},{1... | collective-permute-start | bytes 98312 | tf_op jit(solution)/shard_map/ppermute | solution.py:41
  99.0 4.3 %collective-permute-start.20 = (bf16[4,32,128]{2,1,0:T(8,128)(2,1)S(1)}, bf16[4,32,128]{2,1,0:T(8,128)(2,1)S(1)}, u32[]{:S(2)}, u32[]{:S(2)}) collective-permute-start(bf16[4,32,128]{2,1,0:T(8,128)(2,1)S(1)} %get-tuple-element.36), channel_id=1, source_target_pairs={{0,64},{16,80},{32,96},{48,112},{64,0},{80,16},{96,32},{112,48},{1... | collective-permute-start | bytes 98312 | tf_op jit(solution)/shard_map/ppermute | solution.py:41
  100.2 2.8 %collective-permute-start.19 = (bf16[4,32,128]{2,1,0:T(8,128)(2,1)S(1)}, bf16[4,32,128]{2,1,0:T(8,128)(2,1)S(1)}, u32[]{:S(2)}, u32[]{:S(2)}) collective-permute-start(bf16[4,32,128]{2,1,0:T(8,128)(2,1)S(1)} %get-tuple-element.36), channel_id=1, source_target_pairs={{0,32},{16,48},{32,0},{48,16},{64,96},{80,112},{96,64},{112,80},{1... | collective-permute-start | bytes 98312 | tf_op jit(solution)/shard_map/ppermute | solution.py:41
  103.3 5.5 %collective-permute-start.22 = (bf16[16,32,128]{2,1,0:T(8,128)(2,1)S(1)}, bf16[16,32,128]{2,1,0:T(8,128)(2,1)S(1)}, u32[]{:S(2)}, u32[]{:S(2)}) collective-permute-start(bf16[16,32,128]{2,1,0:T(8,128)(2,1)S(1)} %constant_dynamic-update-slice_fusion.rest_0_), channel_id=1, source_target_pairs={{0,16},{16,0},{32,48},{48,32},{64,80},{80,64},{96,112},{112,96},{1... | collective-permute-start | bytes 393224 | tf_op jit(solution)/shard_map/ppermute | solution.py:41
  113.0 8.8 %collective-permute-start.25 = (f16[17,32,128]{2,1,0:T(8,128)(2,1)S(1)}, f16[17,32,128]{2,1,0:T(8,128)(2,1)S(1)}, u32[]{:S(2)}, u32[]{:S(2)}) collective-permute-start(f16[17,32,128]{2,1,0:T(8,128)(2,1)S(1)} %convert_element_type.22), channel_id=1, source_target_pairs={{0,12},{1,13},{2,14},{3,15},{4,8},{5,9},{6,10},{7,11},{8,4},{9,5},... | collective-permute-start | bytes 417800 | tf_op jit(solution)/shard_map/ppermute | solution.py:41
  114.2 7.7 %collective-permute-start.24 = (f16[17,32,128]{2,1,0:T(8,128)(2,1)S(1)}, f16[17,32,128]{2,1,0:T(8,128)(2,1)S(1)}, u32[]{:S(2)}, u32[]{:S(2)}) collective-permute-start(f16[17,32,128]{2,1,0:T(8,128)(2,1)S(1)} %convert_element_type.20), channel_id=1, source_target_pairs={{0,8},{1,9},{2,10},{3,11},{4,12},{5,13},{6,14},{7,15},{8,0},{9,1},... | collective-permute-start | bytes 417800 | tf_op jit(solution)/shard_map/ppermute | solution.py:41
  115.4 7.3 %collective-permute-start.23 = (f16[17,32,128]{2,1,0:T(8,128)(2,1)S(1)}, f16[17,32,128]{2,1,0:T(8,128)(2,1)S(1)}, u32[]{:S(2)}, u32[]{:S(2)}) collective-permute-start(f16[17,32,128]{2,1,0:T(8,128)(2,1)S(1)} %convert_element_type.18), channel_id=1, source_target_pairs={{0,4},{1,5},{2,6},{3,7},{4,0},{5,1},{6,2},{7,3},{8,12},{9,13},{10,... | collective-permute-start | bytes 417800 | tf_op jit(solution)/shard_map/ppermute | solution.py:41
  122.9 5.2 %collective-permute-start.28 = (f32[4,32,128]{2,1,0:T(8,128)S(1)}, f32[4,32,128]{2,1,0:T(8,128)S(1)}, u32[]{:S(2)}, u32[]{:S(2)}) collective-permute-start(f32[4,32,128]{2,1,0:T(8,128)S(1)} %get-tuple-element.44), channel_id=1, source_target_pairs={{0,3},{1,2},{2,1},{3,0},{4,7},{5,6},{6,5},{7,4},{8,11},{9,10},{10,... | collective-permute-start | bytes 196616 | tf_op jit(solution)/shard_map/ppermute | solution.py:41
  124.5 7.1 %collective-permute-start.27 = (f32[4,32,128]{2,1,0:T(8,128)S(1)}, f32[4,32,128]{2,1,0:T(8,128)S(1)}, u32[]{:S(2)}, u32[]{:S(2)}) collective-permute-start(f32[4,32,128]{2,1,0:T(8,128)S(1)} %get-tuple-element.45), channel_id=1, source_target_pairs={{0,2},{1,3},{2,0},{3,1},{4,6},{5,7},{6,4},{7,5},{8,10},{9,11},{10,... | collective-permute-start | bytes 196616 | tf_op jit(solution)/shard_map/ppermute | solution.py:41
  124.5 7.1 %collective-permute-start.26 = (f32[4,32,128]{2,1,0:T(8,128)S(1)}, f32[4,32,128]{2,1,0:T(8,128)S(1)}, u32[]{:S(2)}, u32[]{:S(2)}) collective-permute-start(f32[4,32,128]{2,1,0:T(8,128)S(1)} %get-tuple-element.46), channel_id=1, source_target_pairs={{0,1},{1,0},{2,3},{3,2},{4,5},{5,4},{6,7},{7,6},{8,9},{9,8},{10,11... | collective-permute-start | bytes 196616 | tf_op jit(solution)/shard_map/ppermute | solution.py:41
  132.4 22.9 %all-to-all-start = ((f32[256,1,128]{2,1,0:T(1,128)}), f32[256,1,128]{2,1,0:T(1,128)S(1)}, u32[]{:S(2)}, u32[]{:S(2)}) async-start(f32[256,1,128]{2,1,0:T(1,128)} %bitcast.8), calls=%async_computation | async-start | bytes 262144 | tf_op jit(solution)/shard_map/all_to_all | solution.py:342

commit v5 on v4

--- a/solution.py
+++ b/solution.py
@@ -100,7 +100,7 @@
     return count * scale
 
 
-def multiply_tiles(src_ref, dst_ref, masks, x_ref, w_ref, acc_ref, first, count, base, flip=0):
+def multiply_tiles(src_ref, dst_ref, x_ref, w_ref, acc_ref, first, count, base, mask=0, flip=0):
     for j in range(count):
         tile = w_ref[base + first + j]
         prod = lax.dot_general(
@@ -109,7 +109,7 @@
             (((1,), (0,)), ((), ())),
             preferred_element_type=F32,
         )
-        acc_ref[dst_ref[first + j]] += prod
+        acc_ref[dst_ref[first + j] ^ mask] += prod
         if flip:
             w_ref[flip + first + j] = tile.T
 
@@ -120,7 +120,7 @@
             out[i] = (acc_ref[tile] * factor).astype(out.dtype)
 
 
-def first_kernel(src_ref, dst_ref, plan_ref, seed_ref, w_ref, held_ref, *rest, orders, scale):
+def first_kernel(src_ref, dst_ref, seed_ref, w_ref, held_ref, *rest, orders, scale):
     *out_refs, x_ref, wide_ref, acc_ref, sem = rest
     copies = []
     tiles = w_ref.shape[0]
@@ -129,9 +129,11 @@
         copies.append(pltpu.make_async_copy(w_ref.at[part], held_ref.at[part], sem.at[i]))
         copies[-1].start()
     acc_ref[...] = jnp.zeros_like(acc_ref)
+    row = lax.axis_index("row")
+    mask = field(row, CORE) << 1
     last = x_ref.shape[0] * EDGE
     for k, column in enumerate(seed_columns(seed_ref)):
-        local = column - plan_ref[2]
+        local = column - row * last
         local = jnp.where((local >= 0) & (local < last), local, -1)
         wide_ref[k] = jnp.broadcast_to(local, wide_ref.shape[1:]).astype(wide_ref.dtype)
 
@@ -143,24 +145,24 @@
         one = jnp.ones(ids.shape, ids.dtype)
         for k in range(wide_ref.shape[0]):
             count = count + jnp.where(wide_ref[k] == ids, one, jnp.zeros_like(one))
-        x_ref[t ^ plan_ref[0]] = (count.astype(F32) * scale).astype(x_ref.dtype)
+        x_ref[t] = (count.astype(F32) * scale).astype(x_ref.dtype)
         return carry
 
     lax.fori_loop(0, x_ref.shape[0], body, 0, unroll=4)
     for i, copy in enumerate(copies):
         copy.wait()
         multiply_tiles(
-            src_ref, dst_ref, None, x_ref, held_ref, acc_ref, i * STREAM, STREAM, 0, tiles
+            src_ref, dst_ref, x_ref, held_ref, acc_ref, i * STREAM, STREAM, 0, mask, tiles
         )
     store_chunks(acc_ref, out_refs, orders, 1.0)
 
 
-def first_pass(src, dst, plan, seed_t, w, n_src, orders, scale):
+def first_pass(src, dst, seed_t, w, n_src, orders, scale):
     seeds = seed_t.shape[1]
     sizes = [len(order) for order in orders]
     return pl.pallas_call(
         functools.partial(first_kernel, orders=orders, scale=scale),
-        in_specs=[SMEM] * 3 + [VMEM, pl.BlockSpec(memory_space=pltpu.HBM)],
+        in_specs=[SMEM] * 2 + [VMEM, pl.BlockSpec(memory_space=pltpu.HBM)],
         out_specs=[VMEM] * (1 + len(sizes)),
         scratch_shapes=[
             pltpu.VMEM((n_src, seeds, EDGE), BF16),
@@ -170,9 +172,9 @@
         ],
         out_shape=[pltpu.VMEM((2 * w.shape[0], EDGE, EDGE), w.dtype)]
         + [jax.ShapeDtypeStruct((rows, seeds, EDGE), BF16) for rows in sizes],
-        compiler_params=pltpu.CompilerParams(vmem_limit_bytes=37 * MIB),
+        compiler_params=pltpu.CompilerParams(vmem_limit_bytes=33 * MIB),
         cost_estimate=LIGHT,
-    )(src, dst, plan, seed_t, w)
+    )(src, dst, seed_t, w)
 
 
 def pass_kernel(src_ref, dst_ref, w_ref, *rest, flipped, in_orders, out_orders, wire):
@@ -183,12 +185,11 @@
         for i, tile in enumerate(order):
             x_ref[tile] = ref[i]
 
-    masks = None
     tiles = w_ref.shape[0] // 2
     base = tiles if flipped else 0
 
     def body(i, carry):
-        multiply_tiles(src_ref, dst_ref, masks, x_ref, w_ref, acc_ref, i * UNROLL, UNROLL, base)
+        multiply_tiles(src_ref, dst_ref, x_ref, w_ref, acc_ref, i * UNROLL, UNROLL, base)
         return carry
 
     lax.fori_loop(0, tiles // UNROLL, body, 0)
@@ -252,7 +253,7 @@
 
 
 def finish_kernel(
-    base_ref, seed_ref, stat_ref, x1_ref, u1_ref, y2_ref, w2_ref, hub_ref, auth_ref, *, users, items, scale
+    seed_ref, stat_ref, x1_ref, u1_ref, y2_ref, w2_ref, hub_ref, auth_ref, *, users, items, scale
 ):
     seeds = seed_ref.shape[1]
     total = jnp.sum(stat_ref[...], axis=0, keepdims=True)
@@ -273,9 +274,10 @@
     out_gain = s_item2 * GROW
     s_user2 = lax.rsqrt(out_gain * out_gain * raw_sq / users + 1e-06)
     columns = seed_columns(seed_ref)
+    base = (lax.axis_index("row") * lax.axis_size("col") + lax.axis_index("col")) * hub_ref.shape[1]
     for t in range(hub_ref.shape[1] // EDGE):
         raw = (alpha * w2_ref[t] + 0.15 * u1_ref[t]) * out_gain
-        tele = teleport_tile(columns, base_ref[0] + t * EDGE, scale)
+        tele = teleport_tile(columns, base + t * EDGE, scale)
         hub_ref[:, t * EDGE : (t + 1) * EDGE] = 0.85 * raw * s_user2 + 0.15 * tele
 
 
@@ -291,16 +293,14 @@
     seed_t = seed_users.T
     core, y, zhi = field(row, CORE), field(row, Y), field(row, ZHI)
     zlo, x = field(col, ZLO), field(col, X)
-    own_base = ((row * n_cols + col) * U_DEV).reshape(1)
-    zero = jnp.zeros((), jnp.int32)
     item_core, item_core_y = core << 1, (core << 1) | (y << 2)
     user_x, user_x_z = x << 4, (x << 4) | (zlo << 2)
-    plan = jnp.stack([user_x, zero, row * (U_DEV * n_cols)])
     cols1, cols2 = tile_cols ^ item_core, tile_cols ^ item_core_y
     rows1, rows2 = tile_rows ^ user_x, tile_rows ^ user_x_z
     held, keep, send = first_pass(
-        rows1, cols1, plan, seed_t, tile_values, 64, HALVES_ZY, scale
-    )
+        tile_rows, tile_cols, seed_t, tile_values, 64, HALVES_ZY, scale
+    )
+    keep, send, rows1, cols1, rows2, cols2 = lax.optimization_barrier((keep, send, rows1, cols1, rows2, cols2))
     (part,) = add_parts(held, exchanged([keep, send], "row", CORE), [BF16])
     (part,) = add_parts(held, gathered(part, "row", ZHI), [BF16])
     x1_all, part = add_parts(held, gathered(part, "row", Y), [F32, BF16])
@@ -342,14 +342,14 @@
     stats = lax.all_to_all(stat.reshape(n_rows * n_cols, 1, EDGE), ("row", "col"), 0, 0)
     return pl.pallas_call(
         functools.partial(finish_kernel, users=users, items=items, scale=scale),
-        in_specs=[SMEM] + [VMEM] * 6,
+        in_specs=[VMEM] * 6,
         out_specs=[VMEM] * 2,
         out_shape=[
             jax.ShapeDtypeStruct((seeds, U_DEV), F32),
             jax.ShapeDtypeStruct((seeds, I_DEV), F32),
         ],
         compiler_params=small,
-    )(own_base, seed_t, stats.reshape(n_rows * n_cols, EDGE), x1, u1, y2, w2)
+    )(seed_t, stats.reshape(n_rows * n_cols, EDGE), x1, u1, y2, w2)
 
 
 def solution(mesh):

time: 156 us -> 155 us (level)
  no operation moved by 1% of the time
where the time goes in v5:
time: 155 us
  starting transfers between devices  67.7 us (44%)
  waiting for transfers between devices  63.4 us (41%)
  Pallas kernels  21.3 us (14%)
    ppermute x29, starting transfers between devices, swapped(): return lax.ppermute(x, axis, [(i, i ^ by << part[0]) for i in range(16)])  57.6 us
    ppermute x29, waiting for transfers between devices, swapped(): return lax.ppermute(x, axis, [(i, i ^ by << part[0]) for i in range(16)])  50.5 us
    all_to_all x1, waiting for transfers between devices, per_device(): lax.all_to_all(stat.reshape(n_rows * n_cols, 1, EDGE), ('row', 'col'), 0, 0)  12.8 us
    pallas_call x3, Pallas kernels, tile_pass(): pl.pallas_call(functools.partial(pass_kernel, flipped=flipped, in_orders=...  12.1 us
    all_to_all x1, starting transfers between devices, per_device(): lax.all_to_all(stat.reshape(n_rows * n_cols, 1, EDGE), ('row', 'col'), 0, 0)  10.1 us
    pallas_call x1, Pallas kernels, first_pass(): pl.pallas_call(functools.partial(first_kernel, orders=orders, scale=scale...  7.2 us
  transfers between devices with their start and end apart: 30, of which 24 were waited for; matrix products, arithmetic and copies ran while one was open for 0% of the time, Pallas kernels for 0%

profile of v5, /device:TPU:1, one launch (start us, length us, event | category | flops | bytes accessed | tf_op | source)
XLA Modules:
  0.0 155.2 jit_solution(11473106111793325148)
XLA Ops:
  1.3 7.2 %shard_map.59 = (bf16[704,128,128]{2,1,0:T(8,128)(2,1)S(1)}, bf16[16,32,128]{2,1,0:T(8,128)(2,1)}, bf16[16,32,128]{2,1,0:T(8,128)(2,1)}) custom-call(s32[352]{0:T(512)} %src_ref.1, s32[352]{0:T(512)} %dst_ref.1, s32[16,32]{1,0:T(8,128)} %bitcast.12, bf16[352,128,128]{2,1,0:T(8,128)(2,1)} %w_ref.1), custom_call_target="tpu_custom_call" | custom-call | flops 1000000 | bytes 100000 | tf_op jit(solution)/shard_map/pallas_call | solution.py:163
  8.6 3.3 %collective-permute-start = (bf16[16,32,128]{2,1,0:T(8,128)(2,1)}, bf16[16,32,128]{2,1,0:T(8,128)(2,1)S(1)}, u32[]{:S(2)}, u32[]{:S(2)}) collective-permute-start(bf16[16,32,128]{2,1,0:T(8,128)(2,1)} %get-tuple-element.33), channel_id=1, source_target_pairs={{0,16},{16,0},{32,48},{48,32},{64,80},{80,64},{96,112},{112,96},{1... | collective-permute-start | bytes 393224 | tf_op jit(solution)/shard_map/ppermute | solution.py:41
  11.9 1.2 collective-permute-done.refs_2_
  13.1 0.9 copy-done
  14.0 5.3 %collective-permute-start.1 = (bf16[16,32,128]{2,1,0:T(8,128)(2,1)S(1)}, bf16[16,32,128]{2,1,0:T(8,128)(2,1)S(1)}, u32[]{:S(2)}, u32[]{:S(2)}) collective-permute-start(bf16[16,32,128]{2,1,0:T(8,128)(2,1)S(1)} %shard_map.60.refs_1_), channel_id=1, source_target_pairs={{0,128},{16,144},{32,160},{48,176},{64,192},{80,208},{96,224},{112... | collective-permute-start | bytes 393224 | tf_op jit(solution)/shard_map/ppermute | solution.py:41
  19.3 3.5 %collective-permute-done.1.refs_2_ = bf16[16,32,128]{2,1,0:T(8,128)(2,1)S(1)} collective-permute-done((bf16[16,32,128]{2,1,0:T(8,128)(2,1)S(1)}, bf16[16,32,128]{2,1,0:T(8,128)(2,1)S(1)}, u32[]{:S(2)}, u32[]{:S(2)}) %collective-permute-start.1) | collective-permute-done | bytes 131104 | tf_op jit(solution)/shard_map/ppermute | solution.py:41
  22.8 2.9 %collective-permute-start.4 = (bf16[16,32,128]{2,1,0:T(8,128)(2,1)S(1)}, bf16[16,32,128]{2,1,0:T(8,128)(2,1)S(1)}, u32[]{:S(2)}, u32[]{:S(2)}) collective-permute-start(bf16[16,32,128]{2,1,0:T(8,128)(2,1)S(1)} %shard_map.61.refs_1_), channel_id=1, source_target_pairs={{0,96},{16,112},{32,64},{48,80},{64,32},{80,48},{96,0},{112,16},{1... | collective-permute-start | bytes 393224 | tf_op jit(solution)/shard_map/ppermute | solution.py:41
  26.4 4.8 %collective-permute-done.4.refs_4_ = bf16[16,32,128]{2,1,0:T(8,128)(2,1)S(1)} collective-permute-done((bf16[16,32,128]{2,1,0:T(8,128)(2,1)S(1)}, bf16[16,32,128]{2,1,0:T(8,128)(2,1)S(1)}, u32[]{:S(2)}, u32[]{:S(2)}) %collective-permute-start.4) | collective-permute-done | bytes 131104 | tf_op jit(solution)/shard_map/ppermute | solution.py:41
  31.3 3.4 %collective-permute-start.5 = (bf16[16,32,128]{2,1,0:T(8,128)(2,1)S(1)}, bf16[16,32,128]{2,1,0:T(8,128)(2,1)S(1)}, u32[]{:S(2)}, u32[]{:S(2)}) collective-permute-start(bf16[16,32,128]{2,1,0:T(8,128)(2,1)S(1)} %get-tuple-element.38.rest_0_), channel_id=1, source_target_pairs={{0,16},{16,0},{32,48},{48,32},{64,80},{80,64},{96,112},{112,96},{1... | collective-permute-start | bytes 393224 | tf_op jit(solution)/shard_map/ppermute | solution.py:41
  34.7 1.0 collective-permute-done.5.rest_1_
  35.7 4.0 %shard_map.63 = (bf16[16,32,128]{2,1,0:T(8,128)(2,1)S(1)}, bf16[16,32,128]{2,1,0:T(8,128)(2,1)S(1)}, bf16[16,32,128]{2,1,0:T(8,128)(2,1)S(1)}, bf16[16,32,128]{2,1,0:T(8,128)(2,1)S(1)}) custom-call(s32[352]{0:T(512)S(1)} %get-tuple-element.37.src_ref, s32[352]{0:T(512)S(1)} %get-tuple-element.35.dst_ref.src_ref, ...), custom_call_target="tpu_custom_call" | custom-call | flops 1000000 | bytes 100000 | tf_op jit(solution)/shard_map/pallas_call | solution.py:218
  39.7 1.3 collective-permute-start.6
  41.0 2.5 %collective-permute-start.7 = (bf16[16,32,128]{2,1,0:T(8,128)(2,1)S(1)}, bf16[16,32,128]{2,1,0:T(8,128)(2,1)S(1)}, u32[]{:S(2)}, u32[]{:S(2)}) collective-permute-start(bf16[16,32,128]{2,1,0:T(8,128)(2,1)S(1)} %get-tuple-element.41), channel_id=1, source_target_pairs={{0,8},{1,9},{2,10},{3,11},{4,12},{5,13},{6,14},{7,15},{8,0},{9,1},... | collective-permute-start | bytes 393224 | tf_op jit(solution)/shard_map/ppermute | solution.py:41
  44.5 5.0 %collective-permute-done.7.refs_3_ = bf16[16,32,128]{2,1,0:T(8,128)(2,1)S(1)} collective-permute-done((bf16[16,32,128]{2,1,0:T(8,128)(2,1)S(1)}, bf16[16,32,128]{2,1,0:T(8,128)(2,1)S(1)}, u32[]{:S(2)}, u32[]{:S(2)}) %collective-permute-start.7) | collective-permute-done | bytes 131104 | tf_op jit(solution)/shard_map/ppermute | solution.py:41
  49.6 2.5 %collective-permute-done.8.refs_4_ = bf16[16,32,128]{2,1,0:T(8,128)(2,1)S(1)} collective-permute-done((bf16[16,32,128]{2,1,0:T(8,128)(2,1)S(1)}, bf16[16,32,128]{2,1,0:T(8,128)(2,1)S(1)}, u32[]{:S(2)}, u32[]{:S(2)}) %collective-permute-start.8) | collective-permute-done | bytes 131104 | tf_op jit(solution)/shard_map/ppermute | solution.py:41
  52.1 4.2 %collective-permute-start.9 = (bf16[16,32,128]{2,1,0:T(8,128)(2,1)S(1)}, bf16[16,32,128]{2,1,0:T(8,128)(2,1)S(1)}, u32[]{:S(2)}, u32[]{:S(2)}) collective-permute-start(bf16[16,32,128]{2,1,0:T(8,128)(2,1)S(1)} %shard_map.64.refs_1_), channel_id=1, source_target_pairs={{0,2},{1,3},{2,0},{3,1},{4,6},{5,7},{6,4},{7,5},{8,10},{9,11},{10,... | collective-permute-start | bytes 393224 | tf_op jit(solution)/shard_map/ppermute | solution.py:41
  56.3 2.9 %collective-permute-done.9.refs_2_ = bf16[16,32,128]{2,1,0:T(8,128)(2,1)S(1)} collective-permute-done((bf16[16,32,128]{2,1,0:T(8,128)(2,1)S(1)}, bf16[16,32,128]{2,1,0:T(8,128)(2,1)S(1)}, u32[]{:S(2)}, u32[]{:S(2)}) %collective-permute-start.9) | collective-permute-done | bytes 131104 | tf_op jit(solution)/shard_map/ppermute | solution.py:41
  59.2 1.7 %collective-permute-start.10 = (bf16[16,32,128]{2,1,0:T(8,128)(2,1)S(1)}, bf16[16,32,128]{2,1,0:T(8,128)(2,1)S(1)}, u32[]{:S(2)}, u32[]{:S(2)}) collective-permute-start(bf16[16,32,128]{2,1,0:T(8,128)(2,1)S(1)} %shard_map.65.refs_1_), channel_id=1, source_target_pairs={{0,1},{1,0},{2,3},{3,2},{4,5},{5,4},{6,7},{7,6},{8,9},{9,8},{10,11... | collective-permute-start | bytes 393224 | tf_op jit(solution)/shard_map/ppermute | solution.py:41
  60.9 3.4 %collective-permute-done.10.refs_2_ = bf16[16,32,128]{2,1,0:T(8,128)(2,1)S(1)} collective-permute-done((bf16[16,32,128]{2,1,0:T(8,128)(2,1)S(1)}, bf16[16,32,128]{2,1,0:T(8,128)(2,1)S(1)}, u32[]{:S(2)}, u32[]{:S(2)}) %collective-permute-start.10) | collective-permute-done | bytes 131104 | tf_op jit(solution)/shard_map/ppermute | solution.py:41
  64.3 2.3 %collective-permute-start.13 = (bf16[16,32,128]{2,1,0:T(8,128)(2,1)S(1)}, bf16[16,32,128]{2,1,0:T(8,128)(2,1)S(1)}, u32[]{:S(2)}, u32[]{:S(2)}) collective-permute-start(bf16[16,32,128]{2,1,0:T(8,128)(2,1)S(1)} %get-tuple-element.43.rest_0_), channel_id=1, source_target_pairs={{0,12},{1,13},{2,14},{3,15},{4,8},{5,9},{6,10},{7,11},{8,4},{9,5},... | collective-permute-start | bytes 393224 | tf_op jit(solution)/shard_map/ppermute | solution.py:41
  66.6 1.0 collective-permute-start.11
  67.6 2.3 %collective-permute-done.13.rest_3_ = bf16[16,32,128]{2,1,0:T(8,128)(2,1)S(1)} collective-permute-done((bf16[16,32,128]{2,1,0:T(8,128)(2,1)S(1)}, bf16[16,32,128]{2,1,0:T(8,128)(2,1)S(1)}, u32[]{:S(2)}, u32[]{:S(2)}) %collective-permute-start.13) | collective-permute-done | bytes 131104 | tf_op jit(solution)/shard_map/ppermute | solution.py:41
  69.9 2.0 %collective-permute-done.12.rest_2_ = bf16[16,32,128]{2,1,0:T(8,128)(2,1)S(1)} collective-permute-done((bf16[16,32,128]{2,1,0:T(8,128)(2,1)S(1)}, bf16[16,32,128]{2,1,0:T(8,128)(2,1)S(1)}, u32[]{:S(2)}, u32[]{:S(2)}) %collective-permute-start.12) | collective-permute-done | bytes 131104 | tf_op jit(solution)/shard_map/ppermute | solution.py:41
  71.9 4.0 %shard_map.67 = (f32[16,32,128]{2,1,0:T(8,128)S(1)}, f32[16,32,128]{2,1,0:T(8,128)S(1)}) custom-call(s32[352]{0:T(512)S(1)} %get-tuple-element.35.dst_ref.src_ref, s32[352]{0:T(512)S(1)} %get-tuple-element.36.dst_ref.src_ref, bf16[704,128,128]{2,1,0:T(8,128)(2,1)S(1)} %get-tuple-element.29.refs_0_.w_ref, bf16[16,32,128]{2,1,0:T(8,128)(2,1)S(1)} %get-tuple-element.43.rest_0_, ...), custom_call_target="tpu_custom_call" | custom-call | flops 1000000 | bytes 100000 | tf_op jit(solution)/shard_map/pallas_call | solution.py:218
  75.9 5.6 %collective-permute-start.14 = (f32[16,32,128]{2,1,0:T(8,128)S(1)}, f32[16,32,128]{2,1,0:T(8,128)S(1)}, u32[]{:S(2)}, u32[]{:S(2)}) collective-permute-start(f32[16,32,128]{2,1,0:T(8,128)S(1)} %get-tuple-element.45), channel_id=1, source_target_pairs={{0,16},{16,0},{32,48},{48,32},{64,80},{80,64},{96,112},{112,96},{1... | collective-permute-start | bytes 786440 | tf_op jit(solution)/shard_map/ppermute | solution.py:41
  81.5 1.2 collective-permute-done.14.refs_2_
  82.7 1.8 %collective-permute-start.17 = (f32[4,32,128]{2,1,0:T(8,128)S(1)}, f32[4,32,128]{2,1,0:T(8,128)S(1)}, u32[]{:S(2)}, u32[]{:S(2)}) collective-permute-start(f32[4,32,128]{2,1,0:T(8,128)S(1)} %get-tuple-element.60), channel_id=1, source_target_pairs={{0,96},{16,112},{32,64},{48,80},{64,32},{80,48},{96,0},{112,16},{1... | collective-permute-start | bytes 196616 | tf_op jit(solution)/shard_map/ppermute | solution.py:41
  84.8 1.3 collective-permute-start.15
  86.1 1.1 collective-permute-done.17.refs_4_
  87.2 2.0 %collective-permute-done.16.refs_3_ = f32[4,32,128]{2,1,0:T(8,128)S(1)} collective-permute-done((f32[4,32,128]{2,1,0:T(8,128)S(1)}, f32[4,32,128]{2,1,0:T(8,128)S(1)}, u32[]{:S(2)}, u32[]{:S(2)}) %collective-permute-start.16) | collective-permute-done | bytes 65568 | tf_op jit(solution)/shard_map/ppermute | solution.py:41
  89.2 5.0 %collective-permute-start.18 = (f32[4,32,128]{2,1,0:T(8,128)S(1)}, f32[4,32,128]{2,1,0:T(8,128)S(1)}, u32[]{:S(2)}, u32[]{:S(2)}) collective-permute-start(f32[4,32,128]{2,1,0:T(8,128)S(1)} %shard_map.69.refs_1_), channel_id=1, source_target_pairs={{0,128},{16,144},{32,160},{48,176},{64,192},{80,208},{96,224},{112... | collective-permute-start | bytes 196616 | tf_op jit(solution)/shard_map/ppermute | solution.py:41
  94.2 2.1 %collective-permute-done.18.refs_2_ = f32[4,32,128]{2,1,0:T(8,128)S(1)} collective-permute-done((f32[4,32,128]{2,1,0:T(8,128)S(1)}, f32[4,32,128]{2,1,0:T(8,128)S(1)}, u32[]{:S(2)}, u32[]{:S(2)}) %collective-permute-start.18) | collective-permute-done | bytes 65568 | tf_op jit(solution)/shard_map/ppermute | solution.py:41
  96.3 1.7 %collective-permute-start.21 = (bf16[4,32,128]{2,1,0:T(8,128)(2,1)S(1)}, bf16[4,32,128]{2,1,0:T(8,128)(2,1)S(1)}, u32[]{:S(2)}, u32[]{:S(2)}) collective-permute-start(bf16[4,32,128]{2,1,0:T(8,128)(2,1)S(1)} %get-tuple-element.48), channel_id=1, source_target_pairs={{0,96},{16,112},{32,64},{48,80},{64,32},{80,48},{96,0},{112,16},{1... | collective-permute-start | bytes 98312 | tf_op jit(solution)/shard_map/ppermute | solution.py:41
  98.0 1.2 collective-permute-start.20
  99.6 2.3 %collective-permute-done.19 = bf16[4,32,128]{2,1,0:T(8,128)(2,1)S(1)} collective-permute-done((bf16[4,32,128]{2,1,0:T(8,128)(2,1)S(1)}, bf16[4,32,128]{2,1,0:T(8,128)(2,1)S(1)}, u32[]{:S(2)}, u32[]{:S(2)}) %collective-permute-start.19) | collective-permute-done | bytes 32800 | tf_op jit(solution)/shard_map/ppermute | solution.py:41
  102.3 4.5 %collective-permute-start.22 = (bf16[16,32,128]{2,1,0:T(8,128)(2,1)S(1)}, bf16[16,32,128]{2,1,0:T(8,128)(2,1)S(1)}, u32[]{:S(2)}, u32[]{:S(2)}) collective-permute-start(bf16[16,32,128]{2,1,0:T(8,128)(2,1)S(1)} %constant_dynamic-update-slice_fusion.rest_0_), channel_id=1, source_target_pairs={{0,16},{16,0},{32,48},{48,32},{64,80},{80,64},{96,112},{112,96},{1... | collective-permute-start | bytes 393224 | tf_op jit(solution)/shard_map/ppermute | solution.py:41
  106.8 1.0 collective-permute-done.22.rest_1_
  107.8 4.1 %shard_map.71 = (f32[16,32,128]{2,1,0:T(8,128)S(1)}, f32[17,32,128]{2,1,0:T(8,128)S(1)}, f32[17,32,128]{2,1,0:T(8,128)S(1)}, f32[17,32,128]{2,1,0:T(8,128)S(1)}) custom-call(s32[352]{0:T(512)S(1)} %get-tuple-element.36.dst_ref.src_ref, s32[352]{0:T(512)S(1)} %get-tuple-element.47.dst_ref, bf16[704,128,128]{2,1,0:T(8,128)(2,1)S(1)} %get-tuple-element.29.refs_0_.w_ref, ...), custom_call_target="tpu_custom_call" | custom-call | flops 1000000 | bytes 100000 | tf_op jit(solution)/shard_map/pallas_call | solution.py:218
  112.0 1.1 collective-permute-start.25
  113.1 1.2 collective-permute-start.24
  114.3 1.1 collective-permute-start.23
  115.4 5.3 %collective-permute-done.25 = f16[17,32,128]{2,1,0:T(8,128)(2,1)S(1)} collective-permute-done((f16[17,32,128]{2,1,0:T(8,128)(2,1)S(1)}, f16[17,32,128]{2,1,0:T(8,128)(2,1)S(1)}, u32[]{:S(2)}, u32[]{:S(2)}) %collective-permute-start.25) | collective-permute-done | bytes 139296 | tf_op jit(solution)/shard_map/ppermute | solution.py:41
  121.8 1.6 %collective-permute-start.28 = (f32[4,32,128]{2,1,0:T(8,128)S(1)}, f32[4,32,128]{2,1,0:T(8,128)S(1)}, u32[]{:S(2)}, u32[]{:S(2)}) collective-permute-start(f32[4,32,128]{2,1,0:T(8,128)S(1)} %get-tuple-element.56), channel_id=1, source_target_pairs={{0,3},{1,2},{2,1},{3,0},{4,7},{5,6},{6,5},{7,4},{8,11},{9,10},{10,... | collective-permute-start | bytes 196616 | tf_op jit(solution)/shard_map/ppermute | solution.py:41
  123.4 2.0 %collective-permute-start.26 = (f32[4,32,128]{2,1,0:T(8,128)S(1)}, f32[4,32,128]{2,1,0:T(8,128)S(1)}, u32[]{:S(2)}, u32[]{:S(2)}) collective-permute-start(f32[4,32,128]{2,1,0:T(8,128)S(1)} %get-tuple-element.58), channel_id=1, source_target_pairs={{0,1},{1,0},{2,3},{3,2},{4,5},{5,4},{6,7},{7,6},{8,9},{9,8},{10,11... | collective-permute-start | bytes 196616 | tf_op jit(solution)/shard_map/ppermute | solution.py:41
  125.5 1.5 collective-permute-done.28.rest_3_
  127.0 3.6 %collective-permute-done.27.rest_2_ = f32[4,32,128]{2,1,0:T(8,128)S(1)} collective-permute-done((f32[4,32,128]{2,1,0:T(8,128)S(1)}, f32[4,32,128]{2,1,0:T(8,128)S(1)}, u32[]{:S(2)}, u32[]{:S(2)}) %collective-permute-start.27) | collective-permute-done | bytes 65568 | tf_op jit(solution)/shard_map/ppermute | solution.py:41
  131.3 10.1 %all-to-all-start = ((f32[256,1,128]{2,1,0:T(1,128)}), f32[256,1,128]{2,1,0:T(1,128)S(1)}, u32[]{:S(2)}, u32[]{:S(2)}) async-start(f32[256,1,128]{2,1,0:T(1,128)} %bitcast.5), calls=%async_computation | async-start | bytes 262144 | tf_op jit(solution)/shard_map/all_to_all | solution.py:342
  141.4 12.8 %all-to-all-done = f32[256,1,128]{2,1,0:T(1,128)S(1)} async-done(((f32[256,1,128]{2,1,0:T(1,128)}), f32[256,1,128]{2,1,0:T(1,128)S(1)}, u32[]{:S(2)}, u32[]{:S(2)}) %all-to-all-start) | async-done | bytes 131104 | tf_op jit(solution)/shard_map/all_to_all | solution.py:342
  (51 shorter events, 6.7 us)
Async XLA Ops:
  8.6 4.5 %collective-permute-start = (bf16[16,32,128]{2,1,0:T(8,128)(2,1)}, bf16[16,32,128]{2,1,0:T(8,128)(2,1)S(1)}, u32[]{:S(2)}, u32[]{:S(2)}) collective-permute-start(bf16[16,32,128]{2,1,0:T(8,128)(2,1)} %get-tuple-element.33), channel_id=1, source_target_pairs={{0,16},{16,0},{32,48},{48,32},{64,80},{80,64},{96,112},{112,96},{1... | collective-permute-start | bytes 393224 | tf_op jit(solution)/shard_map/ppermute | solution.py:41
  13.1 0.9 copy-start
  14.0 8.7 %collective-permute-start.1 = (bf16[16,32,128]{2,1,0:T(8,128)(2,1)S(1)}, bf16[16,32,128]{2,1,0:T(8,128)(2,1)S(1)}, u32[]{:S(2)}, u32[]{:S(2)}) collective-permute-start(bf16[16,32,128]{2,1,0:T(8,128)(2,1)S(1)} %shard_map.60.refs_1_), channel_id=1, source_target_pairs={{0,128},{16,144},{32,160},{48,176},{64,192},{80,208},{96,224},{112... | collective-permute-start | bytes 393224 | tf_op jit(solution)/shard_map/ppermute | solution.py:41
  22.8 8.4 %collective-permute-start.4 = (bf16[16,32,128]{2,1,0:T(8,128)(2,1)S(1)}, bf16[16,32,128]{2,1,0:T(8,128)(2,1)S(1)}, u32[]{:S(2)}, u32[]{:S(2)}) collective-permute-start(bf16[16,32,128]{2,1,0:T(8,128)(2,1)S(1)} %shard_map.61.refs_1_), channel_id=1, source_target_pairs={{0,96},{16,112},{32,64},{48,80},{64,32},{80,48},{96,0},{112,16},{1... | collective-permute-start | bytes 393224 | tf_op jit(solution)/shard_map/ppermute | solution.py:41
  25.7 5.4 %collective-permute-start.3 = (bf16[16,32,128]{2,1,0:T(8,128)(2,1)S(1)}, bf16[16,32,128]{2,1,0:T(8,128)(2,1)S(1)}, u32[]{:S(2)}, u32[]{:S(2)}) collective-permute-start(bf16[16,32,128]{2,1,0:T(8,128)(2,1)S(1)} %shard_map.61.refs_1_), channel_id=1, source_target_pairs={{0,64},{16,80},{32,96},{48,112},{64,0},{80,16},{96,32},{112,48},{1... | collective-permute-start | bytes 393224 | tf_op jit(solution)/shard_map/ppermute | solution.py:41
  26.1 5.2 %collective-permute-start.2 = (bf16[16,32,128]{2,1,0:T(8,128)(2,1)S(1)}, bf16[16,32,128]{2,1,0:T(8,128)(2,1)S(1)}, u32[]{:S(2)}, u32[]{:S(2)}) collective-permute-start(bf16[16,32,128]{2,1,0:T(8,128)(2,1)S(1)} %shard_map.61.refs_1_), channel_id=1, source_target_pairs={{0,32},{16,48},{32,0},{48,16},{64,96},{80,112},{96,64},{112,80},{1... | collective-permute-start | bytes 393224 | tf_op jit(solution)/shard_map/ppermute | solution.py:41
  31.3 4.4 %collective-permute-start.5 = (bf16[16,32,128]{2,1,0:T(8,128)(2,1)S(1)}, bf16[16,32,128]{2,1,0:T(8,128)(2,1)S(1)}, u32[]{:S(2)}, u32[]{:S(2)}) collective-permute-start(bf16[16,32,128]{2,1,0:T(8,128)(2,1)S(1)} %get-tuple-element.38.rest_0_), channel_id=1, source_target_pairs={{0,16},{16,0},{32,48},{48,32},{64,80},{80,64},{96,112},{112,96},{1... | collective-permute-start | bytes 393224 | tf_op jit(solution)/shard_map/ppermute | solution.py:41
  39.7 4.8 %collective-permute-start.6 = (bf16[16,32,128]{2,1,0:T(8,128)(2,1)S(1)}, bf16[16,32,128]{2,1,0:T(8,128)(2,1)S(1)}, u32[]{:S(2)}, u32[]{:S(2)}) collective-permute-start(bf16[16,32,128]{2,1,0:T(8,128)(2,1)S(1)} %get-tuple-element.40), channel_id=1, source_target_pairs={{0,4},{1,5},{2,6},{3,7},{4,0},{5,1},{6,2},{7,3},{8,12},{9,13},{10,... | collective-permute-start | bytes 393224 | tf_op jit(solution)/shard_map/ppermute | solution.py:41
  41.0 8.6 %collective-permute-start.7 = (bf16[16,32,128]{2,1,0:T(8,128)(2,1)S(1)}, bf16[16,32,128]{2,1,0:T(8,128)(2,1)S(1)}, u32[]{:S(2)}, u32[]{:S(2)}) collective-permute-start(bf16[16,32,128]{2,1,0:T(8,128)(2,1)S(1)} %get-tuple-element.41), channel_id=1, source_target_pairs={{0,8},{1,9},{2,10},{3,11},{4,12},{5,13},{6,14},{7,15},{8,0},{9,1},... | collective-permute-start | bytes 393224 | tf_op jit(solution)/shard_map/ppermute | solution.py:41
  43.4 8.6 %collective-permute-start.8 = (bf16[16,32,128]{2,1,0:T(8,128)(2,1)S(1)}, bf16[16,32,128]{2,1,0:T(8,128)(2,1)S(1)}, u32[]{:S(2)}, u32[]{:S(2)}) collective-permute-start(bf16[16,32,128]{2,1,0:T(8,128)(2,1)S(1)} %get-tuple-element.42), channel_id=1, source_target_pairs={{0,12},{1,13},{2,14},{3,15},{4,8},{5,9},{6,10},{7,11},{8,4},{9,5},... | collective-permute-start | bytes 393224 | tf_op jit(solution)/shard_map/ppermute | solution.py:41
  52.1 7.0 %collective-permute-start.9 = (bf16[16,32,128]{2,1,0:T(8,128)(2,1)S(1)}, bf16[16,32,128]{2,1,0:T(8,128)(2,1)S(1)}, u32[]{:S(2)}, u32[]{:S(2)}) collective-permute-start(bf16[16,32,128]{2,1,0:T(8,128)(2,1)S(1)} %shard_map.64.refs_1_), channel_id=1, source_target_pairs={{0,2},{1,3},{2,0},{3,1},{4,6},{5,7},{6,4},{7,5},{8,10},{9,11},{10,... | collective-permute-start | bytes 393224 | tf_op jit(solution)/shard_map/ppermute | solution.py:41
  59.2 5.1 %collective-permute-start.10 = (bf16[16,32,128]{2,1,0:T(8,128)(2,1)S(1)}, bf16[16,32,128]{2,1,0:T(8,128)(2,1)S(1)}, u32[]{:S(2)}, u32[]{:S(2)}) collective-permute-start(bf16[16,32,128]{2,1,0:T(8,128)(2,1)S(1)} %shard_map.65.refs_1_), channel_id=1, source_target_pairs={{0,1},{1,0},{2,3},{3,2},{4,5},{5,4},{6,7},{7,6},{8,9},{9,8},{10,11... | collective-permute-start | bytes 393224 | tf_op jit(solution)/shard_map/ppermute | solution.py:41
  64.3 5.7 %collective-permute-start.13 = (bf16[16,32,128]{2,1,0:T(8,128)(2,1)S(1)}, bf16[16,32,128]{2,1,0:T(8,128)(2,1)S(1)}, u32[]{:S(2)}, u32[]{:S(2)}) collective-permute-start(bf16[16,32,128]{2,1,0:T(8,128)(2,1)S(1)} %get-tuple-element.43.rest_0_), channel_id=1, source_target_pairs={{0,12},{1,13},{2,14},{3,15},{4,8},{5,9},{6,10},{7,11},{8,4},{9,5},... | collective-permute-start | bytes 393224 | tf_op jit(solution)/shard_map/ppermute | solution.py:41
  66.6 5.3 %collective-permute-start.12 = (bf16[16,32,128]{2,1,0:T(8,128)(2,1)S(1)}, bf16[16,32,128]{2,1,0:T(8,128)(2,1)S(1)}, u32[]{:S(2)}, u32[]{:S(2)}) collective-permute-start(bf16[16,32,128]{2,1,0:T(8,128)(2,1)S(1)} %get-tuple-element.43.rest_0_), channel_id=1, source_target_pairs={{0,8},{1,9},{2,10},{3,11},{4,12},{5,13},{6,14},{7,15},{8,0},{9,1},... | collective-permute-start | bytes 393224 | tf_op jit(solution)/shard_map/ppermute | solution.py:41
  66.6 5.3 %collective-permute-start.11 = (bf16[16,32,128]{2,1,0:T(8,128)(2,1)S(1)}, bf16[16,32,128]{2,1,0:T(8,128)(2,1)S(1)}, u32[]{:S(2)}, u32[]{:S(2)}) collective-permute-start(bf16[16,32,128]{2,1,0:T(8,128)(2,1)S(1)} %get-tuple-element.43.rest_0_), channel_id=1, source_target_pairs={{0,4},{1,5},{2,6},{3,7},{4,0},{5,1},{6,2},{7,3},{8,12},{9,13},{10,... | collective-permute-start | bytes 393224 | tf_op jit(solution)/shard_map/ppermute | solution.py:41
  75.9 6.8 %collective-permute-start.14 = (f32[16,32,128]{2,1,0:T(8,128)S(1)}, f32[16,32,128]{2,1,0:T(8,128)S(1)}, u32[]{:S(2)}, u32[]{:S(2)}) collective-permute-start(f32[16,32,128]{2,1,0:T(8,128)S(1)} %get-tuple-element.45), channel_id=1, source_target_pairs={{0,16},{16,0},{32,48},{48,32},{64,80},{80,64},{96,112},{112,96},{1... | collective-permute-start | bytes 786440 | tf_op jit(solution)/shard_map/ppermute | solution.py:41
  82.7 4.4 %collective-permute-start.17 = (f32[4,32,128]{2,1,0:T(8,128)S(1)}, f32[4,32,128]{2,1,0:T(8,128)S(1)}, u32[]{:S(2)}, u32[]{:S(2)}) collective-permute-start(f32[4,32,128]{2,1,0:T(8,128)S(1)} %get-tuple-element.60), channel_id=1, source_target_pairs={{0,96},{16,112},{32,64},{48,80},{64,32},{80,48},{96,0},{112,16},{1... | collective-permute-start | bytes 196616 | tf_op jit(solution)/shard_map/ppermute | solution.py:41
  84.5 4.6 %collective-permute-start.16 = (f32[4,32,128]{2,1,0:T(8,128)S(1)}, f32[4,32,128]{2,1,0:T(8,128)S(1)}, u32[]{:S(2)}, u32[]{:S(2)}) collective-permute-start(f32[4,32,128]{2,1,0:T(8,128)S(1)} %get-tuple-element.61), channel_id=1, source_target_pairs={{0,64},{16,80},{32,96},{48,112},{64,0},{80,16},{96,32},{112,48},{1... | collective-permute-start | bytes 196616 | tf_op jit(solution)/shard_map/ppermute | solution.py:41
  84.8 4.3 %collective-permute-start.15 = (f32[4,32,128]{2,1,0:T(8,128)S(1)}, f32[4,32,128]{2,1,0:T(8,128)S(1)}, u32[]{:S(2)}, u32[]{:S(2)}) collective-permute-start(f32[4,32,128]{2,1,0:T(8,128)S(1)} %get-tuple-element.62), channel_id=1, source_target_pairs={{0,32},{16,48},{32,0},{48,16},{64,96},{80,112},{96,64},{112,80},{1... | collective-permute-start | bytes 196616 | tf_op jit(solution)/shard_map/ppermute | solution.py:41
  89.2 65.1 %copy-start.1 = (s32[32,16]{0,1:T(8,128)S(1)}, s32[32,16]{0,1:T(8,128)}, u32[]{:S(2)}) copy-start(s32[32,16]{0,1:T(8,128)} %param.7) | copy-start | bytes 6148
  89.2 7.1 %collective-permute-start.18 = (f32[4,32,128]{2,1,0:T(8,128)S(1)}, f32[4,32,128]{2,1,0:T(8,128)S(1)}, u32[]{:S(2)}, u32[]{:S(2)}) collective-permute-start(f32[4,32,128]{2,1,0:T(8,128)S(1)} %shard_map.69.refs_1_), channel_id=1, source_target_pairs={{0,128},{16,144},{32,160},{48,176},{64,192},{80,208},{96,224},{112... | collective-permute-start | bytes 196616 | tf_op jit(solution)/shard_map/ppermute | solution.py:41
  96.3 6.0 %collective-permute-start.21 = (bf16[4,32,128]{2,1,0:T(8,128)(2,1)S(1)}, bf16[4,32,128]{2,1,0:T(8,128)(2,1)S(1)}, u32[]{:S(2)}, u32[]{:S(2)}) collective-permute-start(bf16[4,32,128]{2,1,0:T(8,128)(2,1)S(1)} %get-tuple-element.48), channel_id=1, source_target_pairs={{0,96},{16,112},{32,64},{48,80},{64,32},{80,48},{96,0},{112,16},{1... | collective-permute-start | bytes 98312 | tf_op jit(solution)/shard_map/ppermute | solution.py:41
  98.0 4.3 %collective-permute-start.20 = (bf16[4,32,128]{2,1,0:T(8,128)(2,1)S(1)}, bf16[4,32,128]{2,1,0:T(8,128)(2,1)S(1)}, u32[]{:S(2)}, u32[]{:S(2)}) collective-permute-start(bf16[4,32,128]{2,1,0:T(8,128)(2,1)S(1)} %get-tuple-element.48), channel_id=1, source_target_pairs={{0,64},{16,80},{32,96},{48,112},{64,0},{80,16},{96,32},{112,48},{1... | collective-permute-start | bytes 98312 | tf_op jit(solution)/shard_map/ppermute | solution.py:41
  99.2 2.8 %collective-permute-start.19 = (bf16[4,32,128]{2,1,0:T(8,128)(2,1)S(1)}, bf16[4,32,128]{2,1,0:T(8,128)(2,1)S(1)}, u32[]{:S(2)}, u32[]{:S(2)}) collective-permute-start(bf16[4,32,128]{2,1,0:T(8,128)(2,1)S(1)} %get-tuple-element.48), channel_id=1, source_target_pairs={{0,32},{16,48},{32,0},{48,16},{64,96},{80,112},{96,64},{112,80},{1... | collective-permute-start | bytes 98312 | tf_op jit(solution)/shard_map/ppermute | solution.py:41
  102.3 5.5 %collective-permute-start.22 = (bf16[16,32,128]{2,1,0:T(8,128)(2,1)S(1)}, bf16[16,32,128]{2,1,0:T(8,128)(2,1)S(1)}, u32[]{:S(2)}, u32[]{:S(2)}) collective-permute-start(bf16[16,32,128]{2,1,0:T(8,128)(2,1)S(1)} %constant_dynamic-update-slice_fusion.rest_0_), channel_id=1, source_target_pairs={{0,16},{16,0},{32,48},{48,32},{64,80},{80,64},{96,112},{112,96},{1... | collective-permute-start | bytes 393224 | tf_op jit(solution)/shard_map/ppermute | solution.py:41
  112.0 8.8 %collective-permute-start.25 = (f16[17,32,128]{2,1,0:T(8,128)(2,1)S(1)}, f16[17,32,128]{2,1,0:T(8,128)(2,1)S(1)}, u32[]{:S(2)}, u32[]{:S(2)}) collective-permute-start(f16[17,32,128]{2,1,0:T(8,128)(2,1)S(1)} %convert_element_type.22), channel_id=1, source_target_pairs={{0,12},{1,13},{2,14},{3,15},{4,8},{5,9},{6,10},{7,11},{8,4},{9,5},... | collective-permute-start | bytes 417800 | tf_op jit(solution)/shard_map/ppermute | solution.py:41
  113.1 7.7 %collective-permute-start.24 = (f16[17,32,128]{2,1,0:T(8,128)(2,1)S(1)}, f16[17,32,128]{2,1,0:T(8,128)(2,1)S(1)}, u32[]{:S(2)}, u32[]{:S(2)}) collective-permute-start(f16[17,32,128]{2,1,0:T(8,128)(2,1)S(1)} %convert_element_type.20), channel_id=1, source_target_pairs={{0,8},{1,9},{2,10},{3,11},{4,12},{5,13},{6,14},{7,15},{8,0},{9,1},... | collective-permute-start | bytes 417800 | tf_op jit(solution)/shard_map/ppermute | solution.py:41
  114.3 7.3 %collective-permute-start.23 = (f16[17,32,128]{2,1,0:T(8,128)(2,1)S(1)}, f16[17,32,128]{2,1,0:T(8,128)(2,1)S(1)}, u32[]{:S(2)}, u32[]{:S(2)}) collective-permute-start(f16[17,32,128]{2,1,0:T(8,128)(2,1)S(1)} %convert_element_type.18), channel_id=1, source_target_pairs={{0,4},{1,5},{2,6},{3,7},{4,0},{5,1},{6,2},{7,3},{8,12},{9,13},{10,... | collective-permute-start | bytes 417800 | tf_op jit(solution)/shard_map/ppermute | solution.py:41
  121.8 5.2 %collective-permute-start.28 = (f32[4,32,128]{2,1,0:T(8,128)S(1)}, f32[4,32,128]{2,1,0:T(8,128)S(1)}, u32[]{:S(2)}, u32[]{:S(2)}) collective-permute-start(f32[4,32,128]{2,1,0:T(8,128)S(1)} %get-tuple-element.56), channel_id=1, source_target_pairs={{0,3},{1,2},{2,1},{3,0},{4,7},{5,6},{6,5},{7,4},{8,11},{9,10},{10,... | collective-permute-start | bytes 196616 | tf_op jit(solution)/shard_map/ppermute | solution.py:41
  123.4 7.1 %collective-permute-start.27 = (f32[4,32,128]{2,1,0:T(8,128)S(1)}, f32[4,32,128]{2,1,0:T(8,128)S(1)}, u32[]{:S(2)}, u32[]{:S(2)}) collective-permute-start(f32[4,32,128]{2,1,0:T(8,128)S(1)} %get-tuple-element.57), channel_id=1, source_target_pairs={{0,2},{1,3},{2,0},{3,1},{4,6},{5,7},{6,4},{7,5},{8,10},{9,11},{10,... | collective-permute-start | bytes 196616 | tf_op jit(solution)/shard_map/ppermute | solution.py:41
  123.4 7.1 %collective-permute-start.26 = (f32[4,32,128]{2,1,0:T(8,128)S(1)}, f32[4,32,128]{2,1,0:T(8,128)S(1)}, u32[]{:S(2)}, u32[]{:S(2)}) collective-permute-start(f32[4,32,128]{2,1,0:T(8,128)S(1)} %get-tuple-element.58), channel_id=1, source_target_pairs={{0,1},{1,0},{2,3},{3,2},{4,5},{5,4},{6,7},{7,6},{8,9},{9,8},{10,11... | collective-permute-start | bytes 196616 | tf_op jit(solution)/shard_map/ppermute | solution.py:41
  131.3 22.9 %all-to-all-start = ((f32[256,1,128]{2,1,0:T(1,128)}), f32[256,1,128]{2,1,0:T(1,128)S(1)}, u32[]{:S(2)}, u32[]{:S(2)}) async-start(f32[256,1,128]{2,1,0:T(1,128)} %bitcast.5), calls=%async_computation | async-start | bytes 262144 | tf_op jit(solution)/shard_map/all_to_all | solution.py:342

commit v6 on v5

--- a/solution.py
+++ b/solution.py
@@ -301,7 +301,7 @@
         tile_rows, tile_cols, seed_t, tile_values, 64, HALVES_ZY, scale
     )
     keep, send, rows1, cols1, rows2, cols2 = lax.optimization_barrier((keep, send, rows1, cols1, rows2, cols2))
-    (part,) = add_parts(held, exchanged([keep, send], "row", CORE), [BF16])
+    part = added(exchanged([keep, send], "row", CORE)).astype(BF16)
     (part,) = add_parts(held, gathered(part, "row", ZHI), [BF16])
     x1_all, part = add_parts(held, gathered(part, "row", Y), [F32, BF16])
     x1 = lax.dynamic_slice_in_dim(x1_all, (zhi * 4 + y) * 2, 2, 0)

time: 155 us -> 155 us (level)
  no operation moved by 1% of the time
where the time goes in v6:
time: 155 us
  starting transfers between devices  67.6 us (44%)
  waiting for transfers between devices  63.4 us (41%)
  Pallas kernels  21.2 us (14%)
  other arithmetic  1.92 us (1%)
    ppermute x29, starting transfers between devices, swapped(): return lax.ppermute(x, axis, [(i, i ^ by << part[0]) for i in range(16)])  57.6 us
    ppermute x29, waiting for transfers between devices, swapped(): return lax.ppermute(x, axis, [(i, i ^ by << part[0]) for i in range(16)])  50.6 us
    all_to_all x1, waiting for transfers between devices, per_device(): lax.all_to_all(stat.reshape(n_rows * n_cols, 1, EDGE), ('row', 'col'), 0, 0)  12.9 us
    pallas_call x3, Pallas kernels, tile_pass(): pl.pallas_call(functools.partial(pass_kernel, flipped=flipped, in_orders=...  12.1 us
    all_to_all x1, starting transfers between devices, per_device(): lax.all_to_all(stat.reshape(n_rows * n_cols, 1, EDGE), ('row', 'col'), 0, 0)  10 us
    pallas_call x1, Pallas kernels, first_pass(): pl.pallas_call(functools.partial(first_kernel, orders=orders, scale=scale...  7.2 us
  transfers between devices with their start and end apart: 30, of which 24 were waited for; matrix products, arithmetic and copies ran while one was open for 0% of the time, Pallas kernels for 0%

profile of v6, /device:TPU:1, one launch (start us, length us, event | category | flops | bytes accessed | tf_op | source)
XLA Modules:
  0.0 155.2 jit_solution(17523007156963139615)
XLA Ops:
  1.3 7.2 %shard_map.59 = (bf16[704,128,128]{2,1,0:T(8,128)(2,1)S(1)}, bf16[16,32,128]{2,1,0:T(8,128)(2,1)}, bf16[16,32,128]{2,1,0:T(8,128)(2,1)}) custom-call(s32[352]{0:T(512)} %src_ref.1, s32[352]{0:T(512)} %dst_ref.1, s32[16,32]{1,0:T(8,128)} %bitcast.12, bf16[352,128,128]{2,1,0:T(8,128)(2,1)} %w_ref.1), custom_call_target="tpu_custom_call" | custom-call | flops 1000000 | bytes 100000 | tf_op jit(solution)/shard_map/pallas_call | solution.py:163
  8.6 3.3 %collective-permute-start = (bf16[16,32,128]{2,1,0:T(8,128)(2,1)}, bf16[16,32,128]{2,1,0:T(8,128)(2,1)S(1)}, u32[]{:S(2)}, u32[]{:S(2)}) collective-permute-start(bf16[16,32,128]{2,1,0:T(8,128)(2,1)} %get-tuple-element.33), channel_id=1, source_target_pairs={{0,16},{16,0},{32,48},{48,32},{64,80},{80,64},{96,112},{112,96},{1... | collective-permute-start | bytes 393224 | tf_op jit(solution)/shard_map/ppermute | solution.py:41
  11.9 1.2 collective-permute-done
  13.1 0.9 add_convert_fusion.refs_1_
  14.0 5.3 %collective-permute-start.1 = (bf16[16,32,128]{2,1,0:T(8,128)(2,1)S(1)}, bf16[16,32,128]{2,1,0:T(8,128)(2,1)S(1)}, u32[]{:S(2)}, u32[]{:S(2)}) collective-permute-start(bf16[16,32,128]{2,1,0:T(8,128)(2,1)S(1)} %add_convert_fusion.refs_1_), channel_id=1, source_target_pairs={{0,128},{16,144},{32,160},{48,176},{64,192},{80,208},{96,224},{112... | collective-permute-start | bytes 393224 | tf_op jit(solution)/shard_map/ppermute | solution.py:41
  19.3 3.4 %collective-permute-done.1.refs_2_ = bf16[16,32,128]{2,1,0:T(8,128)(2,1)S(1)} collective-permute-done((bf16[16,32,128]{2,1,0:T(8,128)(2,1)S(1)}, bf16[16,32,128]{2,1,0:T(8,128)(2,1)S(1)}, u32[]{:S(2)}, u32[]{:S(2)}) %collective-permute-start.1) | collective-permute-done | bytes 131104 | tf_op jit(solution)/shard_map/ppermute | solution.py:41
  22.8 2.9 %collective-permute-start.4 = (bf16[16,32,128]{2,1,0:T(8,128)(2,1)S(1)}, bf16[16,32,128]{2,1,0:T(8,128)(2,1)S(1)}, u32[]{:S(2)}, u32[]{:S(2)}) collective-permute-start(bf16[16,32,128]{2,1,0:T(8,128)(2,1)S(1)} %shard_map.60.refs_1_), channel_id=1, source_target_pairs={{0,96},{16,112},{32,64},{48,80},{64,32},{80,48},{96,0},{112,16},{1... | collective-permute-start | bytes 393224 | tf_op jit(solution)/shard_map/ppermute | solution.py:41
  26.4 4.8 %collective-permute-done.4.refs_4_ = bf16[16,32,128]{2,1,0:T(8,128)(2,1)S(1)} collective-permute-done((bf16[16,32,128]{2,1,0:T(8,128)(2,1)S(1)}, bf16[16,32,128]{2,1,0:T(8,128)(2,1)S(1)}, u32[]{:S(2)}, u32[]{:S(2)}) %collective-permute-start.4) | collective-permute-done | bytes 131104 | tf_op jit(solution)/shard_map/ppermute | solution.py:41
  31.3 3.4 %collective-permute-start.5 = (bf16[16,32,128]{2,1,0:T(8,128)(2,1)S(1)}, bf16[16,32,128]{2,1,0:T(8,128)(2,1)S(1)}, u32[]{:S(2)}, u32[]{:S(2)}) collective-permute-start(bf16[16,32,128]{2,1,0:T(8,128)(2,1)S(1)} %get-tuple-element.38.rest_0_), channel_id=1, source_target_pairs={{0,16},{16,0},{32,48},{48,32},{64,80},{80,64},{96,112},{112,96},{1... | collective-permute-start | bytes 393224 | tf_op jit(solution)/shard_map/ppermute | solution.py:41
  34.7 1.0 collective-permute-done.5.rest_1_
  35.7 4.0 %shard_map.62 = (bf16[16,32,128]{2,1,0:T(8,128)(2,1)S(1)}, bf16[16,32,128]{2,1,0:T(8,128)(2,1)S(1)}, bf16[16,32,128]{2,1,0:T(8,128)(2,1)S(1)}, bf16[16,32,128]{2,1,0:T(8,128)(2,1)S(1)}) custom-call(s32[352]{0:T(512)S(1)} %get-tuple-element.37.src_ref, s32[352]{0:T(512)S(1)} %get-tuple-element.35.dst_ref.src_ref, ...), custom_call_target="tpu_custom_call" | custom-call | flops 1000000 | bytes 100000 | tf_op jit(solution)/shard_map/pallas_call | solution.py:218
  39.7 1.3 collective-permute-start.6
  41.0 2.5 %collective-permute-start.7 = (bf16[16,32,128]{2,1,0:T(8,128)(2,1)S(1)}, bf16[16,32,128]{2,1,0:T(8,128)(2,1)S(1)}, u32[]{:S(2)}, u32[]{:S(2)}) collective-permute-start(bf16[16,32,128]{2,1,0:T(8,128)(2,1)S(1)} %get-tuple-element.41), channel_id=1, source_target_pairs={{0,8},{1,9},{2,10},{3,11},{4,12},{5,13},{6,14},{7,15},{8,0},{9,1},... | collective-permute-start | bytes 393224 | tf_op jit(solution)/shard_map/ppermute | solution.py:41
  44.5 5.1 %collective-permute-done.7.refs_3_ = bf16[16,32,128]{2,1,0:T(8,128)(2,1)S(1)} collective-permute-done((bf16[16,32,128]{2,1,0:T(8,128)(2,1)S(1)}, bf16[16,32,128]{2,1,0:T(8,128)(2,1)S(1)}, u32[]{:S(2)}, u32[]{:S(2)}) %collective-permute-start.7) | collective-permute-done | bytes 131104 | tf_op jit(solution)/shard_map/ppermute | solution.py:41
  49.6 2.5 %collective-permute-done.8.refs_4_ = bf16[16,32,128]{2,1,0:T(8,128)(2,1)S(1)} collective-permute-done((bf16[16,32,128]{2,1,0:T(8,128)(2,1)S(1)}, bf16[16,32,128]{2,1,0:T(8,128)(2,1)S(1)}, u32[]{:S(2)}, u32[]{:S(2)}) %collective-permute-start.8) | collective-permute-done | bytes 131104 | tf_op jit(solution)/shard_map/ppermute | solution.py:41
  52.1 4.1 %collective-permute-start.9 = (bf16[16,32,128]{2,1,0:T(8,128)(2,1)S(1)}, bf16[16,32,128]{2,1,0:T(8,128)(2,1)S(1)}, u32[]{:S(2)}, u32[]{:S(2)}) collective-permute-start(bf16[16,32,128]{2,1,0:T(8,128)(2,1)S(1)} %shard_map.63.refs_1_), channel_id=1, source_target_pairs={{0,2},{1,3},{2,0},{3,1},{4,6},{5,7},{6,4},{7,5},{8,10},{9,11},{10,... | collective-permute-start | bytes 393224 | tf_op jit(solution)/shard_map/ppermute | solution.py:41
  56.2 2.9 %collective-permute-done.9.refs_2_ = bf16[16,32,128]{2,1,0:T(8,128)(2,1)S(1)} collective-permute-done((bf16[16,32,128]{2,1,0:T(8,128)(2,1)S(1)}, bf16[16,32,128]{2,1,0:T(8,128)(2,1)S(1)}, u32[]{:S(2)}, u32[]{:S(2)}) %collective-permute-start.9) | collective-permute-done | bytes 131104 | tf_op jit(solution)/shard_map/ppermute | solution.py:41
  59.1 1.7 %collective-permute-start.10 = (bf16[16,32,128]{2,1,0:T(8,128)(2,1)S(1)}, bf16[16,32,128]{2,1,0:T(8,128)(2,1)S(1)}, u32[]{:S(2)}, u32[]{:S(2)}) collective-permute-start(bf16[16,32,128]{2,1,0:T(8,128)(2,1)S(1)} %shard_map.64.refs_1_), channel_id=1, source_target_pairs={{0,1},{1,0},{2,3},{3,2},{4,5},{5,4},{6,7},{7,6},{8,9},{9,8},{10,11... | collective-permute-start | bytes 393224 | tf_op jit(solution)/shard_map/ppermute | solution.py:41
  60.9 3.4 %collective-permute-done.10.refs_2_ = bf16[16,32,128]{2,1,0:T(8,128)(2,1)S(1)} collective-permute-done((bf16[16,32,128]{2,1,0:T(8,128)(2,1)S(1)}, bf16[16,32,128]{2,1,0:T(8,128)(2,1)S(1)}, u32[]{:S(2)}, u32[]{:S(2)}) %collective-permute-start.10) | collective-permute-done | bytes 131104 | tf_op jit(solution)/shard_map/ppermute | solution.py:41
  64.3 2.3 %collective-permute-start.13 = (bf16[16,32,128]{2,1,0:T(8,128)(2,1)S(1)}, bf16[16,32,128]{2,1,0:T(8,128)(2,1)S(1)}, u32[]{:S(2)}, u32[]{:S(2)}) collective-permute-start(bf16[16,32,128]{2,1,0:T(8,128)(2,1)S(1)} %get-tuple-element.43.rest_0_), channel_id=1, source_target_pairs={{0,12},{1,13},{2,14},{3,15},{4,8},{5,9},{6,10},{7,11},{8,4},{9,5},... | collective-permute-start | bytes 393224 | tf_op jit(solution)/shard_map/ppermute | solution.py:41
  66.6 1.0 collective-permute-start.11
  67.6 2.3 %collective-permute-done.13.rest_3_ = bf16[16,32,128]{2,1,0:T(8,128)(2,1)S(1)} collective-permute-done((bf16[16,32,128]{2,1,0:T(8,128)(2,1)S(1)}, bf16[16,32,128]{2,1,0:T(8,128)(2,1)S(1)}, u32[]{:S(2)}, u32[]{:S(2)}) %collective-permute-start.13) | collective-permute-done | bytes 131104 | tf_op jit(solution)/shard_map/ppermute | solution.py:41
  69.9 2.0 %collective-permute-done.12.rest_2_ = bf16[16,32,128]{2,1,0:T(8,128)(2,1)S(1)} collective-permute-done((bf16[16,32,128]{2,1,0:T(8,128)(2,1)S(1)}, bf16[16,32,128]{2,1,0:T(8,128)(2,1)S(1)}, u32[]{:S(2)}, u32[]{:S(2)}) %collective-permute-start.12) | collective-permute-done | bytes 131104 | tf_op jit(solution)/shard_map/ppermute | solution.py:41
  71.9 4.0 %shard_map.66 = (f32[16,32,128]{2,1,0:T(8,128)S(1)}, f32[16,32,128]{2,1,0:T(8,128)S(1)}) custom-call(s32[352]{0:T(512)S(1)} %get-tuple-element.35.dst_ref.src_ref, s32[352]{0:T(512)S(1)} %get-tuple-element.36.dst_ref.src_ref, bf16[704,128,128]{2,1,0:T(8,128)(2,1)S(1)} %get-tuple-element.29.refs_0_.w_ref, bf16[16,32,128]{2,1,0:T(8,128)(2,1)S(1)} %get-tuple-element.43.rest_0_, ...), custom_call_target="tpu_custom_call" | custom-call | flops 1000000 | bytes 100000 | tf_op jit(solution)/shard_map/pallas_call | solution.py:218
  75.9 5.6 %collective-permute-start.14 = (f32[16,32,128]{2,1,0:T(8,128)S(1)}, f32[16,32,128]{2,1,0:T(8,128)S(1)}, u32[]{:S(2)}, u32[]{:S(2)}) collective-permute-start(f32[16,32,128]{2,1,0:T(8,128)S(1)} %get-tuple-element.45), channel_id=1, source_target_pairs={{0,16},{16,0},{32,48},{48,32},{64,80},{80,64},{96,112},{112,96},{1... | collective-permute-start | bytes 786440 | tf_op jit(solution)/shard_map/ppermute | solution.py:41
  81.5 1.2 collective-permute-done.14.refs_2_
  82.7 1.8 %collective-permute-start.17 = (f32[4,32,128]{2,1,0:T(8,128)S(1)}, f32[4,32,128]{2,1,0:T(8,128)S(1)}, u32[]{:S(2)}, u32[]{:S(2)}) collective-permute-start(f32[4,32,128]{2,1,0:T(8,128)S(1)} %get-tuple-element.60), channel_id=1, source_target_pairs={{0,96},{16,112},{32,64},{48,80},{64,32},{80,48},{96,0},{112,16},{1... | collective-permute-start | bytes 196616 | tf_op jit(solution)/shard_map/ppermute | solution.py:41
  84.8 1.2 collective-permute-start.15
  86.1 1.1 collective-permute-done.17.refs_4_
  87.1 2.0 %collective-permute-done.16.refs_3_ = f32[4,32,128]{2,1,0:T(8,128)S(1)} collective-permute-done((f32[4,32,128]{2,1,0:T(8,128)S(1)}, f32[4,32,128]{2,1,0:T(8,128)S(1)}, u32[]{:S(2)}, u32[]{:S(2)}) %collective-permute-start.16) | collective-permute-done | bytes 65568 | tf_op jit(solution)/shard_map/ppermute | solution.py:41
  89.2 5.0 %collective-permute-start.18 = (f32[4,32,128]{2,1,0:T(8,128)S(1)}, f32[4,32,128]{2,1,0:T(8,128)S(1)}, u32[]{:S(2)}, u32[]{:S(2)}) collective-permute-start(f32[4,32,128]{2,1,0:T(8,128)S(1)} %shard_map.68.refs_1_), channel_id=1, source_target_pairs={{0,128},{16,144},{32,160},{48,176},{64,192},{80,208},{96,224},{112... | collective-permute-start | bytes 196616 | tf_op jit(solution)/shard_map/ppermute | solution.py:41
  94.1 2.1 %collective-permute-done.18.refs_2_ = f32[4,32,128]{2,1,0:T(8,128)S(1)} collective-permute-done((f32[4,32,128]{2,1,0:T(8,128)S(1)}, f32[4,32,128]{2,1,0:T(8,128)S(1)}, u32[]{:S(2)}, u32[]{:S(2)}) %collective-permute-start.18) | collective-permute-done | bytes 65568 | tf_op jit(solution)/shard_map/ppermute | solution.py:41
  96.3 1.7 %collective-permute-start.21 = (bf16[4,32,128]{2,1,0:T(8,128)(2,1)S(1)}, bf16[4,32,128]{2,1,0:T(8,128)(2,1)S(1)}, u32[]{:S(2)}, u32[]{:S(2)}) collective-permute-start(bf16[4,32,128]{2,1,0:T(8,128)(2,1)S(1)} %get-tuple-element.48), channel_id=1, source_target_pairs={{0,96},{16,112},{32,64},{48,80},{64,32},{80,48},{96,0},{112,16},{1... | collective-permute-start | bytes 98312 | tf_op jit(solution)/shard_map/ppermute | solution.py:41
  98.0 1.2 collective-permute-start.20
  99.6 2.3 %collective-permute-done.19 = bf16[4,32,128]{2,1,0:T(8,128)(2,1)S(1)} collective-permute-done((bf16[4,32,128]{2,1,0:T(8,128)(2,1)S(1)}, bf16[4,32,128]{2,1,0:T(8,128)(2,1)S(1)}, u32[]{:S(2)}, u32[]{:S(2)}) %collective-permute-start.19) | collective-permute-done | bytes 32800 | tf_op jit(solution)/shard_map/ppermute | solution.py:41
  102.3 4.5 %collective-permute-start.22 = (bf16[16,32,128]{2,1,0:T(8,128)(2,1)S(1)}, bf16[16,32,128]{2,1,0:T(8,128)(2,1)S(1)}, u32[]{:S(2)}, u32[]{:S(2)}) collective-permute-start(bf16[16,32,128]{2,1,0:T(8,128)(2,1)S(1)} %constant_dynamic-update-slice_fusion.rest_0_), channel_id=1, source_target_pairs={{0,16},{16,0},{32,48},{48,32},{64,80},{80,64},{96,112},{112,96},{1... | collective-permute-start | bytes 393224 | tf_op jit(solution)/shard_map/ppermute | solution.py:41
  106.8 1.0 collective-permute-done.22.rest_1_
  107.8 4.1 %shard_map.70 = (f32[16,32,128]{2,1,0:T(8,128)S(1)}, f32[17,32,128]{2,1,0:T(8,128)S(1)}, f32[17,32,128]{2,1,0:T(8,128)S(1)}, f32[17,32,128]{2,1,0:T(8,128)S(1)}) custom-call(s32[352]{0:T(512)S(1)} %get-tuple-element.36.dst_ref.src_ref, s32[352]{0:T(512)S(1)} %get-tuple-element.47.dst_ref, bf16[704,128,128]{2,1,0:T(8,128)(2,1)S(1)} %get-tuple-element.29.refs_0_.w_ref, ...), custom_call_target="tpu_custom_call" | custom-call | flops 1000000 | bytes 100000 | tf_op jit(solution)/shard_map/pallas_call | solution.py:218
  111.9 1.1 collective-permute-start.25
  113.1 1.2 collective-permute-start.24
  114.3 1.1 collective-permute-start.23
  115.4 5.3 %collective-permute-done.25 = f16[17,32,128]{2,1,0:T(8,128)(2,1)S(1)} collective-permute-done((f16[17,32,128]{2,1,0:T(8,128)(2,1)S(1)}, f16[17,32,128]{2,1,0:T(8,128)(2,1)S(1)}, u32[]{:S(2)}, u32[]{:S(2)}) %collective-permute-start.25) | collective-permute-done | bytes 139296 | tf_op jit(solution)/shard_map/ppermute | solution.py:41
  121.8 1.6 %collective-permute-start.28 = (f32[4,32,128]{2,1,0:T(8,128)S(1)}, f32[4,32,128]{2,1,0:T(8,128)S(1)}, u32[]{:S(2)}, u32[]{:S(2)}) collective-permute-start(f32[4,32,128]{2,1,0:T(8,128)S(1)} %get-tuple-element.56), channel_id=1, source_target_pairs={{0,3},{1,2},{2,1},{3,0},{4,7},{5,6},{6,5},{7,4},{8,11},{9,10},{10,... | collective-permute-start | bytes 196616 | tf_op jit(solution)/shard_map/ppermute | solution.py:41
  123.4 2.0 %collective-permute-start.26 = (f32[4,32,128]{2,1,0:T(8,128)S(1)}, f32[4,32,128]{2,1,0:T(8,128)S(1)}, u32[]{:S(2)}, u32[]{:S(2)}) collective-permute-start(f32[4,32,128]{2,1,0:T(8,128)S(1)} %get-tuple-element.58), channel_id=1, source_target_pairs={{0,1},{1,0},{2,3},{3,2},{4,5},{5,4},{6,7},{7,6},{8,9},{9,8},{10,11... | collective-permute-start | bytes 196616 | tf_op jit(solution)/shard_map/ppermute | solution.py:41
  125.5 1.5 collective-permute-done.28.rest_3_
  127.0 3.6 %collective-permute-done.27.rest_2_ = f32[4,32,128]{2,1,0:T(8,128)S(1)} collective-permute-done((f32[4,32,128]{2,1,0:T(8,128)S(1)}, f32[4,32,128]{2,1,0:T(8,128)S(1)}, u32[]{:S(2)}, u32[]{:S(2)}) %collective-permute-start.27) | collective-permute-done | bytes 65568 | tf_op jit(solution)/shard_map/ppermute | solution.py:41
  131.3 10.0 %all-to-all-start = ((f32[256,1,128]{2,1,0:T(1,128)}), f32[256,1,128]{2,1,0:T(1,128)S(1)}, u32[]{:S(2)}, u32[]{:S(2)}) async-start(f32[256,1,128]{2,1,0:T(1,128)} %bitcast.5), calls=%async_computation | async-start | bytes 262144 | tf_op jit(solution)/shard_map/all_to_all | solution.py:342
  141.4 12.9 %all-to-all-done = f32[256,1,128]{2,1,0:T(1,128)S(1)} async-done(((f32[256,1,128]{2,1,0:T(1,128)}), f32[256,1,128]{2,1,0:T(1,128)S(1)}, u32[]{:S(2)}, u32[]{:S(2)}) %all-to-all-start) | async-done | bytes 131104 | tf_op jit(solution)/shard_map/all_to_all | solution.py:342
  (49 shorter events, 6.7 us)
Async XLA Ops:
  8.6 4.5 %collective-permute-start = (bf16[16,32,128]{2,1,0:T(8,128)(2,1)}, bf16[16,32,128]{2,1,0:T(8,128)(2,1)S(1)}, u32[]{:S(2)}, u32[]{:S(2)}) collective-permute-start(bf16[16,32,128]{2,1,0:T(8,128)(2,1)} %get-tuple-element.33), channel_id=1, source_target_pairs={{0,16},{16,0},{32,48},{48,32},{64,80},{80,64},{96,112},{112,96},{1... | collective-permute-start | bytes 393224 | tf_op jit(solution)/shard_map/ppermute | solution.py:41
  14.0 8.7 %collective-permute-start.1 = (bf16[16,32,128]{2,1,0:T(8,128)(2,1)S(1)}, bf16[16,32,128]{2,1,0:T(8,128)(2,1)S(1)}, u32[]{:S(2)}, u32[]{:S(2)}) collective-permute-start(bf16[16,32,128]{2,1,0:T(8,128)(2,1)S(1)} %add_convert_fusion.refs_1_), channel_id=1, source_target_pairs={{0,128},{16,144},{32,160},{48,176},{64,192},{80,208},{96,224},{112... | collective-permute-start | bytes 393224 | tf_op jit(solution)/shard_map/ppermute | solution.py:41
  22.8 8.4 %collective-permute-start.4 = (bf16[16,32,128]{2,1,0:T(8,128)(2,1)S(1)}, bf16[16,32,128]{2,1,0:T(8,128)(2,1)S(1)}, u32[]{:S(2)}, u32[]{:S(2)}) collective-permute-start(bf16[16,32,128]{2,1,0:T(8,128)(2,1)S(1)} %shard_map.60.refs_1_), channel_id=1, source_target_pairs={{0,96},{16,112},{32,64},{48,80},{64,32},{80,48},{96,0},{112,16},{1... | collective-permute-start | bytes 393224 | tf_op jit(solution)/shard_map/ppermute | solution.py:41
  25.7 5.4 %collective-permute-start.3 = (bf16[16,32,128]{2,1,0:T(8,128)(2,1)S(1)}, bf16[16,32,128]{2,1,0:T(8,128)(2,1)S(1)}, u32[]{:S(2)}, u32[]{:S(2)}) collective-permute-start(bf16[16,32,128]{2,1,0:T(8,128)(2,1)S(1)} %shard_map.60.refs_1_), channel_id=1, source_target_pairs={{0,64},{16,80},{32,96},{48,112},{64,0},{80,16},{96,32},{112,48},{1... | collective-permute-start | bytes 393224 | tf_op jit(solution)/shard_map/ppermute | solution.py:41
  26.1 5.2 %collective-permute-start.2 = (bf16[16,32,128]{2,1,0:T(8,128)(2,1)S(1)}, bf16[16,32,128]{2,1,0:T(8,128)(2,1)S(1)}, u32[]{:S(2)}, u32[]{:S(2)}) collective-permute-start(bf16[16,32,128]{2,1,0:T(8,128)(2,1)S(1)} %shard_map.60.refs_1_), channel_id=1, source_target_pairs={{0,32},{16,48},{32,0},{48,16},{64,96},{80,112},{96,64},{112,80},{1... | collective-permute-start | bytes 393224 | tf_op jit(solution)/shard_map/ppermute | solution.py:41
  31.3 4.4 %collective-permute-start.5 = (bf16[16,32,128]{2,1,0:T(8,128)(2,1)S(1)}, bf16[16,32,128]{2,1,0:T(8,128)(2,1)S(1)}, u32[]{:S(2)}, u32[]{:S(2)}) collective-permute-start(bf16[16,32,128]{2,1,0:T(8,128)(2,1)S(1)} %get-tuple-element.38.rest_0_), channel_id=1, source_target_pairs={{0,16},{16,0},{32,48},{48,32},{64,80},{80,64},{96,112},{112,96},{1... | collective-permute-start | bytes 393224 | tf_op jit(solution)/shard_map/ppermute | solution.py:41
  39.7 4.8 %collective-permute-start.6 = (bf16[16,32,128]{2,1,0:T(8,128)(2,1)S(1)}, bf16[16,32,128]{2,1,0:T(8,128)(2,1)S(1)}, u32[]{:S(2)}, u32[]{:S(2)}) collective-permute-start(bf16[16,32,128]{2,1,0:T(8,128)(2,1)S(1)} %get-tuple-element.40), channel_id=1, source_target_pairs={{0,4},{1,5},{2,6},{3,7},{4,0},{5,1},{6,2},{7,3},{8,12},{9,13},{10,... | collective-permute-start | bytes 393224 | tf_op jit(solution)/shard_map/ppermute | solution.py:41
  41.0 8.6 %collective-permute-start.7 = (bf16[16,32,128]{2,1,0:T(8,128)(2,1)S(1)}, bf16[16,32,128]{2,1,0:T(8,128)(2,1)S(1)}, u32[]{:S(2)}, u32[]{:S(2)}) collective-permute-start(bf16[16,32,128]{2,1,0:T(8,128)(2,1)S(1)} %get-tuple-element.41), channel_id=1, source_target_pairs={{0,8},{1,9},{2,10},{3,11},{4,12},{5,13},{6,14},{7,15},{8,0},{9,1},... | collective-permute-start | bytes 393224 | tf_op jit(solution)/shard_map/ppermute | solution.py:41
  43.4 8.6 %collective-permute-start.8 = (bf16[16,32,128]{2,1,0:T(8,128)(2,1)S(1)}, bf16[16,32,128]{2,1,0:T(8,128)(2,1)S(1)}, u32[]{:S(2)}, u32[]{:S(2)}) collective-permute-start(bf16[16,32,128]{2,1,0:T(8,128)(2,1)S(1)} %get-tuple-element.42), channel_id=1, source_target_pairs={{0,12},{1,13},{2,14},{3,15},{4,8},{5,9},{6,10},{7,11},{8,4},{9,5},... | collective-permute-start | bytes 393224 | tf_op jit(solution)/shard_map/ppermute | solution.py:41
  52.1 7.0 %collective-permute-start.9 = (bf16[16,32,128]{2,1,0:T(8,128)(2,1)S(1)}, bf16[16,32,128]{2,1,0:T(8,128)(2,1)S(1)}, u32[]{:S(2)}, u32[]{:S(2)}) collective-permute-start(bf16[16,32,128]{2,1,0:T(8,128)(2,1)S(1)} %shard_map.63.refs_1_), channel_id=1, source_target_pairs={{0,2},{1,3},{2,0},{3,1},{4,6},{5,7},{6,4},{7,5},{8,10},{9,11},{10,... | collective-permute-start | bytes 393224 | tf_op jit(solution)/shard_map/ppermute | solution.py:41
  59.1 5.1 %collective-permute-start.10 = (bf16[16,32,128]{2,1,0:T(8,128)(2,1)S(1)}, bf16[16,32,128]{2,1,0:T(8,128)(2,1)S(1)}, u32[]{:S(2)}, u32[]{:S(2)}) collective-permute-start(bf16[16,32,128]{2,1,0:T(8,128)(2,1)S(1)} %shard_map.64.refs_1_), channel_id=1, source_target_pairs={{0,1},{1,0},{2,3},{3,2},{4,5},{5,4},{6,7},{7,6},{8,9},{9,8},{10,11... | collective-permute-start | bytes 393224 | tf_op jit(solution)/shard_map/ppermute | solution.py:41
  64.3 5.7 %collective-permute-start.13 = (bf16[16,32,128]{2,1,0:T(8,128)(2,1)S(1)}, bf16[16,32,128]{2,1,0:T(8,128)(2,1)S(1)}, u32[]{:S(2)}, u32[]{:S(2)}) collective-permute-start(bf16[16,32,128]{2,1,0:T(8,128)(2,1)S(1)} %get-tuple-element.43.rest_0_), channel_id=1, source_target_pairs={{0,12},{1,13},{2,14},{3,15},{4,8},{5,9},{6,10},{7,11},{8,4},{9,5},... | collective-permute-start | bytes 393224 | tf_op jit(solution)/shard_map/ppermute | solution.py:41
  66.6 5.3 %collective-permute-start.12 = (bf16[16,32,128]{2,1,0:T(8,128)(2,1)S(1)}, bf16[16,32,128]{2,1,0:T(8,128)(2,1)S(1)}, u32[]{:S(2)}, u32[]{:S(2)}) collective-permute-start(bf16[16,32,128]{2,1,0:T(8,128)(2,1)S(1)} %get-tuple-element.43.rest_0_), channel_id=1, source_target_pairs={{0,8},{1,9},{2,10},{3,11},{4,12},{5,13},{6,14},{7,15},{8,0},{9,1},... | collective-permute-start | bytes 393224 | tf_op jit(solution)/shard_map/ppermute | solution.py:41
  66.6 5.3 %collective-permute-start.11 = (bf16[16,32,128]{2,1,0:T(8,128)(2,1)S(1)}, bf16[16,32,128]{2,1,0:T(8,128)(2,1)S(1)}, u32[]{:S(2)}, u32[]{:S(2)}) collective-permute-start(bf16[16,32,128]{2,1,0:T(8,128)(2,1)S(1)} %get-tuple-element.43.rest_0_), channel_id=1, source_target_pairs={{0,4},{1,5},{2,6},{3,7},{4,0},{5,1},{6,2},{7,3},{8,12},{9,13},{10,... | collective-permute-start | bytes 393224 | tf_op jit(solution)/shard_map/ppermute | solution.py:41
  75.9 6.8 %collective-permute-start.14 = (f32[16,32,128]{2,1,0:T(8,128)S(1)}, f32[16,32,128]{2,1,0:T(8,128)S(1)}, u32[]{:S(2)}, u32[]{:S(2)}) collective-permute-start(f32[16,32,128]{2,1,0:T(8,128)S(1)} %get-tuple-element.45), channel_id=1, source_target_pairs={{0,16},{16,0},{32,48},{48,32},{64,80},{80,64},{96,112},{112,96},{1... | collective-permute-start | bytes 786440 | tf_op jit(solution)/shard_map/ppermute | solution.py:41
  82.7 4.4 %collective-permute-start.17 = (f32[4,32,128]{2,1,0:T(8,128)S(1)}, f32[4,32,128]{2,1,0:T(8,128)S(1)}, u32[]{:S(2)}, u32[]{:S(2)}) collective-permute-start(f32[4,32,128]{2,1,0:T(8,128)S(1)} %get-tuple-element.60), channel_id=1, source_target_pairs={{0,96},{16,112},{32,64},{48,80},{64,32},{80,48},{96,0},{112,16},{1... | collective-permute-start | bytes 196616 | tf_op jit(solution)/shard_map/ppermute | solution.py:41
  84.5 4.6 %collective-permute-start.16 = (f32[4,32,128]{2,1,0:T(8,128)S(1)}, f32[4,32,128]{2,1,0:T(8,128)S(1)}, u32[]{:S(2)}, u32[]{:S(2)}) collective-permute-start(f32[4,32,128]{2,1,0:T(8,128)S(1)} %get-tuple-element.61), channel_id=1, source_target_pairs={{0,64},{16,80},{32,96},{48,112},{64,0},{80,16},{96,32},{112,48},{1... | collective-permute-start | bytes 196616 | tf_op jit(solution)/shard_map/ppermute | solution.py:41
  84.8 4.3 %collective-permute-start.15 = (f32[4,32,128]{2,1,0:T(8,128)S(1)}, f32[4,32,128]{2,1,0:T(8,128)S(1)}, u32[]{:S(2)}, u32[]{:S(2)}) collective-permute-start(f32[4,32,128]{2,1,0:T(8,128)S(1)} %get-tuple-element.62), channel_id=1, source_target_pairs={{0,32},{16,48},{32,0},{48,16},{64,96},{80,112},{96,64},{112,80},{1... | collective-permute-start | bytes 196616 | tf_op jit(solution)/shard_map/ppermute | solution.py:41
  89.1 65.1 %copy-start = (s32[32,16]{0,1:T(8,128)S(1)}, s32[32,16]{0,1:T(8,128)}, u32[]{:S(2)}) copy-start(s32[32,16]{0,1:T(8,128)} %param.7) | copy-start | bytes 6148
  89.2 7.1 %collective-permute-start.18 = (f32[4,32,128]{2,1,0:T(8,128)S(1)}, f32[4,32,128]{2,1,0:T(8,128)S(1)}, u32[]{:S(2)}, u32[]{:S(2)}) collective-permute-start(f32[4,32,128]{2,1,0:T(8,128)S(1)} %shard_map.68.refs_1_), channel_id=1, source_target_pairs={{0,128},{16,144},{32,160},{48,176},{64,192},{80,208},{96,224},{112... | collective-permute-start | bytes 196616 | tf_op jit(solution)/shard_map/ppermute | solution.py:41
  96.3 6.0 %collective-permute-start.21 = (bf16[4,32,128]{2,1,0:T(8,128)(2,1)S(1)}, bf16[4,32,128]{2,1,0:T(8,128)(2,1)S(1)}, u32[]{:S(2)}, u32[]{:S(2)}) collective-permute-start(bf16[4,32,128]{2,1,0:T(8,128)(2,1)S(1)} %get-tuple-element.48), channel_id=1, source_target_pairs={{0,96},{16,112},{32,64},{48,80},{64,32},{80,48},{96,0},{112,16},{1... | collective-permute-start | bytes 98312 | tf_op jit(solution)/shard_map/ppermute | solution.py:41
  98.0 4.3 %collective-permute-start.20 = (bf16[4,32,128]{2,1,0:T(8,128)(2,1)S(1)}, bf16[4,32,128]{2,1,0:T(8,128)(2,1)S(1)}, u32[]{:S(2)}, u32[]{:S(2)}) collective-permute-start(bf16[4,32,128]{2,1,0:T(8,128)(2,1)S(1)} %get-tuple-element.48), channel_id=1, source_target_pairs={{0,64},{16,80},{32,96},{48,112},{64,0},{80,16},{96,32},{112,48},{1... | collective-permute-start | bytes 98312 | tf_op jit(solution)/shard_map/ppermute | solution.py:41
  99.2 2.8 %collective-permute-start.19 = (bf16[4,32,128]{2,1,0:T(8,128)(2,1)S(1)}, bf16[4,32,128]{2,1,0:T(8,128)(2,1)S(1)}, u32[]{:S(2)}, u32[]{:S(2)}) collective-permute-start(bf16[4,32,128]{2,1,0:T(8,128)(2,1)S(1)} %get-tuple-element.48), channel_id=1, source_target_pairs={{0,32},{16,48},{32,0},{48,16},{64,96},{80,112},{96,64},{112,80},{1... | collective-permute-start | bytes 98312 | tf_op jit(solution)/shard_map/ppermute | solution.py:41
  102.3 5.5 %collective-permute-start.22 = (bf16[16,32,128]{2,1,0:T(8,128)(2,1)S(1)}, bf16[16,32,128]{2,1,0:T(8,128)(2,1)S(1)}, u32[]{:S(2)}, u32[]{:S(2)}) collective-permute-start(bf16[16,32,128]{2,1,0:T(8,128)(2,1)S(1)} %constant_dynamic-update-slice_fusion.rest_0_), channel_id=1, source_target_pairs={{0,16},{16,0},{32,48},{48,32},{64,80},{80,64},{96,112},{112,96},{1... | collective-permute-start | bytes 393224 | tf_op jit(solution)/shard_map/ppermute | solution.py:41
  111.9 8.8 %collective-permute-start.25 = (f16[17,32,128]{2,1,0:T(8,128)(2,1)S(1)}, f16[17,32,128]{2,1,0:T(8,128)(2,1)S(1)}, u32[]{:S(2)}, u32[]{:S(2)}) collective-permute-start(f16[17,32,128]{2,1,0:T(8,128)(2,1)S(1)} %convert_element_type.34), channel_id=1, source_target_pairs={{0,12},{1,13},{2,14},{3,15},{4,8},{5,9},{6,10},{7,11},{8,4},{9,5},... | collective-permute-start | bytes 417800 | tf_op jit(solution)/shard_map/ppermute | solution.py:41
  113.1 7.7 %collective-permute-start.24 = (f16[17,32,128]{2,1,0:T(8,128)(2,1)S(1)}, f16[17,32,128]{2,1,0:T(8,128)(2,1)S(1)}, u32[]{:S(2)}, u32[]{:S(2)}) collective-permute-start(f16[17,32,128]{2,1,0:T(8,128)(2,1)S(1)} %convert_element_type.32), channel_id=1, source_target_pairs={{0,8},{1,9},{2,10},{3,11},{4,12},{5,13},{6,14},{7,15},{8,0},{9,1},... | collective-permute-start | bytes 417800 | tf_op jit(solution)/shard_map/ppermute | solution.py:41
  114.3 7.3 %collective-permute-start.23 = (f16[17,32,128]{2,1,0:T(8,128)(2,1)S(1)}, f16[17,32,128]{2,1,0:T(8,128)(2,1)S(1)}, u32[]{:S(2)}, u32[]{:S(2)}) collective-permute-start(f16[17,32,128]{2,1,0:T(8,128)(2,1)S(1)} %convert_element_type.30), channel_id=1, source_target_pairs={{0,4},{1,5},{2,6},{3,7},{4,0},{5,1},{6,2},{7,3},{8,12},{9,13},{10,... | collective-permute-start | bytes 417800 | tf_op jit(solution)/shard_map/ppermute | solution.py:41
  121.8 5.2 %collective-permute-start.28 = (f32[4,32,128]{2,1,0:T(8,128)S(1)}, f32[4,32,128]{2,1,0:T(8,128)S(1)}, u32[]{:S(2)}, u32[]{:S(2)}) collective-permute-start(f32[4,32,128]{2,1,0:T(8,128)S(1)} %get-tuple-element.56), channel_id=1, source_target_pairs={{0,3},{1,2},{2,1},{3,0},{4,7},{5,6},{6,5},{7,4},{8,11},{9,10},{10,... | collective-permute-start | bytes 196616 | tf_op jit(solution)/shard_map/ppermute | solution.py:41
  123.4 7.1 %collective-permute-start.27 = (f32[4,32,128]{2,1,0:T(8,128)S(1)}, f32[4,32,128]{2,1,0:T(8,128)S(1)}, u32[]{:S(2)}, u32[]{:S(2)}) collective-permute-start(f32[4,32,128]{2,1,0:T(8,128)S(1)} %get-tuple-element.57), channel_id=1, source_target_pairs={{0,2},{1,3},{2,0},{3,1},{4,6},{5,7},{6,4},{7,5},{8,10},{9,11},{10,... | collective-permute-start | bytes 196616 | tf_op jit(solution)/shard_map/ppermute | solution.py:41
  123.4 7.1 %collective-permute-start.26 = (f32[4,32,128]{2,1,0:T(8,128)S(1)}, f32[4,32,128]{2,1,0:T(8,128)S(1)}, u32[]{:S(2)}, u32[]{:S(2)}) collective-permute-start(f32[4,32,128]{2,1,0:T(8,128)S(1)} %get-tuple-element.58), channel_id=1, source_target_pairs={{0,1},{1,0},{2,3},{3,2},{4,5},{5,4},{6,7},{7,6},{8,9},{9,8},{10,11... | collective-permute-start | bytes 196616 | tf_op jit(solution)/shard_map/ppermute | solution.py:41
  131.3 22.9 %all-to-all-start = ((f32[256,1,128]{2,1,0:T(1,128)}), f32[256,1,128]{2,1,0:T(1,128)S(1)}, u32[]{:S(2)}, u32[]{:S(2)}) async-start(f32[256,1,128]{2,1,0:T(1,128)} %bitcast.5), calls=%async_computation | async-start | bytes 262144 | tf_op jit(solution)/shard_map/all_to_all | solution.py:342
